TPU v7x, 32 devices: a whole 2x2x4 slice. The times are simulated.
32 devices in a mesh: group: 2 (over x), ty: 8 (over z, y), tx: 2 (over core).
Axes of the slice: x: 2, y: 2, z: 4, core: 2. Of those that a mesh axis runs over, the one named last changes fastest.
Arguments:
- sweeps: bfloat16 [8192, 48, 128], P(('group', 'ty', 'tx')), parts along dimension 0, may hold values from -12 to 12
- route_block: int32 [32, 16, 16], P(('group', 'ty', 'tx')), parts along dimension 0, may hold values from 0 to 255
- route_cell: int32 [32, 16, 16], P(('group', 'ty', 'tx')), parts along dimension 0, may hold values from 0 to 383
- route_templ: int32 [32, 16, 16], P(('group', 'ty', 'tx')), parts along dimension 0, may hold values from 0 to 31
- route_count: int32 [32, 16], P(('group', 'ty', 'tx')), parts along dimension 0, may hold values from 2 to 16, as said below
- footprint: bfloat16 [32, 128, 128], replicated, may hold values from 0 to 13, as said below
- conv_first: bfloat16 [9, 64, 48], replicated, may hold values from -0.3125 to 0.3125
- bias_first: float32 [64], replicated, may hold values from -3 to 3
- conv_second: bfloat16 [9, 64, 64], replicated, may hold values from -0.25 to 0.25
- bias_second: float32 [64], replicated, may hold values from -3 to 3
Outputs:
- encoded: bfloat16 [64, 3072, 512], P(None, ('group', 'ty'), 'tx'), parts along dimension 1
There are 2 independent parts, one for each index of `group`. A program takes and returns all parts, laid end to end along the dimension named above; an argument that names none is the same for every part. Nothing has to cross between parts.
Inputs may be any that keep to these rules, and one draw needn't show every extreme that they name: `route_count`: in every draw one tile receives 16 live slots from every device. `footprint`: nonnegative weights.
All inputs are finite; a program needn't handle non-finite values.
Results may differ from a plain program's by a relative error of at most 0.0036.
Values may be sent and summed in bfloat16 or wider, within the bound.
No kernel may reach another device: no remote copies, remote signals or barrier semaphores. Data moves between devices by JAX's collectives and lax.ppermute only.
A program may use at most 256 MiB of HBM per device.

v0:
```python
import jax
import jax.numpy as jnp
from jax import lax
from jax.sharding import PartitionSpec as P

TH = 192
TW = 256
CBLK = 384


def extended(cells, sides, width):
    for axis, dim in sides:
        count = lax.axis_size(axis)
        ends = count - 1
        head = lax.slice_in_dim(cells, 0, width, axis=dim)
        tail = lax.slice_in_dim(cells, cells.shape[dim] - width, cells.shape[dim], axis=dim)
        cells = jnp.concatenate(
            [
                lax.ppermute(tail, axis, [(i, (i + 1) % count) for i in range(ends)]),
                cells,
                lax.ppermute(head, axis, [((i + 1) % count, i) for i in range(ends)]),
            ],
            axis=dim,
        )
    return cells


def slot_terms(pieces, footprint, row_weight):
    samples, slot_info = pieces
    template = slot_info[..., 1]
    is_live = slot_info[..., 2].astype(jnp.float32)
    matrices = footprint[template]
    terms = jnp.einsum("psxy,pscy->pscx", matrices, samples, preferred_element_type=jnp.float32)
    terms = terms * is_live[:, :, None, None]
    weights = row_weight[template] * is_live[:, :, None]
    return (terms, weights, slot_info[..., 0])


def stencil(padded, kernel, bias):
    height = padded.shape[1] - 2
    span_cols = padded.shape[2] - 2
    summed = jnp.zeros((kernel.shape[1], height, span_cols), jnp.float32)
    for tap_row in range(3):
        for tap_col in range(3):
            window = padded[:, tap_row : tap_row + height, tap_col : tap_col + span_cols]
            summed = summed + jnp.einsum(
                "oc,chw->ohw",
                kernel[3 * tap_row + tap_col],
                window,
                preferred_element_type=jnp.float32,
            )
    return summed + bias[:, None, None]


def shards(
    sweeps,
    route_block,
    route_cell,
    route_templ,
    route_count,
    footprint,
    conv_first,
    bias_first,
    conv_second,
    bias_second,
):
    capacity = route_block.shape[2]
    channels = sweeps.shape[1]
    block_len = sweeps.shape[2]
    packets = sweeps[route_block[0]]
    slot_index = jnp.arange(capacity, dtype=jnp.int32)
    is_live = (slot_index[None, :] < route_count[0][:, None]).astype(jnp.int32)
    slot_info = jnp.stack([route_cell[0], route_templ[0], is_live], axis=2)
    row_weight = jnp.sum(footprint.astype(jnp.float32), axis=2)
    terms, weights, targets = slot_terms(
        (
            lax.all_to_all(packets, ("ty", "tx"), split_axis=0, concat_axis=0, tiled=True),
            lax.all_to_all(slot_info, ("ty", "tx"), split_axis=0, concat_axis=0, tiled=True),
        ),
        footprint,
        row_weight,
    )
    flat_targets = targets.reshape(-1)
    numerator = jax.ops.segment_sum(
        terms.reshape(-1, channels, block_len), flat_targets, num_segments=CBLK
    )
    denominator = jax.ops.segment_sum(
        weights.reshape(-1, block_len), flat_targets, num_segments=CBLK
    )
    composite = (numerator / (1.0 + denominator)[:, None, :]).astype(jnp.bfloat16)
    composite = jnp.transpose(composite, (1, 0, 2)).reshape(channels, TH, TW)
    padded = extended(composite, (("ty", 1), ("tx", 2)), 1)
    hidden = jax.nn.silu(stencil(padded, conv_first, bias_first)).astype(jnp.bfloat16)
    padded_hidden = extended(hidden, (("ty", 1), ("tx", 2)), 1)
    return stencil(padded_hidden, conv_second, bias_second).astype(jnp.bfloat16)


def solution(mesh):
    in_specs = (
        P(("group", "ty", "tx"), None, None),
        P(("group", "ty", "tx"), None, None),
        P(("group", "ty", "tx"), None, None),
        P(("group", "ty", "tx"), None, None),
        P(("group", "ty", "tx"), None),
        P(),
        P(),
        P(),
        P(),
        P(),
    )
    out_specs = P(None, ("group", "ty"), "tx")
    return jax.shard_map(shards, mesh=mesh, in_specs=in_specs, out_specs=out_specs, check_vma=False)
```

profile of v0, /device:TPU:9, one launch (start us, length us, event | category | flops | bytes accessed | tf_op | source)
XLA Modules:
  0.0 454.1 jit_solution(104721033087421726)
XLA Ops:
  1.7 11.4 %all_to_all.10 = s32[16,16,3]{1,2,0:T(4,128)S(1)} all-to-all(s32[16,16,3]{1,2,0:T(4,128)S(1)} %pad_add_fusion), channel_id=1, replica_groups=mesh['group'=2,'ty'=8,'tx'=2] {'ty','tx'}, dimensions={0} | all-to-all | bytes 6144 | tf_op jit(solution)/shard_map/all_to_all | solution.py:78
  24.4 8.6 %gather_fusion.1 = bf16[256,128,128]{2,1,0:T(8,128)(2,1)} fusion(bf16[32,128,128]{2,1,0:T(8,128)(2,1)S(1)} %copy-done.3, s32[1024]{0:T(1024)S(1)} %pad_clamp_fusion), kind=kCustom, calls=%fused_computation.1 | custom fusion | bytes 16778240 | tf_op jit(solution)/shard_map/gather | solution.py:32
  36.2 54.4 %all-to-all-done.1 = bf16[16,16,48,128]{3,2,1,0:T(8,128)(2,1)} async-done(((bf16[16,16,48,128]{3,2,1,0:T(8,128)(2,1)}), bf16[16,16,48,128]{3,2,1,0:T(8,128)(2,1)}, u32[]{:S(2)}, u32[]{:S(2)}) %all-to-all-start.1) | async-done | bytes 3145760 | tf_op jit(solution)/shard_map/all_to_all | solution.py:77
  90.6 12.9 %broadcast_multiply_fusion = f32[16,16,48,128]{3,2,1,0:T(8,128)} fusion(f32[16,16]{1,0:T(8,128)S(1)} %bitcast.107, bf16[16,16,48,128]{3,2,1,0:T(8,128)(2,1)} %all-to-all-done.1, bf16[16,16,128,128]{3,2,1,0:T(8,128)(2,1)} %bitcast.104), kind=kOutput, calls=%fused_computation.66 | convolution fusion | flops 404226048 | bytes 17826816 | tf_op jit(solution)/shard_map/psxy,pscy->pscx/dot_general | solution.py:33
  107.8 36.6 %scatter_fusion = f32[384,48,128]{2,1,0:T(8,128)} fusion(f32[384,48,128]{2,1,0:T(8,128)} %broadcast_in_dim.4, s32[256]{0:T(256)S(1)} %reshape.112, f32[256,48,128]{2,1,0:T(8,128)} %bitcast.105), kind=kCustom, calls=%fused_computation.3 | custom fusion | flops 1572864 | bytes 18875392 | tf_op jit(solution)/shard_map/scatter-add | solution.py:84
  152.4 8.0 %reshape.85 = bf16[48,192,256]{2,1,0:T(8,128)(2,1)} reshape(bf16[48,384,128]{2,1,0:T(8,128)(2,1)} %copy.28) | data formatting | bytes 9437184 | tf_op jit(solution)/shard_map/reshape | solution.py:91
  172.9 8.4 %fusion.75 = f32[192,256,64]{1,2,0:T(8,128)} fusion(bf16[9,64,48]{1,2,0:T(8,128)(2,1)S(1)} %copy-done.9, bf16[48,192,256]{2,1,0:T(8,128)(2,1)S(1)} %copy-done.5), kind=kOutput, calls=%fused_computation.99 | convolution fusion | flops 301989888 | bytes 17313792 | tf_op jit(solution)/shard_map/oc,chw->ohw/dot_general | solution.py:46
  197.3 8.7 %fusion.21 = f32[192,256,64]{1,2,0:T(8,128)} fusion(bf16[48,192,256]{2,0,1:T(8,128)(2,1)} %copy-done.6, bf16[48,1,256]{2,0,1:T(8,128)(2,1)S(1)} %collective-permute-done, bf16[9,64,48]{1,2,0:T(8,128)(2,1)S(1)} %copy-done.9), kind=kOutput, calls=%fused_computation.43 | convolution fusion | flops 311476224 | bytes 17338368 | tf_op jit(solution)/shard_map/oc,chw->ohw/dot_general | solution.py:46
  206.0 8.6 %fusion.25 = f32[192,256,64]{1,2,0:T(8,128)} fusion(bf16[48,1,256]{2,0,1:T(8,128)(2,1)S(1)} %collective-permute-done.1, bf16[48,192,256]{2,0,1:T(8,128)(2,1)} %copy-done.6, bf16[9,64,48]{1,2,0:T(8,128)(2,1)S(1)} %copy-done.9), kind=kOutput, calls=%fused_computation.47 | convolution fusion | flops 311476224 | bytes 17338368 | tf_op jit(solution)/shard_map/oc,chw->ohw/dot_general | solution.py:46
  216.5 9.0 %fusion.39 = f32[192,256,64]{1,2,0:T(8,128)} fusion(bf16[48,194,256]{2,0,1:T(8,128)(2,1)} %copy-done.2, bf16[48,194,1]{2,0,1:T(8,128)(2,1)S(1)} %copy.33, bf16[9,64,48]{1,2,0:T(8,128)(2,1)S(1)} %copy-done.9), kind=kOutput, calls=%fused_computation.58 | convolution fusion | flops 311427072 | bytes 19746816 | tf_op jit(solution)/shard_map/oc,chw->ohw/dot_general | solution.py:46
  225.5 8.9 %fusion.36 = f32[192,256,64]{1,2,0:T(8,128)} fusion(bf16[48,194,256]{2,0,1:T(8,128)(2,1)} %copy-done.2, bf16[48,194,1]{2,0,1:T(8,128)(2,1)S(1)} %copy.33, bf16[9,64,48]{1,2,0:T(8,128)(2,1)S(1)} %copy-done.9), kind=kOutput, calls=%fused_computation.56 | convolution fusion | flops 311427072 | bytes 19746816 | tf_op jit(solution)/shard_map/oc,chw->ohw/dot_general | solution.py:46
  236.9 10.3 %fusion.33 = f32[192,256,64]{1,2,0:T(8,128)} fusion(bf16[48,194,256]{2,0,1:T(8,128)(2,1)} %copy-done.2, bf16[48,194,1]{2,0,1:T(8,128)(2,1)} %copy.36, bf16[9,64,48]{1,2,0:T(8,128)(2,1)S(1)} %copy-done.9), kind=kOutput, calls=%fused_computation.54 | convolution fusion | flops 311427072 | bytes 17381568 | tf_op jit(solution)/shard_map/oc,chw->ohw/dot_general | solution.py:46
  247.1 9.5 %fusion.30 = f32[192,256,64]{1,2,0:T(8,128)} fusion(bf16[48,194,256]{2,0,1:T(8,128)(2,1)} %copy-done.2, bf16[48,194,1]{2,0,1:T(8,128)(2,1)S(1)} %copy-done.7, bf16[9,64,48]{1,2,0:T(8,128)(2,1)S(1)} %copy-done.9), kind=kOutput, calls=%fused_computation.52 | convolution fusion | flops 311427072 | bytes 19746816 | tf_op jit(solution)/shard_map/oc,chw->ohw/dot_general | solution.py:46
  262.9 37.3 %fusion.3 = bf16[64,192,256]{2,0,1:T(8,128)(2,1)} fusion(f32[192,256,64]{1,2,0:T(8,128)} %fusion.25, f32[192,256,64]{1,2,0:T(8,128)} %fusion.43, f32[192,256,64]{1,2,0:T(8,128)} %fusion.30, f32[192,256,64]{1,2,0:T(8,128)} %fusion.75, f32[192,256,64]{1,2,0:T(8,128)} %fusion.36, f32[192,256,64]{1,2,0:T(8,128)} %fusion.33, f32[192,256,64]{1,2,0:T(8,128)} %fusion.39, ...), kind=kOutput, calls=%fused_computation.11 | convolution fusion | flops 355467264 | bytes 111753920 | tf_op jit(solution)/shard_map/oc,chw->ohw/dot_general | solution.py:46
  307.5 9.1 %fusion.56 = f32[192,256,64]{1,2,0:T(8,128)} fusion(bf16[64,192,256]{2,0,1:T(8,128)(2,1)} %fusion.3, bf16[9,64,64]{2,1,0:T(8,128)(2,1)S(1)} %copy-done.8), kind=kOutput, calls=%fused_computation.80 | convolution fusion | flops 402653184 | bytes 18890752 | tf_op jit(solution)/shard_map/oc,chw->ohw/dot_general | solution.py:46
  334.1 9.1 %fusion.16 = f32[192,256,64]{1,2,0:T(8,128)} fusion(bf16[64,192,256]{2,0,1:T(8,128)(2,1)} %fusion.3, bf16[64,1,256]{2,0,1:T(8,128)(2,1)S(1)} %collective-permute-done.4, bf16[9,64,64]{2,1,0:T(8,128)(2,1)S(1)} %copy-done.8), kind=kOutput, calls=%fused_computation.38 | convolution fusion | flops 415236096 | bytes 18923520 | tf_op jit(solution)/shard_map/oc,chw->ohw/dot_general | solution.py:46
  343.3 9.0 %fusion.6 = f32[192,256,64]{1,2,0:T(8,128)} fusion(bf16[64,1,256]{2,0,1:T(8,128)(2,1)S(1)} %collective-permute-done.5, bf16[64,192,256]{2,0,1:T(8,128)(2,1)} %fusion.3, bf16[9,64,64]{2,1,0:T(8,128)(2,1)S(1)} %copy-done.8), kind=kOutput, calls=%fused_computation.27 | convolution fusion | flops 415236096 | bytes 18923520 | tf_op jit(solution)/shard_map/oc,chw->ohw/dot_general | solution.py:46
  359.4 15.2 %pad_maximum_fusion = (bf16[64,194,257]{2,0,1:T(8,128)(2,1)S(1)}, bf16[64,194,257]{2,0,1:T(8,128)(2,1)S(1)}) fusion(bf16[64,194,1]{2,0,1:T(8,128)(2,1)} %copy.42, bf16[64,1,256]{2,0,1:T(8,128)(2,1)S(1)} %collective-permute-done.5, bf16[64,192,256]{2,0,1:T(8,128)(2,1)} %fusion.3, bf16[64,1,256]{2,0,1:T(8,128)(2,1)S(1)} %collective-permute-done.4, ...), kind=kLoop, calls=%fused_computation.13 | loop fusion | flops 51054592 | bytes 19170304 | tf_op jit(solution)/shard_map/concatenate | solution.py:17
  374.6 7.0 %fusion.10 = f32[192,256,64]{1,2,0:T(8,128)} fusion(bf16[64,194,257]{2,0,1:T(8,128)(2,1)S(1)} %get-tuple-element.7, bf16[9,64,64]{2,1,0:T(8,128)(2,1)S(1)} %copy-done.8), kind=kOutput, calls=%fused_computation.31 | convolution fusion | flops 402653184 | bytes 18890752 | tf_op jit(solution)/shard_map/oc,chw->ohw/dot_general | solution.py:46
  382.0 6.6 %fusion.14 = f32[192,256,64]{1,2,0:T(8,128)} fusion(bf16[64,194,257]{2,0,1:T(8,128)(2,1)S(1)} %get-tuple-element.7, bf16[9,64,64]{2,1,0:T(8,128)(2,1)S(1)} %copy-done.8), kind=kOutput, calls=%fused_computation.35 | convolution fusion | flops 402653184 | bytes 18890752 | tf_op jit(solution)/shard_map/oc,chw->ohw/dot_general | solution.py:46
  388.6 6.3 %fusion.12 = f32[192,256,64]{1,2,0:T(8,128)} fusion(bf16[64,194,257]{2,0,1:T(8,128)(2,1)S(1)} %get-tuple-element.8, bf16[9,64,64]{2,1,0:T(8,128)(2,1)S(1)} %copy-done.8), kind=kOutput, calls=%fused_computation.33 | convolution fusion | flops 402653184 | bytes 18890752 | tf_op jit(solution)/shard_map/oc,chw->ohw/dot_general | solution.py:46
  394.8 6.3 %fusion.18 = f32[192,256,64]{1,2,0:T(8,128)} fusion(bf16[64,194,257]{2,0,1:T(8,128)(2,1)S(1)} %get-tuple-element.8, bf16[9,64,64]{2,1,0:T(8,128)(2,1)S(1)} %copy-done.8), kind=kOutput, calls=%fused_computation.40 | convolution fusion | flops 402653184 | bytes 18890752 | tf_op jit(solution)/shard_map/oc,chw->ohw/dot_general | solution.py:46
  407.4 37.4 %fusion.20 = bf16[64,192,256]{2,0,1:T(8,128)(2,1)} fusion(f32[64]{0:T(128)S(1)} %copy-done.10, f32[192,256,64]{1,2,0:T(8,128)} %fusion.6, f32[192,256,64]{1,2,0:T(8,128)} %fusion.8, f32[192,256,64]{1,2,0:T(8,128)} %fusion.10, f32[192,256,64]{1,2,0:T(8,128)} %fusion.56, f32[192,256,64]{1,2,0:T(8,128)} %fusion.12, f32[192,256,64]{1,2,0:T(8,128)} %fusion.14, ...), kind=kOutput, calls=%fused_computation.42 | convolution fusion | flops 434110464 | bytes 113263104 | tf_op jit(solution)/shard_map/oc,chw->ohw/dot_general | solution.py:46
  444.8 9.1 %copy.43 = bf16[64,192,256]{2,1,0:T(8,128)(2,1)} copy(bf16[64,192,256]{2,0,1:T(8,128)(2,1)} %fusion.20) | data formatting | bytes 12582912 | tf_op jit(solution)/shard_map/convert_element_type | solution.py:95
  (86 shorter events, 105.8 us)
Async XLA Ops:
  0.0 14.0 %copy-start = (bf16[256,48,128]{2,1,0:T(8,128)(2,1)S(1)}, bf16[256,48,128]{2,1,0:T(8,128)(2,1)}, u32[]{:S(2)}) copy-start(bf16[256,48,128]{2,1,0:T(8,128)(2,1)} %param.10) | copy-start | bytes 9437188
  16.6 7.8 %copy-start.3 = (bf16[32,128,128]{2,1,0:T(8,128)(2,1)S(1)}, bf16[32,128,128]{2,1,0:T(8,128)(2,1)}, u32[]{:S(2)}) copy-start(bf16[32,128,128]{2,1,0:T(8,128)(2,1)} %param.15) | copy-start | bytes 3145732
  16.7 73.9 %all-to-all-start.1 = ((bf16[16,16,48,128]{3,2,1,0:T(8,128)(2,1)}), bf16[16,16,48,128]{3,2,1,0:T(8,128)(2,1)}, u32[]{:S(2)}, u32[]{:S(2)}) async-start(bf16[16,16,48,128]{3,2,1,0:T(8,128)(2,1)} %bitcast.106), calls=%async_computation.1 | async-start | bytes 6291456 | tf_op jit(solution)/shard_map/all_to_all | solution.py:77
  152.4 20.5 %copy-start.9 = (bf16[9,64,48]{1,2,0:T(8,128)(2,1)S(1)}, bf16[9,64,48]{1,2,0:T(8,128)(2,1)}, u32[]{:S(2)}) copy-start(bf16[9,64,48]{1,2,0:T(8,128)(2,1)} %param.16) | copy-start | bytes 165892
  160.4 12.5 %copy-start.5 = (bf16[48,192,256]{2,1,0:T(8,128)(2,1)S(1)}, bf16[48,192,256]{2,1,0:T(8,128)(2,1)}, u32[]{:S(2)}) copy-start(bf16[48,192,256]{2,1,0:T(8,128)(2,1)} %reshape.85) | copy-start | bytes 14155780
  165.5 15.8 %copy-start.6 = (bf16[48,192,256]{2,0,1:T(8,128)(2,1)}, bf16[48,192,256]{2,0,1:T(8,128)(2,1)S(1)}, u32[]{:S(2)}) copy-start(bf16[48,192,256]{2,0,1:T(8,128)(2,1)S(1)} %copy.29) | copy-start | bytes 14155780
  165.5 15.8 %collective-permute-start = (bf16[48,1,256]{2,0,1:T(8,128)(2,1)S(1)}, bf16[48,1,256]{2,0,1:T(8,128)(2,1)S(1)}, u32[]{:S(2)}, u32[]{:S(2)}) collective-permute-start(bf16[48,1,256]{2,0,1:T(8,128)(2,1)S(1)} %get-tuple-element.15), channel_id=1, source_target_pairs={{0,2},{2,4},{4,6},{6,8},{8,10},{10,12},{12,14},{1,3},{3,5},{5,7},{... | collective-permute-start | bytes 73736 | tf_op jit(solution)/shard_map/ppermute | solution.py:19
  170.8 13.3 %collective-permute-start.1 = (bf16[48,1,256]{2,0,1:T(8,128)(2,1)S(1)}, bf16[48,1,256]{2,0,1:T(8,128)(2,1)S(1)}, u32[]{:S(2)}, u32[]{:S(2)}) collective-permute-start(bf16[48,1,256]{2,0,1:T(8,128)(2,1)S(1)} %get-tuple-element.16), channel_id=1, source_target_pairs={{2,0},{4,2},{6,4},{8,6},{10,8},{12,10},{14,12},{3,1},{5,3},{7,5},{... | collective-permute-start | bytes 73736 | tf_op jit(solution)/shard_map/ppermute | solution.py:21
  191.4 23.3 %collective-permute-start.2 = (bf16[48,194,1]{1,0,2:T(8,128)(2,1)S(1)}, bf16[48,194,1]{1,0,2:T(8,128)(2,1)S(1)}, u32[]{:S(2)}, u32[]{:S(2)}) collective-permute-start(bf16[48,194,1]{1,0,2:T(8,128)(2,1)S(1)} %copy.32), channel_id=1, source_target_pairs={{0,1},{2,3},{4,5},{6,7},{8,9},{10,11},{12,13},{14,15},{16,17},{18,... | collective-permute-start | bytes 55880 | tf_op jit(solution)/shard_map/ppermute | solution.py:19
  194.2 40.2 %collective-permute-start.3 = (bf16[48,194,1]{1,0,2:T(8,128)(2,1)S(1)}, bf16[48,194,1]{1,0,2:T(8,128)(2,1)S(1)}, u32[]{:S(2)}, u32[]{:S(2)}) collective-permute-start(bf16[48,194,1]{1,0,2:T(8,128)(2,1)S(1)} %copy.35), channel_id=1, source_target_pairs={{1,0},{3,2},{5,4},{7,6},{9,8},{11,10},{13,12},{15,14},{17,16},{19,... | collective-permute-start | bytes 55880 | tf_op jit(solution)/shard_map/ppermute | solution.py:21
  236.9 10.3 %copy-start.7 = (bf16[48,194,1]{2,0,1:T(8,128)(2,1)S(1)}, bf16[48,194,1]{2,0,1:T(8,128)(2,1)}, u32[]{:S(2)}) copy-start(bf16[48,194,1]{2,0,1:T(8,128)(2,1)} %copy.36) | copy-start | bytes 55876
  236.9 19.7 %slice-start = ((s8[4767744]{0:T(1024)(128)(4,1)}), s8[4194304]{0:T(1024)(128)(4,1)S(1)}, s32[]{:S(2)}) async-start(s8[4767744]{0:T(1024)(128)(4,1)} %bitcast.100), calls=%async_computation.2 | async-start | bytes 8388608
  247.1 9.5 %slice-start.1 = ((s8[4767744]{0:T(1024)(128)(4,1)}), s8[573440]{0:T(1024)(128)(4,1)S(1)}, s32[]{:S(2)}) async-start(s8[4767744]{0:T(1024)(128)(4,1)} %bitcast.100), calls=%async_computation.3 | async-start | bytes 1146880
  256.6 6.2 %copy-start.11 = (f32[64]{0:T(128)S(1)}, f32[64]{0:T(128)}, u32[]{:S(2)}) copy-start(f32[64]{0:T(128)} %param.17) | copy-start | bytes 772
  262.8 44.6 %copy-start.8 = (bf16[9,64,64]{2,1,0:T(8,128)(2,1)S(1)}, bf16[9,64,64]{2,1,0:T(8,128)(2,1)}, u32[]{:S(2)}) copy-start(bf16[9,64,64]{2,1,0:T(8,128)(2,1)} %param.18) | copy-start | bytes 221188
  301.0 15.6 %collective-permute-start.4 = (bf16[64,1,256]{2,0,1:T(8,128)(2,1)S(1)}, bf16[64,1,256]{2,0,1:T(8,128)(2,1)S(1)}, u32[]{:S(2)}, u32[]{:S(2)}) collective-permute-start(bf16[64,1,256]{2,0,1:T(8,128)(2,1)S(1)} %get-tuple-element.11), channel_id=1, source_target_pairs={{0,2},{2,4},{4,6},{6,8},{8,10},{10,12},{12,14},{1,3},{3,5},{5,7},{... | collective-permute-start | bytes 98312 | tf_op jit(solution)/shard_map/ppermute | solution.py:19
  304.3 12.2 %slice-start.2 = ((s8[6291456]{0:T(1024)(128)(4,1)}), s8[4194304]{0:T(1024)(128)(4,1)S(1)}, s32[]{:S(2)}) async-start(s8[6291456]{0:T(1024)(128)(4,1)} %bitcast.102), calls=%async_computation.4 | async-start | bytes 8388608
  304.3 12.2 %slice-start.3 = ((s8[6291456]{0:T(1024)(128)(4,1)}), s8[2097152]{0:T(1024)(128)(4,1)S(1)}, s32[]{:S(2)}) async-start(s8[6291456]{0:T(1024)(128)(4,1)} %bitcast.102), calls=%async_computation.5 | async-start | bytes 4194304
  304.4 12.2 %collective-permute-start.5 = (bf16[64,1,256]{2,0,1:T(8,128)(2,1)S(1)}, bf16[64,1,256]{2,0,1:T(8,128)(2,1)S(1)}, u32[]{:S(2)}, u32[]{:S(2)}) collective-permute-start(bf16[64,1,256]{2,0,1:T(8,128)(2,1)S(1)} %get-tuple-element.12), channel_id=1, source_target_pairs={{2,0},{4,2},{6,4},{8,6},{10,8},{12,10},{14,12},{3,1},{5,3},{7,5},{... | collective-permute-start | bytes 98312 | tf_op jit(solution)/shard_map/ppermute | solution.py:21
  325.9 26.4 %collective-permute-start.6 = (bf16[64,194,1]{1,0,2:T(8,128)(2,1)S(1)}, bf16[64,194,1]{1,0,2:T(8,128)(2,1)S(1)}, u32[]{:S(2)}, u32[]{:S(2)}) collective-permute-start(bf16[64,194,1]{1,0,2:T(8,128)(2,1)S(1)} %copy.39), channel_id=1, source_target_pairs={{0,1},{2,3},{4,5},{6,7},{8,9},{10,11},{12,13},{14,15},{16,17},{18,... | collective-permute-start | bytes 74504 | tf_op jit(solution)/shard_map/ppermute | solution.py:19
  331.1 24.9 %collective-permute-start.7 = (bf16[64,194,1]{1,0,2:T(8,128)(2,1)S(1)}, bf16[64,194,1]{1,0,2:T(8,128)(2,1)S(1)}, u32[]{:S(2)}, u32[]{:S(2)}) collective-permute-start(bf16[64,194,1]{1,0,2:T(8,128)(2,1)S(1)} %copy.41), channel_id=1, source_target_pairs={{1,0},{3,2},{5,4},{7,6},{9,8},{11,10},{13,12},{15,14},{17,16},{19,... | collective-permute-start | bytes 74504 | tf_op jit(solution)/shard_map/ppermute | solution.py:21
  374.6 7.4 %copy-start.4 = (bf16[64,194,257]{2,0,1:T(8,128)(2,1)}, bf16[64,194,257]{2,0,1:T(8,128)(2,1)S(1)}, u32[]{:S(2)}) copy-start(bf16[64,194,257]{2,0,1:T(8,128)(2,1)S(1)} %get-tuple-element.7) | copy-start | bytes 19145476
  401.2 6.2 %copy-start.10 = (f32[64]{0:T(128)S(1)}, f32[64]{0:T(128)}, u32[]{:S(2)}) copy-start(f32[64]{0:T(128)} %param.19) | copy-start | bytes 772
  407.4 46.5 %copy-start.1 = (bf16[256,48,128]{2,1,0:T(8,128)(2,1)S(1)}, bf16[256,48,128]{2,1,0:T(8,128)(2,1)}, u32[]{:S(2)}) copy-start(bf16[256,48,128]{2,1,0:T(8,128)(2,1)} %param.10) | copy-start | bytes 9437188
  (1 other events, 2.2 us)
where the time goes:
time: 461 us; the launch traced here: 454 us
  matrix products  217 us (47%)
  local copies, waits for them, and re-layouts  77.6 us (17%)
  other arithmetic  64.7 us (14%)
  waiting for transfers between devices  54.4 us (12%)
  starting transfers between devices  28.5 us (6%)
  blocking collectives  11.4 us (2%)
    dot_general x18, matrix products, stencil(): jnp.einsum('oc,chw->ohw', kernel[3 * tap_row + tap_col], window, preferre...  204 us
    all_to_all x1, waiting for transfers between devices, shards(): lax.all_to_all(packets, ('ty', 'tx'), split_axis=0, concat_axis=0, tiled=...  54.4 us
    scatter-add x1, other arithmetic, shards(): jax.ops.segment_sum(terms.reshape(-1, channels, block_len), flat_targets,...  36.6 us
    concatenate x2, other arithmetic, extended(): jnp.concatenate([lax.ppermute(tail, axis, [(i, (i + 1) % count) for i in...  16.4 us
    reshape x2, local copies, waits for them, and re-layouts, shards(): composite = jnp.transpose(composite, (1, 0, 2)).reshape(channels, TH, TW)  13.1 us
    dot_general x1, matrix products, slot_terms(): jnp.einsum('psxy,pscy->pscx', matrices, samples, preferred_element_type=j...  12.9 us
    slice x4, local copies, waits for them, and re-layouts, extended(): head = lax.slice_in_dim(cells, 0, width, axis=dim)  12.1 us
    all_to_all x1, blocking collectives, shards(): lax.all_to_all(slot_info, ('ty', 'tx'), split_axis=0, concat_axis=0, tile...  11.4 us
  transfers between devices with their start and end apart: 9, of which 1 were waited for; matrix products, arithmetic and copies ran while one was open for 22% of the time, Pallas kernels for 0%

commit v1 on v0

v1 whole, which is shorter than its diff:
```python
import functools

import jax
import jax.numpy as jnp
from jax import lax
from jax.experimental import pallas as pl
from jax.experimental.pallas import tpu as pltpu
from jax.sharding import PartitionSpec as P

TH = 192
TW = 256
CBLK = 384
LANES = 128
HALO = 2
EDGE_TILES = 2
INFO_ROWS = 16
CELL_BASE = 32
STEPS = 4
UNROLL = 8
GROUP_ONE = 3
GROUP_TWO = 2
OUT_ROWS = 16
VMEM_LIMIT = 56 * 1024 * 1024

F32 = jnp.float32
BF16 = jnp.bfloat16


def lane_index(shape):
    return lax.broadcasted_iota(jnp.int32, shape, len(shape) - 1)


def silu(value):
    half = 0.5 * value
    return half + half * jnp.tanh(half)


def composite_kernel(
    capacity, channels, cell_ref, templ_ref, col_ref, recv_ref, table_ref, weight_ref,
    comp_ref, edge_ref, acc, den, strip,
):
    step = pl.program_id(0)
    sources = recv_ref.shape[0]
    col = col_ref[0]

    @pl.when(step == 0)
    def clear():
        def clear_block(i, carry):
            acc[i] = jnp.zeros(acc.shape[1:], F32)
            return carry

        lax.fori_loop(0, acc.shape[0], clear_block, 0, unroll=4)
        den[...] = jnp.zeros(den.shape, F32)
        strip[...] = jnp.zeros(strip.shape, F32)

    per_source = capacity // UNROLL

    def add_slots(i, carry):
        source = i // per_source
        first = (i % per_source) * UNROLL
        slot = (step * sources + source) * capacity + first
        terms = []
        for u in range(UNROLL):
            row = pl.multiple_of((first + u) * channels, 16)
            block = recv_ref[source, pl.ds(row, channels), :]
            terms.append(
                jnp.dot(block, table_ref[templ_ref[slot + u]], preferred_element_type=F32)
            )
        for u in range(UNROLL):
            cell = cell_ref[slot + u]
            acc[cell] += terms[u]
            den[pl.ds(cell, 1), :] += weight_ref[pl.ds(templ_ref[slot + u], 1), :]
        return carry

    lax.fori_loop(0, sources * per_source, add_slots, 0)

    @pl.when(step == pl.num_programs(0) - 1)
    def finish():
        den[...] = 1.0 / (1.0 + den[...])
        lane = lane_index((channels, LANES))

        def one_row(r, carry):
            out = pl.multiple_of(r * channels, 16)
            parts = []
            for m in range(2):
                value = (acc[2 * r + m] * den[pl.ds(2 * r + m, 1), :]).astype(BF16)
                comp_ref[pl.ds(out, channels), m * LANES : (m + 1) * LANES] = value
                parts.append(value)
            side = jnp.where(col == 0, parts[1], parts[0]).astype(F32)
            at = r + HALO
            start = jnp.where(col == 0, LANES - 2, 0)
            side = pltpu.roll(side, (at - start + LANES) % LANES, 1)
            for p in range(2):
                tile = (at + p) // LANES
                strip[p, tile] = jnp.where(lane == (at + p) % LANES, side, strip[p, tile])
            return carry

        lax.fori_loop(0, TH, one_row, 0, unroll=2)
        edge_ref[...] = strip[...].astype(BF16)


def encoder_kernel(
    channels, hid, place_ref, comp_ref, up_ref, down_ref, own_ref, side_ref, side_up_ref, side_down_ref,
    first_ref, second_ref, edge_first_ref, edge_second_ref, bias_first_ref, bias_second_ref,
    out_ref, field, hidden, edge_one, edge_two, stage, sems,
):
    col = place_ref[0]
    at_top = place_ref[1]
    at_bottom = place_ref[2]
    target = jnp.where(col == 0, LANES - 1, 0)
    left_scale = jnp.where(col == 0, 0.0, 1.0)
    right_scale = jnp.where(col == 0, 1.0, 0.0)
    rows_ext = TH + 2 * HALO
    rows_hid = TH + 2

    def taps_sum(full, count, edge, first_row):
        rows = count * hid
        parts = []
        for r in range(count):
            at = first_row + r
            parts.append(
                pltpu.roll(edge[at // LANES], (target - at % LANES + LANES) % LANES, 1)
            )
        fix = jnp.concatenate(parts, axis=0)
        lane = lane_index((rows, LANES))
        left = full[0:rows]
        mid = full[rows : 2 * rows]
        right = full[2 * rows : 3 * rows]
        left_a = pltpu.roll(left[:, :LANES], 1, 1)
        left_b = pltpu.roll(left[:, LANES:], 1, 1)
        right_a = pltpu.roll(right[:, :LANES], LANES - 1, 1)
        right_b = pltpu.roll(right[:, LANES:], LANES - 1, 1)
        out_a = (
            mid[:, :LANES]
            + jnp.where(lane == 0, fix * left_scale, left_a)
            + jnp.where(lane == LANES - 1, right_b, right_a)
        )
        out_b = (
            mid[:, LANES:]
            + jnp.where(lane == 0, left_a, left_b)
            + jnp.where(lane == LANES - 1, fix * right_scale, right_b)
        )
        return out_a, out_b

    @pl.when(pl.program_id(0) == 0)
    def first_layer():
        copies = [
            pltpu.make_async_copy(
                comp_ref, field.at[pl.ds(HALO * channels, TH * channels), :], sems.at[0]
            ),
            pltpu.make_async_copy(up_ref, field.at[pl.ds(0, HALO * channels), :], sems.at[1]),
            pltpu.make_async_copy(
                down_ref,
                field.at[pl.ds((TH + HALO) * channels, HALO * channels), :],
                sems.at[2],
            ),
        ]
        for copy in copies:
            copy.start()
        for copy in copies:
            copy.wait()

        lane = lane_index((channels, LANES))
        strips = []
        for p in range(2):
            head = jnp.where(
                (lane >= p) & (lane < p + HALO),
                pltpu.roll(side_up_ref[p].astype(F32), (LANES - TH % LANES) % LANES, 1),
                side_ref[p, 0].astype(F32),
            )
            base = (TH + HALO) % LANES + p
            tail = jnp.where(
                (lane >= base) & (lane < base + HALO),
                pltpu.roll(side_down_ref[p].astype(F32), TH % LANES, 1),
                side_ref[p, 1].astype(F32),
            )
            strips.append(jnp.concatenate([head, tail], axis=1))
        strips[1] = pltpu.roll(strips[1], EDGE_TILES * LANES - 1, 1)
        near = jnp.where(col == 0, strips[0], strips[1])
        far = jnp.where(col == 0, strips[1], strips[0])

        own = [
            jnp.concatenate([own_ref[p, 0], own_ref[p, 1]], axis=1).astype(F32) for p in range(2)
        ]
        own[1] = pltpu.roll(own[1], EDGE_TILES * LANES - 1, 1)
        own = jnp.where(col == 0, own[1], own[0])
        wide = lane_index((channels, EDGE_TILES * LANES))
        for k, row in enumerate([0, 1, TH + HALO, TH + HALO + 1]):
            tiles = field[row * channels : (row + 1) * channels, :].astype(F32)
            tile = jnp.where(col == 0, tiles[:, LANES:], tiles[:, :LANES])
            moved = pltpu.roll(tile, (row % LANES - target + LANES) % LANES, 1)
            own = jnp.where(wide == row, jnp.concatenate([moved, moved], axis=1), own)

        stack = jnp.concatenate([near, far, own], axis=0).astype(BF16)
        result = jnp.dot(edge_first_ref[...], stack, preferred_element_type=F32)
        span = EDGE_TILES * LANES
        total = result[0 : 2 * hid]
        for a in range(1, 3):
            total = total + pltpu.roll(result[2 * hid * a : 2 * hid * (a + 1)], span - a, 1)
        beyond = total[0:hid] + bias_first_ref[0:hid, 0:1]
        beyond = silu(beyond)
        lane_hid = lane_index((hid, span))
        drop = ((lane_hid == 0) & (at_top == 1)) | ((lane_hid == rows_hid - 1) & (at_bottom == 1))
        beyond = jnp.where(drop | (lane_hid >= rows_hid), 0.0, beyond)
        spill = jnp.dot(edge_second_ref[...], beyond.astype(BF16), preferred_element_type=F32)
        second = spill[0:hid]
        for a in range(1, 3):
            second = second + pltpu.roll(spill[hid * a : hid * (a + 1)], span - a, 1)
        for tile in range(EDGE_TILES):
            edge_one[tile] = total[hid : 2 * hid, tile * LANES : (tile + 1) * LANES]
            edge_two[tile] = second[:, tile * LANES : (tile + 1) * LANES]

        rows = GROUP_ONE * hid
        groups = -(-rows_hid // GROUP_ONE)

        def one_group(g, carry):
            first_row = jnp.minimum(g * GROUP_ONE, rows_hid - GROUP_ONE)
            window = field[
                pl.ds(pl.multiple_of(first_row * channels, 16), (GROUP_ONE + 2) * channels), :
            ]
            full = jnp.dot(first_ref[...], window, preferred_element_type=F32)
            out_a, out_b = taps_sum(full, GROUP_ONE, edge_one, first_row)
            place = pl.ds(pl.multiple_of(first_row * hid, 16), rows)
            bias = bias_first_ref[...]
            hidden[place, 0:LANES] = silu(out_a + bias).astype(BF16)
            hidden[place, LANES:TW] = silu(out_b + bias).astype(BF16)
            return carry

        lax.fori_loop(0, groups, one_group, 0)

        @pl.when(at_top == 1)
        def clear_top():
            hidden[0:hid, :] = jnp.zeros((hid, TW), BF16)

        @pl.when(at_bottom == 1)
        def clear_bottom():
            hidden[(rows_hid - 1) * hid : rows_hid * hid, :] = jnp.zeros((hid, TW), BF16)

    base = pl.program_id(0) * OUT_ROWS
    for g in range(OUT_ROWS // GROUP_TWO):
        row = base + g * GROUP_TWO
        window = hidden[pl.ds(pl.multiple_of(row * hid, 16), (GROUP_TWO + 2) * hid), :]
        full = jnp.dot(second_ref[...], window, preferred_element_type=F32)
        out_a, out_b = taps_sum(full, GROUP_TWO, edge_two, row)
        bias = bias_second_ref[...]
        for half, value in enumerate((out_a + bias, out_b + bias)):
            for r in range(GROUP_TWO):
                stage[half, pl.ds(g * GROUP_TWO + r, hid, stride=OUT_ROWS), :] = value[
                    r * hid : (r + 1) * hid
                ]
    for half in range(2):
        out_ref[:, :, half * LANES : (half + 1) * LANES] = (
            stage[half].reshape(hid, OUT_ROWS, LANES).astype(BF16)
        )


def banded(kernel, count):
    hid, channels = kernel.shape[1:]
    taps = kernel.reshape(3, 3, hid, channels)
    full = jnp.zeros((3, count, hid, count + 2, channels), kernel.dtype)
    for r in range(count):
        full = full.at[:, r, :, r : r + 3, :].set(jnp.transpose(taps, (1, 2, 0, 3)))
    return full.reshape(3 * count * hid, (count + 2) * channels)


def whole_in_vmem():
    return pl.BlockSpec(memory_space=pltpu.VMEM)


def composite(received, cells, templates, col, table, row_weight, capacity, channels):
    peers = received.shape[0]
    per_step = peers // STEPS
    rows = received.shape[1]
    return pl.pallas_call(
        functools.partial(composite_kernel, capacity, channels),
        grid_spec=pltpu.PrefetchScalarGridSpec(
            num_scalar_prefetch=3,
            grid=(STEPS,),
            in_specs=[
                pl.BlockSpec((per_step, rows, LANES), lambda i, *_: (i, 0, 0)),
                whole_in_vmem(),
                whole_in_vmem(),
            ],
            out_specs=[whole_in_vmem(), whole_in_vmem()],
            scratch_shapes=[
                pltpu.VMEM((CBLK + 1, channels, LANES), F32),
                pltpu.VMEM((CBLK + 8, LANES), F32),
                pltpu.VMEM((2, EDGE_TILES, channels, LANES), F32),
            ],
        ),
        out_shape=[
            jax.ShapeDtypeStruct((TH * channels, TW), BF16),
            jax.ShapeDtypeStruct((2, EDGE_TILES, channels, LANES), BF16),
        ],
        compiler_params=pltpu.CompilerParams(
            dimension_semantics=("arbitrary",), vmem_limit_bytes=VMEM_LIMIT
        ),
        name="composite",
    )(cells, templates, col, received, table, row_weight)


def encoder(place, field, up, down, own, side, side_up, side_down, weights, channels, hid):
    return pl.pallas_call(
        functools.partial(encoder_kernel, channels, hid),
        grid_spec=pltpu.PrefetchScalarGridSpec(
            num_scalar_prefetch=1,
            grid=(TH // OUT_ROWS,),
            in_specs=[pl.BlockSpec(memory_space=pl.ANY)] * 3 + [whole_in_vmem()] * 10,
            out_specs=pl.BlockSpec((hid, OUT_ROWS, TW), lambda i, *_: (0, i, 0)),
            scratch_shapes=[
                pltpu.VMEM(((TH + 2 * HALO) * channels, TW), BF16),
                pltpu.VMEM(((TH + 2) * hid, TW), BF16),
                pltpu.VMEM((EDGE_TILES, hid, LANES), F32),
                pltpu.VMEM((EDGE_TILES, hid, LANES), F32),
                pltpu.VMEM((2, hid * OUT_ROWS, LANES), F32),
                pltpu.SemaphoreType.DMA((3,)),
            ],
        ),
        out_shape=jax.ShapeDtypeStruct((hid, TH, TW), BF16),
        compiler_params=pltpu.CompilerParams(
            dimension_semantics=("arbitrary",), vmem_limit_bytes=VMEM_LIMIT
        ),
        name="encoder",
    )(place, field, up, down, own, side, side_up, side_down, *weights)


def layer_weights(conv_first, bias_first, conv_second, bias_second, col):
    hid = conv_first.shape[1]
    inner = jnp.where(col == 0, 2, 0)
    taps_one = conv_first.reshape(3, 3, hid, -1)
    taps_two = conv_second.reshape(3, 3, hid, -1)
    in_one = lax.dynamic_index_in_dim(taps_one, inner, 1, keepdims=False)
    out_one = lax.dynamic_index_in_dim(taps_one, 2 - inner, 1, keepdims=False)
    in_two = lax.dynamic_index_in_dim(taps_two, inner, 1, keepdims=False)
    nothing = jnp.zeros_like(in_one)
    beyond = jnp.concatenate([taps_one[:, 1], in_one, out_one], axis=2)
    onto = jnp.concatenate([in_one, nothing, nothing], axis=2)
    edge_first = jnp.concatenate([beyond, onto], axis=1).reshape(6 * hid, -1)
    edge_second = in_two.reshape(3 * hid, -1)
    spread_one = jnp.broadcast_to(bias_first[None, :, None], (GROUP_ONE, hid, LANES))
    spread_two = jnp.broadcast_to(bias_second[None, :, None], (GROUP_TWO, hid, LANES))
    return (
        banded(conv_first, GROUP_ONE),
        banded(conv_second, GROUP_TWO),
        edge_first,
        edge_second,
        spread_one.reshape(-1, LANES),
        spread_two.reshape(-1, LANES),
    )


def shards(
    sweeps, route_block, route_cell, route_templ, route_count, footprint,
    conv_first, bias_first, conv_second, bias_second,
):
    peers, capacity = route_block.shape[1:]
    channels = sweeps.shape[1]
    hid = conv_first.shape[1]
    rows = lax.axis_size("ty")
    col = lax.axis_index("tx")
    row = lax.axis_index("ty")

    live = lax.broadcasted_iota(jnp.int32, (peers, capacity), 1) < route_count[0][:, None]
    cell = jnp.where(live, route_cell[0], CBLK)
    info = jnp.stack([cell // CELL_BASE, cell % CELL_BASE, route_templ[0]], axis=1).astype(BF16)
    info = jnp.pad(info, ((0, 0), (0, INFO_ROWS - 3), (0, LANES - capacity)))
    packets = sweeps[route_block[0]].reshape(peers, capacity * channels, LANES)
    packets = jnp.concatenate([packets, info], axis=1)
    received = lax.all_to_all(packets, ("ty", "tx"), split_axis=0, concat_axis=0, tiled=True)

    arrived = received[:, capacity * channels : capacity * channels + 3, :capacity].astype(jnp.int32)
    cells = (arrived[:, 0] * CELL_BASE + arrived[:, 1]).reshape(-1)
    templates = arrived[:, 2].reshape(-1)
    table = jnp.transpose(footprint, (0, 2, 1))
    row_weight = jnp.sum(footprint.astype(F32), axis=2)
    field, own = composite(
        received, cells, templates, col.reshape(1), table, row_weight, capacity, channels
    )

    rim = HALO * channels
    onward = [(i, i + 1) for i in range(rows - 1)]
    back = [(i + 1, i) for i in range(rows - 1)]
    cross = [
        (2 * i + j, 2 * k + 1 - j) for i, k in onward for j in range(2)
    ]
    cross_back = [(b, a) for a, b in cross]
    up = lax.ppermute(field[-rim:], "ty", onward)
    down = lax.ppermute(field[:rim], "ty", back)
    side = lax.ppermute(own, "tx", [(0, 1), (1, 0)])
    side_up = lax.ppermute(own[:, 1], ("ty", "tx"), cross)
    side_down = lax.ppermute(own[:, 0], ("ty", "tx"), cross_back)

    place = jnp.stack([col, row == 0, row == rows - 1]).astype(jnp.int32)
    weights = layer_weights(conv_first, bias_first, conv_second, bias_second, col)
    return encoder(place, field, up, down, own, side, side_up, side_down, weights, channels, hid)


def solution(mesh):
    split = ("group", "ty", "tx")
    in_specs = (
        P(split, None, None),
        P(split, None, None),
        P(split, None, None),
        P(split, None, None),
        P(split, None),
        P(),
        P(),
        P(),
        P(),
        P(),
    )
    out_specs = P(None, ("group", "ty"), "tx")
    return jax.shard_map(shards, mesh=mesh, in_specs=in_specs, out_specs=out_specs, check_vma=False)
```

time: 461 us -> 193 us (0.42)
  matrix products: 217 us -> 0 us
  Pallas kernels: 0 us -> 66.5 us
  other arithmetic: 64.7 us -> 10 us
  local copies, waits for them, and re-layouts: 77.6 us -> 32.1 us
  blocking collectives: 11.4 us -> 0 us
  starting transfers between devices: 28.5 us -> 20.6 us
  waiting for transfers between devices: 54.4 us -> 61 us
    dot_general x19 -> x0, matrix products: 217 us -> none  [the longest x18 204 us: stencil(): jnp.einsum('oc,chw->ohw', kernel[3 * tap_row + tap_col], window, preferre...]
    pallas_call x0 -> x2, Pallas kernels: none -> 66.5 us  [the longest x1 45 us: encoder(): pl.pallas_call(functools.partial(encoder_kernel, channels, hid), grid_spe...]
    scatter-add x2 -> x0, other arithmetic: 39.5 us -> none  [the longest x1 36.6 us: shards(): jax.ops.segment_sum(terms.reshape(-1, channels, block_len), flat_targets,...]
    slice x8 -> x1, local copies, waits for them, and re-layouts: 19.4 us -> 1.47 us  [shards(): down = lax.ppermute(field[:rim], 'ty', back)]
    concatenate x2, other arithmetic: 16.4 us -> 3.9 us  [the longest x1 3.81 us: shards(): packets = jnp.concatenate([packets, info], axis=1)]
    ppermute x4 -> x0, local copies, waits for them, and re-layouts: 11.4 us -> none  [the longest x2 5.86 us: extended(): lax.ppermute(head, axis, [((i + 1) % count, i) for i in range(ends)])]
    all_to_all x1 -> x0, blocking collectives: 11.4 us -> none  [shards(): lax.all_to_all(slot_info, ('ty', 'tx'), split_axis=0, concat_axis=0, tile...]
    convert_element_type x1 -> x0, local copies, waits for them, and re-layouts: 9.05 us -> none  [shards(): return stencil(padded_hidden, conv_second, bias_second).astype(jnp.bfloat16)]
  transfers between devices with their start and end apart: 9 -> 6, of which waited for: 1 -> 1; matrix products, arithmetic and copies ran while one was open for 22% -> 15% of each run, Pallas kernels for 0% -> 0%
where the time goes in v1:
time: 193 us; the launch traced here: 190 us
  Pallas kernels  66.5 us (34%)
  waiting for transfers between devices  61 us (32%)
  local copies, waits for them, and re-layouts  32.1 us (17%)
  starting transfers between devices  20.6 us (11%)
  other arithmetic  10 us (5%)
    all_to_all x1, waiting for transfers between devices, shards(): lax.all_to_all(packets, ('ty', 'tx'), split_axis=0, concat_axis=0, tiled=...  60.9 us
    pallas_call x1, Pallas kernels, encoder(): pl.pallas_call(functools.partial(encoder_kernel, channels, hid), grid_spe...  45 us
    pallas_call x1, Pallas kernels, composite(): pl.pallas_call(functools.partial(composite_kernel, capacity, channels), g...  21.4 us
    scatter x5, local copies, waits for them, and re-layouts, banded(): full = full.at[:, r, :, r:r + 3, :].set(jnp.transpose(taps, (1, 2, 0, 3)))  8.12 us
    reshape x3, local copies, waits for them, and re-layouts, banded(): return full.reshape(3 * count * hid, (count + 2) * channels)  6.97 us
    all_to_all x1, starting transfers between devices, shards(): lax.all_to_all(packets, ('ty', 'tx'), split_axis=0, concat_axis=0, tiled=...  6.74 us
    ppermute x1, starting transfers between devices, shards(): side_up = lax.ppermute(own[:, 1], ('ty', 'tx'), cross)  4.81 us
    ppermute x1, starting transfers between devices, shards(): up = lax.ppermute(field[-rim:], 'ty', onward)  4.44 us
  transfers between devices with their start and end apart: 6, of which 1 were waited for; matrix products, arithmetic and copies ran while one was open for 15% of the time, Pallas kernels for 0%

profile of v1, /device:TPU:9, one launch (start us, length us, event | category | flops | bytes accessed | tf_op | source)
XLA Modules:
  0.0 190.4 jit_solution(16020131473224824437)
XLA Ops:
  0.0 0.8 convert_bitcast_fusion
  2.6 2.6 %gather_fusion = bf16[256,48,128]{2,1,0:T(8,128)(2,1)} fusion(bf16[256,48,128]{2,1,0:T(8,128)(2,1)S(1)} %copy-done, s32[1024]{0:T(1024)S(1)} %pad_clamp_fusion), kind=kCustom, calls=%fused_computation | custom fusion | bytes 6292480 | tf_op jit(solution)/shard_map/gather | solution.py:367
  5.3 3.8 %pad_maximum_fusion = bf16[16,784,128]{2,1,0:T(8,128)(2,1)} fusion(bf16[16,16,128]{2,1,0:T(8,128)(2,1)S(1)} %fusion.10, bf16[16,768,128]{2,1,0:T(8,128)(2,1)} %bitcast.43), kind=kLoop, calls=%fused_computation.1 | loop fusion | flops 6422528 | bytes 6422528 | tf_op jit(solution)/shard_map/concatenate | solution.py:368
  9.1 6.7 %all-to-all-start = ((bf16[16,784,128]{2,1,0:T(8,128)(2,1)}), bf16[16,784,128]{2,1,0:T(8,128)(2,1)}, u32[]{:S(2)}, u32[]{:S(2)}) async-start(bf16[16,784,128]{2,1,0:T(8,128)(2,1)} %pad_maximum_fusion), calls=%async_computation | async-start | bytes 6422528 | tf_op jit(solution)/shard_map/all_to_all | solution.py:369
  15.8 2.3 %copy.41 = bf16[32,128,128]{1,2,0:T(8,128)(2,1)} copy(bf16[32,128,128]{2,1,0:T(8,128)(2,1)} %param.25) | data formatting | bytes 2097152 | tf_op args[5]
  18.2 0.9 scatter.16
  19.1 1.4 constant_dynamic-slice_fusion
  20.6 2.2 %convert_reduce_fusion.weight_ref = f32[32,128]{1,0:T(8,128)} fusion(bf16[32,128,128]{2,1,0:T(8,128)(2,1)} %param.25), kind=kLoop, calls=%fused_computation.2 | loop fusion | flops 1044480 | bytes 1064960 | tf_op jit(solution)/shard_map/reduce_sum | solution.py:375
  24.1 60.9 %all-to-all-done.recv_ref = bf16[16,784,128]{2,1,0:T(8,128)(2,1)} async-done(((bf16[16,784,128]{2,1,0:T(8,128)(2,1)}), bf16[16,784,128]{2,1,0:T(8,128)(2,1)}, u32[]{:S(2)}, u32[]{:S(2)}) %all-to-all-start) | async-done | bytes 3211296 | tf_op jit(solution)/shard_map/all_to_all | solution.py:369
  87.2 21.4 %composite.1 = (bf16[9216,256]{1,0:T(8,128)(2,1)}, bf16[2,2,48,128]{3,2,1,0:T(8,128)(2,1)}) custom-call(s32[256]{0:T(256)} %add.71.cell_ref, s32[256]{0:T(256)} %reshape_squeeze.3.templ_ref, s32[1]{0:T(128)} %bitcast.col_ref, bf16[16,784,128]{2,1,0:T(8,128)(2,1)} %all-to-all-done.recv_ref, bf16[32,128,128]{2,1,0:T(8,128)(2,1)} %bitcast.44, ...), custom_call_target="tpu_custom_call" | custom-call | tf_op jit(solution)/shard_map/composite/pallas_call | solution.py:274
  108.6 1.4 slice_bitcast_fusion.1
  110.8 1.9 %collective-permute-start.4 = (bf16[2,48,128]{2,1,0:T(8,128)(2,1)}, bf16[2,48,128]{2,1,0:T(8,128)(2,1)}, u32[]{:S(2)}, u32[]{:S(2)}) collective-permute-start(bf16[2,48,128]{2,1,0:T(8,128)(2,1)} %get-tuple-element.78), channel_id=1, source_target_pairs={{3,0},{2,1},{5,2},{4,3},{7,4},{6,5},{9,6},{8,7},{11,8},{10,9},{13,... | collective-permute-start | bytes 73736 | tf_op jit(solution)/shard_map/ppermute | solution.py:391
  112.7 4.8 %collective-permute-start.3 = (bf16[2,48,128]{2,1,0:T(8,128)(2,1)}, bf16[2,48,128]{2,1,0:T(8,128)(2,1)}, u32[]{:S(2)}, u32[]{:S(2)}) collective-permute-start(bf16[2,48,128]{2,1,0:T(8,128)(2,1)} %get-tuple-element.79), channel_id=1, source_target_pairs={{0,3},{1,2},{2,5},{3,4},{4,7},{5,6},{6,9},{7,8},{8,11},{9,10},{10,... | collective-permute-start | bytes 73736 | tf_op jit(solution)/shard_map/ppermute | solution.py:390
  117.5 1.5 fusion.14
  119.0 1.9 %collective-permute-start.1 = (bf16[96,256]{1,0:T(8,128)(2,1)}, bf16[96,256]{1,0:T(8,128)(2,1)S(1)}, u32[]{:S(2)}, u32[]{:S(2)}) collective-permute-start(bf16[96,256]{1,0:T(8,128)(2,1)} %get-tuple-element.73), channel_id=1, source_target_pairs={{2,0},{4,2},{6,4},{8,6},{10,8},{12,10},{14,12},{3,1},{5,3},{7,5},{... | collective-permute-start | bytes 147464 | tf_op jit(solution)/shard_map/ppermute | solution.py:388
  120.9 4.4 %collective-permute-start = (bf16[96,256]{1,0:T(8,128)(2,1)}, bf16[96,256]{1,0:T(8,128)(2,1)}, u32[]{:S(2)}, u32[]{:S(2)}) collective-permute-start(bf16[96,256]{1,0:T(8,128)(2,1)} %get-tuple-element.74), channel_id=1, source_target_pairs={{0,2},{2,4},{4,6},{6,8},{8,10},{10,12},{12,14},{1,3},{3,5},{5,7},{... | collective-permute-start | bytes 147464 | tf_op jit(solution)/shard_map/ppermute | solution.py:387
  126.0 1.0 copy.61
  127.6 1.3 broadcast_in_dim.32
  131.0 0.9 scatter.21
  131.9 5.0 %scatter.24 = bf16[3,2,64,4,64]{4,3,2,1,0:T(4,128)(2,1)} dynamic-update-slice(bf16[3,2,64,4,64]{4,3,2,1,0:T(4,128)(2,1)} %scatter.21, bf16[3,1,64,3,64]{4,3,2,1,0:T(4,128)(2,1)S(1)} %bitcast.50, s32[]{:T(128)} %constant.187.clone.1, s32[]{:T(128)} %constant.191.clone.1, s32[]{:T(128)} %constant.187.clone.1, s32[]{:T(128)} %constant.191.clone.1, s32[]{:T(128)} %constant.187.clone.1) | dynamic-update-slice | bytes 147460 | tf_op jit(solution)/shard_map/scatter | solution.py:262
  136.9 2.0 %reshape.420.second_ref = bf16[384,256]{1,0:T(8,128)(2,1)} reshape(bf16[3,2,64,4,64]{4,3,2,1,0:T(4,128)(2,1)} %scatter.24) | data formatting | bytes 393216 | tf_op jit(solution)/shard_map/reshape | solution.py:263
  138.9 2.5 %copy.50 = bf16[3,3,64,5,48]{4,3,2,1,0:T(8,128)(2,1)} copy(bf16[3,3,64,5,48]{2,4,3,1,0:T(8,128)(2,1)} %constant_dynamic-update-slice_fusion) | data formatting | bytes 552960 | tf_op jit(solution)/shard_map/reshape | solution.py:263
  141.4 2.5 %reshape.435.first_ref = bf16[576,240]{1,0:T(8,128)(2,1)} reshape(bf16[3,3,64,5,48]{4,3,2,1,0:T(8,128)(2,1)} %copy.50) | data formatting | bytes 552960 | tf_op jit(solution)/shard_map/reshape | solution.py:263
  145.4 45.0 %encoder.1 = bf16[64,192,256]{2,1,0:T(8,128)(2,1)} custom-call(s32[3]{0:T(128)} %pad_add_fusion.place_ref, bf16[9216,256]{1,0:T(8,128)(2,1)} %get-tuple-element.67.comp_ref, bf16[96,256]{1,0:T(8,128)(2,1)} %collective-permute-done.up_ref, bf16[96,256]{1,0:T(8,128)(2,1)} %copy-done.3, bf16[2,2,48,128]{3,2,1,0:T(8,128)(2,1)} %get-tuple-element.68.own_ref, ...), custom_call_target="tpu_custom_call" | custom-call | tf_op jit(solution)/shard_map/encoder/pallas_call | solution.py:303
  (43 shorter events, 10.9 us)
Async XLA Ops:
  0.0 2.6 %copy-start = (bf16[256,48,128]{2,1,0:T(8,128)(2,1)S(1)}, bf16[256,48,128]{2,1,0:T(8,128)(2,1)}, u32[]{:S(2)}) copy-start(bf16[256,48,128]{2,1,0:T(8,128)(2,1)} %param.20) | copy-start | bytes 9437188
  9.1 6.7 %copy-start.1 = (bf16[9,64,48]{1,2,0:T(8,128)(2,1)S(1)}, bf16[9,64,48]{1,2,0:T(8,128)(2,1)}, u32[]{:S(2)}) copy-start(bf16[9,64,48]{1,2,0:T(8,128)(2,1)} %param.26) | copy-start | bytes 165892
  9.1 76.0 %all-to-all-start = ((bf16[16,784,128]{2,1,0:T(8,128)(2,1)}), bf16[16,784,128]{2,1,0:T(8,128)(2,1)}, u32[]{:S(2)}, u32[]{:S(2)}) async-start(bf16[16,784,128]{2,1,0:T(8,128)(2,1)} %pad_maximum_fusion), calls=%async_computation | async-start | bytes 6422528 | tf_op jit(solution)/shard_map/all_to_all | solution.py:369
  20.6 106.4 %copy-start.6 = (f32[64]{0:T(128)S(1)}, f32[64]{0:T(128)}, u32[]{:S(2)}) copy-start(f32[64]{0:T(128)} %param.29) | copy-start | bytes 772
  110.0 33.9 %collective-permute-start.2 = (bf16[2,2,48,128]{3,2,1,0:T(8,128)(2,1)}, bf16[2,2,48,128]{3,2,1,0:T(8,128)(2,1)S(1)}, u32[]{:S(2)}, u32[]{:S(2)}) collective-permute-start(bf16[2,2,48,128]{3,2,1,0:T(8,128)(2,1)} %get-tuple-element.68.own_ref), channel_id=1, source_target_pairs={{0,1},{1,0},{2,3},{3,2},{4,5},{5,4},{6,7},{7,6},{8,9},{9,8},{10,11... | collective-permute-start | bytes 147464 | tf_op jit(solution)/shard_map/ppermute | solution.py:389
  110.8 33.1 %collective-permute-start.4 = (bf16[2,48,128]{2,1,0:T(8,128)(2,1)}, bf16[2,48,128]{2,1,0:T(8,128)(2,1)}, u32[]{:S(2)}, u32[]{:S(2)}) collective-permute-start(bf16[2,48,128]{2,1,0:T(8,128)(2,1)} %get-tuple-element.78), channel_id=1, source_target_pairs={{3,0},{2,1},{5,2},{4,3},{7,4},{6,5},{9,6},{8,7},{11,8},{10,9},{13,... | collective-permute-start | bytes 73736 | tf_op jit(solution)/shard_map/ppermute | solution.py:391
  112.7 31.1 %collective-permute-start.3 = (bf16[2,48,128]{2,1,0:T(8,128)(2,1)}, bf16[2,48,128]{2,1,0:T(8,128)(2,1)}, u32[]{:S(2)}, u32[]{:S(2)}) collective-permute-start(bf16[2,48,128]{2,1,0:T(8,128)(2,1)} %get-tuple-element.79), channel_id=1, source_target_pairs={{0,3},{1,2},{2,5},{3,4},{4,7},{5,6},{6,9},{7,8},{8,11},{9,10},{10,... | collective-permute-start | bytes 73736 | tf_op jit(solution)/shard_map/ppermute | solution.py:390
  119.0 24.9 %collective-permute-start.1 = (bf16[96,256]{1,0:T(8,128)(2,1)}, bf16[96,256]{1,0:T(8,128)(2,1)S(1)}, u32[]{:S(2)}, u32[]{:S(2)}) collective-permute-start(bf16[96,256]{1,0:T(8,128)(2,1)} %get-tuple-element.73), channel_id=1, source_target_pairs={{2,0},{4,2},{6,4},{8,6},{10,8},{12,10},{14,12},{3,1},{5,3},{7,5},{... | collective-permute-start | bytes 147464 | tf_op jit(solution)/shard_map/ppermute | solution.py:388
  120.9 23.0 %collective-permute-start = (bf16[96,256]{1,0:T(8,128)(2,1)}, bf16[96,256]{1,0:T(8,128)(2,1)}, u32[]{:S(2)}, u32[]{:S(2)}) collective-permute-start(bf16[96,256]{1,0:T(8,128)(2,1)} %get-tuple-element.74), channel_id=1, source_target_pairs={{0,2},{2,4},{4,6},{6,8},{8,10},{10,12},{12,14},{1,3},{3,5},{5,7},{... | collective-permute-start | bytes 147464 | tf_op jit(solution)/shard_map/ppermute | solution.py:387
  130.2 14.5 %copy-start.4 = (f32[192]{0:T(256)S(1)}, f32[192]{0:T(256)}, u32[]{:S(2)}) copy-start(f32[192]{0:T(256)} %broadcast_in_dim.29) | copy-start | bytes 2308
  131.0 12.9 %copy-start.5 = (f32[128]{0:T(128)S(1)}, f32[128]{0:T(128)}, u32[]{:S(2)}) copy-start(f32[128]{0:T(128)} %broadcast_in_dim.32) | copy-start | bytes 1540
  143.9 1.5 copy-start.2
  143.9 1.5 copy-start.3

commit v2 on v1

v2 whole, which is shorter than its diff:
```python
import functools

import jax
import jax.numpy as jnp
from jax import lax
from jax.experimental import pallas as pl
from jax.experimental.pallas import tpu as pltpu
from jax.sharding import PartitionSpec as P

TH = 192
TW = 256
CBLK = 384
LANES = 128
HALO = 2
EDGE_TILES = 2
LANE_BASE = 8
ROW_STEPS = 4
CHUNK = 8
LOADS = 4
GROUP_ONE = 3
GROUP_TWO = 2
OUT_ROWS = 32
PREP = 8
VMEM_LIMIT = 56 * 1024 * 1024

F32 = jnp.float32
BF16 = jnp.bfloat16


def lane_index(shape):
    return lax.broadcasted_iota(jnp.int32, shape, len(shape) - 1)


def silu(value):
    half = 0.5 * value
    return half + half * jnp.tanh(half)


def composite_kernel(
    capacity, channels, cell_ref, templ_ref, col_ref, recv_ref, table_ref, weight_ref,
    comp_ref, edge_ref, acc, den, strip, recv, sems,
):
    step = pl.program_id(0)
    peers = recv_ref.shape[0]
    part = peers // LOADS
    col = col_ref[0]

    @pl.when(step == 0)
    def add_up():
        copies = [
            pltpu.make_async_copy(
                recv_ref.at[pl.ds(k * part, part)], recv.at[pl.ds(k * part, part)], sems.at[k]
            )
            for k in range(LOADS)
        ]
        for copy in copies:
            copy.start()

        def clear_block(i, carry):
            acc[i] = jnp.zeros(acc.shape[1:], F32)
            return carry

        lax.fori_loop(0, CBLK, clear_block, 0, unroll=8)
        den[...] = jnp.zeros(den.shape, F32)
        strip[...] = jnp.zeros(strip.shape, BF16)

        def add_slots(source, carry):
            terms = []
            for q in range(capacity):
                block = recv[source, q * channels : (q + 1) * channels, :]
                template = templ_ref[source * capacity + q]
                terms.append(jnp.dot(block, table_ref[template], preferred_element_type=F32))
            for q in range(capacity):
                cell = cell_ref[source * capacity + q]
                acc[cell] += terms[q]
                template = templ_ref[source * capacity + q]
                den[pl.ds(cell, 1), :] += weight_ref[pl.ds(template, 1), :]
            return carry

        for k in range(LOADS):
            copies[k].wait()
            lax.fori_loop(k * part, (k + 1) * part, add_slots, 0)
        den[...] = 1.0 / (1.0 + den[...])

    rows = TH // ROW_STEPS
    lane = lane_index((channels, LANES))
    near = jnp.where(col == 0, LANES - 1, 0)
    far = jnp.where(col == 0, LANES - 2, 1)

    def some_rows(i, carry):
        base = step * rows + i * CHUNK
        picked = [jnp.zeros((channels, LANES), F32), jnp.zeros((channels, LANES), F32)]
        for u in range(CHUNK):
            r = base + u
            out = pl.multiple_of((i * CHUNK + u) * channels, 16)
            parts = []
            for m in range(2):
                value = acc[2 * r + m] * den[pl.ds(2 * r + m, 1), :]
                comp_ref[pl.ds(out, channels), m * LANES : (m + 1) * LANES] = value.astype(BF16)
                parts.append(value)
            side = jnp.where(col == 0, parts[1], parts[0])
            at = (r + LANE_BASE) % LANES
            for p, start in enumerate((near, far)):
                moved = pltpu.roll(side, (at - start + LANES) % LANES, 1)
                picked[p] = jnp.where(lane == at, moved, picked[p])
        tile = (base + LANE_BASE) // LANES
        first = (base + LANE_BASE) % LANES
        inside = (lane >= first) & (lane < first + CHUNK)
        for p in range(2):
            strip[p, tile] = jnp.where(
                inside, picked[p], strip[p, tile].astype(F32)
            ).astype(BF16)
        return carry

    lax.fori_loop(0, rows // CHUNK, some_rows, 0)

    @pl.when(step == ROW_STEPS - 1)
    def finish():
        edge_ref[...] = strip[...]


def shifted(value, left, right):
    lane = lane_index((value.shape[0], LANES))
    first, last = value[:, :LANES], value[:, LANES:]
    first_left, last_left = pltpu.roll(first, 1, 1), pltpu.roll(last, 1, 1)
    first_right, last_right = pltpu.roll(first, LANES - 1, 1), pltpu.roll(last, LANES - 1, 1)
    before = (
        jnp.where(lane == 0, left, first_left),
        jnp.where(lane == 0, first_left, last_left),
    )
    after = (
        jnp.where(lane == LANES - 1, last_right, first_right),
        jnp.where(lane == LANES - 1, right, last_right),
    )
    return before, after


def encoder_kernel(
    channels, hid, place_ref, comp_ref, up_ref, down_ref, own_ref, side_ref, side_up_ref, side_down_ref,
    first_ref, second_ref, edge_first_ref, bias_first_ref, bias_second_ref,
    out_ref, field, hidden, edge_one, edge_two, stage, sems,
):
    col = place_ref[0]
    at_top = place_ref[1]
    at_bottom = place_ref[2]
    target = jnp.where(col == 0, LANES - 1, 0)
    rows_hid = TH + 2
    span = EDGE_TILES * LANES

    def halo_columns(strip, lane_at):
        moved = pltpu.roll(
            strip[lane_at // LANES], (target - lane_at % LANES + LANES) % LANES, 1
        )
        nothing = jnp.zeros_like(moved)
        return jnp.where(col == 0, nothing, moved), jnp.where(col == 0, moved, nothing)

    @pl.when(pl.program_id(0) == 0)
    def first_layer():
        copies = [
            pltpu.make_async_copy(up_ref, field.at[pl.ds(0, HALO), 1], sems.at[0]),
            pltpu.make_async_copy(down_ref, field.at[pl.ds(TH + HALO, HALO), 1], sems.at[1]),
            pltpu.make_async_copy(comp_ref, field.at[pl.ds(HALO, TH), 1], sems.at[2]),
        ]
        for copy in copies:
            copy.start()
        for copy in copies:
            copy.wait()

        wide = lane_index((channels, span))

        def strip_of(ref, p):
            return jnp.concatenate([ref[p, 0], ref[p, 1]], axis=1).astype(F32)

        def put(strip, lane_at, tile, start):
            moved = pltpu.roll(tile, (lane_at % LANES - start + LANES) % LANES, 1)
            return jnp.where(wide == lane_at, jnp.concatenate([moved, moved], axis=1), strip)

        own = strip_of(own_ref, 0)
        sides = [strip_of(side_ref, p) for p in range(2)]
        starts = [jnp.where(col == 0, 0, LANES - 1), jnp.where(col == 0, 1, LANES - 2)]
        for ref, at_row, lane_at in (
            (side_up_ref, 0, LANE_BASE - HALO),
            (side_down_ref, TH + HALO, TH + LANE_BASE),
        ):
            for k in range(HALO):
                tiles = ref[k].astype(F32)
                tile = jnp.where(col == 0, tiles[:, :LANES], tiles[:, LANES:])
                sides = [put(sides[p], lane_at + k, tile, starts[p]) for p in range(2)]
                tiles = field[at_row + k, 1].astype(F32)
                tile = jnp.where(col == 0, tiles[:, LANES:], tiles[:, :LANES])
                own = put(own, lane_at + k, tile, target)

        stack = jnp.concatenate([sides[0], sides[1], own], axis=0).astype(BF16)
        result = jnp.dot(edge_first_ref[...], stack, preferred_element_type=F32)
        total = result[0:hid]
        for a in range(1, 3):
            total = total + pltpu.roll(result[hid * a : hid * (a + 1)], span - a, 1)
        beyond = silu(total + bias_first_ref[0:hid, 0:1])
        lane_hid = lane_index((hid, span))
        first_lane = LANE_BASE - HALO
        drop = ((lane_hid == first_lane) & (at_top == 1)) | (
            (lane_hid == first_lane + rows_hid - 1) & (at_bottom == 1)
        )
        beyond = jnp.where(drop, 0.0, beyond).astype(BF16)
        for tile in range(EDGE_TILES):
            edge_one[tile] = sides[0][:, tile * LANES : (tile + 1) * LANES].astype(BF16)
            edge_two[tile] = beyond[:, tile * LANES : (tile + 1) * LANES]

        def prepare(i, carry):
            for u in range(PREP):
                row = i * PREP + u
                left, right = halo_columns(edge_one, row + LANE_BASE - HALO)
                before, after = shifted(field[row, 1], left, right)
                for half in range(2):
                    place = slice(half * LANES, (half + 1) * LANES)
                    field[row, 0, :, place] = before[half]
                    field[row, 2, :, place] = after[half]
            return carry

        rows_ext = TH + 2 * HALO
        lax.fori_loop(0, -(-rows_ext // PREP), prepare, 0)

        def one_group(first_row):
            window = field[pl.ds(first_row, GROUP_ONE + 2)]
            window = window.reshape((GROUP_ONE + 2) * 3 * channels, TW)
            full = jnp.dot(first_ref[...], window, preferred_element_type=F32)
            for r in range(GROUP_ONE):
                value = full[r * hid : (r + 1) * hid]
                bias = bias_first_ref[0:hid, :]
                value = silu(value + jnp.concatenate([bias, bias], axis=1)).astype(BF16)
                row = first_row + r
                left, right = halo_columns(edge_two, row + LANE_BASE - HALO)
                before, after = shifted(value, left, right)
                hidden[row, 1] = value
                for half in range(2):
                    place = slice(half * LANES, (half + 1) * LANES)
                    hidden[row, 0, :, place] = before[half]
                    hidden[row, 2, :, place] = after[half]

        def some_groups(i, carry):
            for u in range(PREP):
                one_group((i * PREP + u) * GROUP_ONE)
            return carry

        lax.fori_loop(0, rows_hid // (GROUP_ONE * PREP), some_groups, 0)
        done = rows_hid // (GROUP_ONE * PREP) * GROUP_ONE * PREP
        while done < rows_hid:
            one_group(min(done, rows_hid - GROUP_ONE))
            done += GROUP_ONE

        @pl.when(at_top == 1)
        def clear_top():
            hidden[0] = jnp.zeros(hidden.shape[1:], BF16)

        @pl.when(at_bottom == 1)
        def clear_bottom():
            hidden[rows_hid - 1] = jnp.zeros(hidden.shape[1:], BF16)

    base = pl.program_id(0) * OUT_ROWS
    for g in range(OUT_ROWS // GROUP_TWO):
        window = hidden[pl.ds(base + g * GROUP_TWO, GROUP_TWO + 2)]
        window = window.reshape((GROUP_TWO + 2) * 3 * hid, TW)
        full = jnp.dot(second_ref[...], window, preferred_element_type=F32)
        bias = bias_second_ref[...]
        for half in range(2):
            value = full[:, half * LANES : (half + 1) * LANES] + bias
            for r in range(GROUP_TWO):
                stage[half, pl.ds(g * GROUP_TWO + r, hid, stride=OUT_ROWS), :] = value[
                    r * hid : (r + 1) * hid
                ]
    for half in range(2):
        out_ref[:, :, half * LANES : (half + 1) * LANES] = (
            stage[half].reshape(hid, OUT_ROWS, LANES).astype(BF16)
        )


def banded(kernel, count):
    hid, channels = kernel.shape[1:]
    taps = jnp.transpose(kernel.reshape(3, 3, hid, channels), (2, 0, 1, 3))
    taps = taps.reshape(hid, 9 * channels)
    span = 3 * channels
    rows = [jnp.pad(taps, ((0, 0), (r * span, (count - 1 - r) * span))) for r in range(count)]
    return jnp.concatenate(rows, axis=0)


def whole_in_vmem():
    return pl.BlockSpec(memory_space=pltpu.VMEM)


def composite(received, cells, templates, col, table, row_weight, capacity, channels):
    peers = received.shape[0]
    rows = TH // ROW_STEPS * channels
    return pl.pallas_call(
        functools.partial(composite_kernel, capacity, channels),
        grid_spec=pltpu.PrefetchScalarGridSpec(
            num_scalar_prefetch=3,
            grid=(ROW_STEPS,),
            in_specs=[pl.BlockSpec(memory_space=pl.ANY), whole_in_vmem(), whole_in_vmem()],
            out_specs=[pl.BlockSpec((rows, TW), lambda i, *_: (i, 0)), whole_in_vmem()],
            scratch_shapes=[
                pltpu.VMEM((CBLK + 1, channels, LANES), F32),
                pltpu.VMEM((CBLK + 8, LANES), F32),
                pltpu.VMEM((2, EDGE_TILES, channels, LANES), BF16),
                pltpu.VMEM((peers, capacity * channels, LANES), BF16),
                pltpu.SemaphoreType.DMA((LOADS,)),
            ],
        ),
        out_shape=[
            jax.ShapeDtypeStruct((TH * channels, TW), BF16),
            jax.ShapeDtypeStruct((2, EDGE_TILES, channels, LANES), BF16),
        ],
        compiler_params=pltpu.CompilerParams(
            dimension_semantics=("arbitrary",), vmem_limit_bytes=VMEM_LIMIT
        ),
        name="composite",
    )(cells, templates, col, received, table, row_weight)


def encoder(place, field, up, down, own, side, side_up, side_down, weights, channels, hid):
    return pl.pallas_call(
        functools.partial(encoder_kernel, channels, hid),
        grid_spec=pltpu.PrefetchScalarGridSpec(
            num_scalar_prefetch=1,
            grid=(TH // OUT_ROWS,),
            in_specs=[pl.BlockSpec(memory_space=pl.ANY)] * 3 + [whole_in_vmem()] * 9,
            out_specs=pl.BlockSpec((hid, OUT_ROWS, TW), lambda i, *_: (0, i, 0)),
            scratch_shapes=[
                pltpu.VMEM((-(-(TH + 2 * HALO) // PREP) * PREP, 3, channels, TW), BF16),
                pltpu.VMEM((TH + 2, 3, hid, TW), BF16),
                pltpu.VMEM((EDGE_TILES, channels, LANES), BF16),
                pltpu.VMEM((EDGE_TILES, hid, LANES), BF16),
                pltpu.VMEM((2, hid * OUT_ROWS, LANES), F32),
                pltpu.SemaphoreType.DMA((3,)),
            ],
        ),
        out_shape=jax.ShapeDtypeStruct((hid, TH, TW), BF16),
        compiler_params=pltpu.CompilerParams(
            dimension_semantics=("arbitrary",), vmem_limit_bytes=VMEM_LIMIT
        ),
        name="encoder",
    )(place, field, up, down, own, side, side_up, side_down, *weights)


def layer_weights(conv_first, bias_first, conv_second, bias_second, col):
    hid = conv_first.shape[1]
    taps = conv_first.reshape(3, 3, hid, -1)
    inner = jnp.where(col == 0, taps[:, 2], taps[:, 0])
    outer = jnp.where(col == 0, taps[:, 0], taps[:, 2])
    edge_first = jnp.concatenate([taps[:, 1], inner, outer], axis=2).reshape(3 * hid, -1)
    return (
        banded(conv_first, GROUP_ONE),
        banded(conv_second, GROUP_TWO),
        edge_first,
        jnp.broadcast_to(bias_first[:, None], (hid, LANES)),
        jnp.broadcast_to(bias_second[None, :, None], (GROUP_TWO, hid, LANES)).reshape(-1, LANES),
    )


def shards(
    sweeps, route_block, route_cell, route_templ, route_count, footprint,
    conv_first, bias_first, conv_second, bias_second,
):
    peers, capacity = route_block.shape[1:]
    channels = sweeps.shape[1]
    hid = conv_first.shape[1]
    rows = lax.axis_size("ty")
    col = lax.axis_index("tx")
    row = lax.axis_index("ty")
    tiles = ("ty", "tx")

    packets = sweeps[route_block[0]].reshape(peers, capacity * channels, LANES)
    received = lax.all_to_all(packets, tiles, split_axis=0, concat_axis=0, tiled=True)

    live = lax.broadcasted_iota(jnp.int32, (peers, capacity), 1) < route_count[0][:, None]
    cell = jnp.where(live, route_cell[0], CBLK)
    info = jnp.concatenate([cell, route_templ[0]], axis=1)
    info = lax.all_gather(info, tiles, axis=0, tiled=False)
    info = lax.dynamic_index_in_dim(info, lax.axis_index(tiles), 1, keepdims=False)
    cells = info[:, :capacity].reshape(-1)
    templates = info[:, capacity:].reshape(-1)
    table = jnp.transpose(footprint, (0, 2, 1))
    row_weight = jnp.sum(footprint.astype(F32), axis=2)
    place = jnp.stack([col, row == 0, row == rows - 1]).astype(jnp.int32)
    weights = layer_weights(conv_first, bias_first, conv_second, bias_second, col)
    ready = lax.optimization_barrier((received, cells, templates, table, row_weight, place, weights))
    received, cells, templates, table, row_weight, place, weights = ready
    field, own = composite(
        received, cells, templates, place[:1], table, row_weight, capacity, channels
    )

    field = field.reshape(TH, channels, TW)
    onward = [(i, i + 1) for i in range(rows - 1)]
    back = [(i + 1, i) for i in range(rows - 1)]
    swap = [(0, 1), (1, 0)]
    up = lax.ppermute(field[-HALO:], "ty", onward)
    down = lax.ppermute(field[:HALO], "ty", back)
    side = lax.ppermute(own, "tx", swap)
    side_up = lax.ppermute(up, "tx", swap)
    side_down = lax.ppermute(down, "tx", swap)
    return encoder(place, field, up, down, own, side, side_up, side_down, weights, channels, hid)


def solution(mesh):
    split = ("group", "ty", "tx")
    in_specs = (
        P(split, None, None),
        P(split, None, None),
        P(split, None, None),
        P(split, None, None),
        P(split, None),
        P(),
        P(),
        P(),
        P(),
        P(),
    )
    out_specs = P(None, ("group", "ty"), "tx")
    return jax.shard_map(shards, mesh=mesh, in_specs=in_specs, out_specs=out_specs, check_vma=False)
```

time: 193 us -> 166 us (0.86)
  blocking collectives: 0 us -> 79.4 us
  waiting for transfers between devices: 61 us -> 1.43 us
  local copies, waits for them, and re-layouts: 32.1 us -> 12.5 us
  Pallas kernels: 66.5 us -> 48.5 us
  starting transfers between devices: 20.6 us -> 15 us
  other arithmetic: 10 us -> 7.01 us
    all_gather x0 -> x1, blocking collectives: none -> 79.4 us  [shards(): info = lax.all_gather(info, tiles, axis=0, tiled=False)]
    all_to_all x1, waiting for transfers between devices: 60.9 us -> 0.01 us  [shards(): lax.all_to_all(packets, tiles, split_axis=0, concat_axis=0, tiled=True)]
    pallas_call x1, Pallas kernels: 45 us -> 34.8 us  [encoder(): pl.pallas_call(functools.partial(encoder_kernel, channels, hid), grid_spe...]
    scatter x5 -> x0, local copies, waits for them, and re-layouts: 8.12 us -> none  [banded(): full = full.at[:, r, :, r:r + 3, :].set(jnp.transpose(taps, (1, 2, 0, 3)))]
    pallas_call x1, Pallas kernels: 21.4 us -> 13.7 us  [composite(): pl.pallas_call(functools.partial(composite_kernel, capacity, channels), g...]
    ppermute x5, starting transfers between devices: 13.9 us -> 8.23 us  [the longest x1 4.26 us: shards(): down = lax.ppermute(field[:HALO], 'ty', back)]
    reshape x4 -> x5, local copies, waits for them, and re-layouts: 8.01 us -> 2.59 us  [the longest x1 1.05 us: banded(): taps = jnp.transpose(kernel.reshape(3, 3, hid, channels), (2, 0, 1, 3))]
    unnamed x15 -> x25, local copies, waits for them, and re-layouts: 2.34 us -> 3.93 us
  transfers between devices with their start and end apart: 6 -> 6, of which waited for: 1 -> 2; matrix products, arithmetic and copies ran while one was open for 15% -> 7% of each run, Pallas kernels for 0% -> 0%
where the time goes in v2:
time: 166 us; the launch traced here: 164 us
  blocking collectives  79.4 us (48%)
  Pallas kernels  48.5 us (29%)
  starting transfers between devices  15 us (9%)
  local copies, waits for them, and re-layouts  12.5 us (8%)
  other arithmetic  7.01 us (4%)
    all_gather x1, blocking collectives, shards(): info = lax.all_gather(info, tiles, axis=0, tiled=False)  79.4 us
    pallas_call x1, Pallas kernels, encoder(): pl.pallas_call(functools.partial(encoder_kernel, channels, hid), grid_spe...  34.8 us
    pallas_call x1, Pallas kernels, composite(): pl.pallas_call(functools.partial(composite_kernel, capacity, channels), g...  13.7 us
    all_to_all x1, starting transfers between devices, shards(): lax.all_to_all(packets, tiles, split_axis=0, concat_axis=0, tiled=True)  6.76 us
    ppermute x1, starting transfers between devices, shards(): down = lax.ppermute(field[:HALO], 'ty', back)  4.26 us
    unnamed x25, local copies, waits for them, and re-layouts  3.93 us
  transfers between devices with their start and end apart: 6, of which 2 were waited for; matrix products, arithmetic and copies ran while one was open for 7% of the time, Pallas kernels for 0%

profile of v2, /device:TPU:9, one launch (start us, length us, event | category | flops | bytes accessed | tf_op | source)
XLA Modules:
  0.0 164.0 jit_solution(8966426820379927736)
XLA Ops:
  0.0 0.8 compare_select_fusion
  0.9 1.0 copy-done
  1.9 2.6 %gather_fusion = bf16[256,48,128]{2,1,0:T(8,128)(2,1)} fusion(bf16[256,48,128]{2,1,0:T(8,128)(2,1)S(1)} %copy-done, s32[1024]{0:T(1024)S(1)} %pad_clamp_fusion), kind=kCustom, calls=%fused_computation | custom fusion | bytes 6292480 | tf_op jit(solution)/shard_map/gather | solution.py:371
  4.6 6.8 %all-to-all-start = ((bf16[16,768,128]{2,1,0:T(8,128)(2,1)}), bf16[16,768,128]{2,1,0:T(8,128)(2,1)}, u32[]{:S(2)}, u32[]{:S(2)}) async-start(bf16[16,768,128]{2,1,0:T(8,128)(2,1)} %bitcast.31), calls=%async_computation | async-start | bytes 6291456 | tf_op jit(solution)/shard_map/all_to_all | solution.py:372
  11.8 0.7 copy.25
  12.7 79.4 %all-gather = s32[256,32]{1,0:T(8,128)S(1)} all-gather(s32[16,32]{1,0:T(8,128)S(1)} %pad_add_fusion), channel_id=2, replica_groups=mesh['group'=2,'ty'=8,'tx'=2] {'ty','tx'}, dimensions={0}, use_global_device_ids=true | all-gather | bytes 34816 | tf_op jit(solution)/shard_map/all_gather | solution.py:377
  92.2 0.7 reshape.75.templ_ref
  92.8 0.6 reshape.74.cell_ref
  93.5 1.0 copy.21
  94.7 2.3 %copy.17 = bf16[32,128,128]{1,2,0:T(8,128)(2,1)} copy(bf16[32,128,128]{2,1,0:T(8,128)(2,1)} %param.15) | data formatting | bytes 2097152 | tf_op args[5]
  97.0 0.7 pad_add_fusion.1.place_ref
  97.7 1.6 pad_maximum_fusion.edge_first_ref
  99.2 0.8 fusion.8.second_ref
  100.0 0.9 fusion.7.first_ref
  100.8 2.2 %convert_reduce_fusion.weight_ref = f32[32,128]{1,0:T(8,128)} fusion(bf16[32,128,128]{2,1,0:T(8,128)(2,1)} %param.15), kind=kLoop, calls=%fused_computation.1 | loop fusion | flops 1044480 | bytes 1064960 | tf_op jit(solution)/shard_map/reduce_sum | solution.py:382
  103.0 0.7 broadcast_in_dim.22.bias_first_ref
  103.7 0.7 broadcast_in_dim.25.bias_second_ref
  104.4 13.7 %composite.1 = (bf16[9216,256]{1,0:T(8,128)(2,1)}, bf16[2,2,48,128]{3,2,1,0:T(8,128)(2,1)}) custom-call(s32[256]{0:T(256)} %reshape.74.cell_ref, s32[256]{0:T(256)} %reshape.75.templ_ref, s32[1]{0:T(128)} %bitcast.46, bf16[16,768,128]{2,1,0:T(8,128)(2,1)} %all-to-all-done.recv_ref, bf16[32,128,128]{2,1,0:T(8,128)(2,1)} %bitcast.33, ...), custom_call_target="tpu_custom_call" | custom-call | tf_op jit(solution)/shard_map/composite/pallas_call | solution.py:293
  118.1 0.8 fusion.9
  118.9 1.9 %collective-permute-start = (bf16[2,48,256]{2,1,0:T(8,128)(2,1)S(1)}, bf16[2,48,256]{2,1,0:T(8,128)(2,1)S(1)}, u32[]{:S(2)}, u32[]{:S(2)}) collective-permute-start(bf16[2,48,256]{2,1,0:T(8,128)(2,1)S(1)} %bitcast.44), channel_id=1, source_target_pairs={{0,2},{2,4},{4,6},{6,8},{8,10},{10,12},{12,14},{1,3},{3,5},{5,7},{... | collective-permute-start | bytes 147464 | tf_op jit(solution)/shard_map/ppermute | solution.py:395
  120.9 4.3 %collective-permute-start.1 = (bf16[2,48,256]{2,1,0:T(8,128)(2,1)S(1)}, bf16[2,48,256]{2,1,0:T(8,128)(2,1)S(1)}, u32[]{:S(2)}, u32[]{:S(2)}) collective-permute-start(bf16[2,48,256]{2,1,0:T(8,128)(2,1)S(1)} %bitcast.43), channel_id=1, source_target_pairs={{2,0},{4,2},{6,4},{8,6},{10,8},{12,10},{14,12},{3,1},{5,3},{7,5},{... | collective-permute-start | bytes 147464 | tf_op jit(solution)/shard_map/ppermute | solution.py:396
  126.4 1.3 collective-permute-start.4
  127.8 0.9 collective-permute-done.4.side_down_ref
  129.2 34.8 %encoder.1 = bf16[64,192,256]{2,1,0:T(8,128)(2,1)} custom-call(s32[3]{0:T(128)} %pad_add_fusion.1.place_ref, bf16[192,48,256]{2,1,0:T(8,128)(2,1)} %bitcast.32, bf16[2,48,256]{2,1,0:T(8,128)(2,1)} %copy-done.2, bf16[2,48,256]{2,1,0:T(8,128)(2,1)} %copy-done.3, bf16[2,2,48,128]{3,2,1,0:T(8,128)(2,1)} %get-tuple-element.25.own_ref, ...), custom_call_target="tpu_custom_call" | custom-call | tf_op jit(solution)/shard_map/encoder/pallas_call | solution.py:320
  (43 shorter events, 2.8 us)
Async XLA Ops:
  0.0 1.9 %copy-start = (bf16[256,48,128]{2,1,0:T(8,128)(2,1)S(1)}, bf16[256,48,128]{2,1,0:T(8,128)(2,1)}, u32[]{:S(2)}) copy-start(bf16[256,48,128]{2,1,0:T(8,128)(2,1)} %param.10) | copy-start | bytes 9437188
  4.5 6.8 %copy-start.11 = (f32[64]{0:T(128)S(1)}, f32[64]{0:T(128)}, u32[]{:S(2)}) copy-start(f32[64]{0:T(128)} %param.19) | copy-start | bytes 772
  4.5 6.9 %copy-start.1 = (bf16[9,64,48]{1,2,0:T(8,128)(2,1)S(1)}, bf16[9,64,48]{1,2,0:T(8,128)(2,1)}, u32[]{:S(2)}) copy-start(bf16[9,64,48]{1,2,0:T(8,128)(2,1)} %param.16) | copy-start | bytes 165892
  4.5 8.0 %copy-start.8 = (s32[1,16,16]{2,1,0:T(8,128)S(1)}, s32[1,16,16]{2,1,0:T(8,128)}, u32[]{:S(2)}) copy-start(s32[1,16,16]{2,1,0:T(8,128)} %param.12) | copy-start | bytes 3076
  4.6 8.0 %copy-start.10 = (s32[1,16]{1,0:T(1,128)S(1)}, s32[1,16]{1,0:T(1,128)}, u32[]{:S(2)}) copy-start(s32[1,16]{1,0:T(1,128)} %param.14) | copy-start | bytes 196
  4.6 8.0 %copy-start.7 = (s32[1,16,16]{2,1,0:T(8,128)S(1)}, s32[1,16,16]{2,1,0:T(8,128)}, u32[]{:S(2)}) copy-start(s32[1,16,16]{2,1,0:T(8,128)} %param.13) | copy-start | bytes 3076
  4.6 98.4 %all-to-all-start = ((bf16[16,768,128]{2,1,0:T(8,128)(2,1)}), bf16[16,768,128]{2,1,0:T(8,128)(2,1)}, u32[]{:S(2)}, u32[]{:S(2)}) async-start(bf16[16,768,128]{2,1,0:T(8,128)(2,1)} %bitcast.31), calls=%async_computation | async-start | bytes 6291456 | tf_op jit(solution)/shard_map/all_to_all | solution.py:372
  11.3 91.7 %copy-start.9 = (f32[64]{0:T(128)S(1)}, f32[64]{0:T(128)}, u32[]{:S(2)}) copy-start(f32[64]{0:T(128)} %param.17) | copy-start | bytes 772
  118.9 6.7 %collective-permute-start = (bf16[2,48,256]{2,1,0:T(8,128)(2,1)S(1)}, bf16[2,48,256]{2,1,0:T(8,128)(2,1)S(1)}, u32[]{:S(2)}, u32[]{:S(2)}) collective-permute-start(bf16[2,48,256]{2,1,0:T(8,128)(2,1)S(1)} %bitcast.44), channel_id=1, source_target_pairs={{0,2},{2,4},{4,6},{6,8},{8,10},{10,12},{12,14},{1,3},{3,5},{5,7},{... | collective-permute-start | bytes 147464 | tf_op jit(solution)/shard_map/ppermute | solution.py:395
  120.9 5.6 %collective-permute-start.1 = (bf16[2,48,256]{2,1,0:T(8,128)(2,1)S(1)}, bf16[2,48,256]{2,1,0:T(8,128)(2,1)S(1)}, u32[]{:S(2)}, u32[]{:S(2)}) collective-permute-start(bf16[2,48,256]{2,1,0:T(8,128)(2,1)S(1)} %bitcast.43), channel_id=1, source_target_pairs={{2,0},{4,2},{6,4},{8,6},{10,8},{12,10},{14,12},{3,1},{5,3},{7,5},{... | collective-permute-start | bytes 147464 | tf_op jit(solution)/shard_map/ppermute | solution.py:396
  125.1 2.6 %collective-permute-start.2 = (bf16[2,2,48,128]{3,2,1,0:T(8,128)(2,1)}, bf16[2,2,48,128]{3,2,1,0:T(8,128)(2,1)S(1)}, u32[]{:S(2)}, u32[]{:S(2)}) collective-permute-start(bf16[2,2,48,128]{3,2,1,0:T(8,128)(2,1)} %get-tuple-element.25.own_ref), channel_id=1, source_target_pairs={{0,1},{1,0},{2,3},{3,2},{4,5},{5,4},{6,7},{7,6},{8,9},{9,8},{10,11... | collective-permute-start | bytes 147464 | tf_op jit(solution)/shard_map/ppermute | solution.py:397
  125.7 3.0 %copy-start.2 = (bf16[2,48,256]{2,1,0:T(8,128)(2,1)}, bf16[2,48,256]{2,1,0:T(8,128)(2,1)S(1)}, u32[]{:S(2)}) copy-start(bf16[2,48,256]{2,1,0:T(8,128)(2,1)S(1)} %collective-permute-done.up_ref) | copy-start | bytes 147460
  125.7 2.1 %collective-permute-start.3 = (bf16[2,48,256]{2,1,0:T(8,128)(2,1)S(1)}, bf16[2,48,256]{2,1,0:T(8,128)(2,1)S(1)}, u32[]{:S(2)}, u32[]{:S(2)}) collective-permute-start(bf16[2,48,256]{2,1,0:T(8,128)(2,1)S(1)} %collective-permute-done.up_ref), channel_id=1, source_target_pairs={{0,1},{1,0},{2,3},{3,2},{4,5},{5,4},{6,7},{7,6},{8,9},{9,8},{10,11... | collective-permute-start | bytes 147464 | tf_op jit(solution)/shard_map/ppermute | solution.py:398
  126.4 2.2 %copy-start.3 = (bf16[2,48,256]{2,1,0:T(8,128)(2,1)}, bf16[2,48,256]{2,1,0:T(8,128)(2,1)S(1)}, u32[]{:S(2)}) copy-start(bf16[2,48,256]{2,1,0:T(8,128)(2,1)S(1)} %collective-permute-done.1.down_ref) | copy-start | bytes 147460
  126.4 2.2 %collective-permute-start.4 = (bf16[2,48,256]{2,1,0:T(8,128)(2,1)S(1)}, bf16[2,48,256]{2,1,0:T(8,128)(2,1)S(1)}, u32[]{:S(2)}, u32[]{:S(2)}) collective-permute-start(bf16[2,48,256]{2,1,0:T(8,128)(2,1)S(1)} %collective-permute-done.1.down_ref), channel_id=1, source_target_pairs={{0,1},{1,0},{2,3},{3,2},{4,5},{5,4},{6,7},{7,6},{8,9},{9,8},{10,11... | collective-permute-start | bytes 147464 | tf_op jit(solution)/shard_map/ppermute | solution.py:399
  127.8 0.9 copy-start.4
  127.8 0.9 copy-start.5
  128.6 0.6 copy-start.6

commit v3 on v2

--- a/solution.py
+++ b/solution.py
@@ -17,10 +17,12 @@
 ROW_STEPS = 4
 CHUNK = 8
 LOADS = 4
-GROUP_ONE = 3
-GROUP_TWO = 2
-OUT_ROWS = 32
-PREP = 8
+GROUP = 2
+OUT_ROWS = 16
+LAG = 2
+PACK_STEPS = 1
+INFO_ROWS = 16
+CELL_BASE = 32
 VMEM_LIMIT = 56 * 1024 * 1024
 
 F32 = jnp.float32
@@ -36,9 +38,44 @@
     return half + half * jnp.tanh(half)
 
 
+def pack_kernel(
+    channels, block_ref, count_ref, sweeps_ref, cell_ref, templ_ref, out_ref, padded, sem
+):
+    part = out_ref.shape[0]
+    capacity = block_ref.shape[1]
+    held = capacity * channels
+    first = pl.program_id(0) * part
+
+    def send_tile(d, carry):
+        for q in range(capacity):
+            pltpu.make_async_copy(
+                sweeps_ref.at[block_ref[first + d, q]],
+                out_ref.at[d, pl.ds(q * channels, channels), :],
+                sem,
+            ).start()
+        return carry
+
+    lax.fori_loop(0, part, send_tile, 0)
+    padded[...] = jnp.zeros(padded.shape, F32)
+    padded[0, :, 0:capacity] = cell_ref[0].astype(F32)
+    padded[1, :, 0:capacity] = templ_ref[0].astype(F32)
+    lane = lane_index((1, LANES))
+    which = lax.broadcasted_iota(jnp.int32, (INFO_ROWS, LANES), 0)
+    for d in range(part):
+        live = lane < count_ref[0, first + d]
+        cell = jnp.where(live, padded[0, pl.ds(first + d, 1), :], float(CBLK))
+        high = jnp.floor(cell * (1.0 / CELL_BASE))
+        low = cell - high * CELL_BASE
+        template = padded[1, pl.ds(first + d, 1), :]
+        rows = jnp.where(which == 0, high, jnp.where(which == 1, low, template))
+        out_ref[d, held : held + INFO_ROWS, :] = rows.astype(BF16)
+    arrived = out_ref.at[:, pl.ds(0, held), :]
+    pltpu.make_async_copy(arrived, arrived, sem).wait()
+
+
 def composite_kernel(
-    capacity, channels, cell_ref, templ_ref, col_ref, recv_ref, table_ref, weight_ref,
-    comp_ref, edge_ref, acc, den, strip, recv, sems,
+    capacity, channels, col_ref, recv_ref, table_ref, weight_ref,
+    comp_ref, edge_ref, acc, den, strip, recv, raw, numbers, slots, sems,
 ):
     step = pl.program_id(0)
     peers = recv_ref.shape[0]
@@ -47,14 +84,30 @@
 
     @pl.when(step == 0)
     def add_up():
+        held = capacity * channels
+        listing = pltpu.make_async_copy(
+            recv_ref.at[:, pl.ds(held, INFO_ROWS), :], raw, sems.at[LOADS]
+        )
+        listing.start()
         copies = [
             pltpu.make_async_copy(
-                recv_ref.at[pl.ds(k * part, part)], recv.at[pl.ds(k * part, part)], sems.at[k]
+                recv_ref.at[pl.ds(k * part, part), pl.ds(0, held), :],
+                recv.at[pl.ds(k * part, part)],
+                sems.at[k],
             )
             for k in range(LOADS)
         ]
         for copy in copies:
             copy.start()
+        listing.wait()
+        for source in range(peers):
+            rows = raw[source].astype(F32)
+            numbers[source : source + 1, :] = (
+                rows[0:1] * CELL_BASE + rows[1:2]
+            ).astype(jnp.int32)
+            numbers[peers + source : peers + source + 1, :] = rows[2:3].astype(jnp.int32)
+        moved = pltpu.make_async_copy(numbers, slots, sems.at[LOADS + 1])
+        moved.start()
 
         def clear_block(i, carry):
             acc[i] = jnp.zeros(acc.shape[1:], F32)
@@ -63,17 +116,19 @@
         lax.fori_loop(0, CBLK, clear_block, 0, unroll=8)
         den[...] = jnp.zeros(den.shape, F32)
         strip[...] = jnp.zeros(strip.shape, BF16)
+
+        moved.wait()
 
         def add_slots(source, carry):
             terms = []
             for q in range(capacity):
                 block = recv[source, q * channels : (q + 1) * channels, :]
-                template = templ_ref[source * capacity + q]
+                template = slots[peers + source, q]
                 terms.append(jnp.dot(block, table_ref[template], preferred_element_type=F32))
             for q in range(capacity):
-                cell = cell_ref[source * capacity + q]
+                cell = slots[source, q]
                 acc[cell] += terms[q]
-                template = templ_ref[source * capacity + q]
+                template = slots[peers + source, q]
                 den[pl.ds(cell, 1), :] += weight_ref[pl.ds(template, 1), :]
             return carry
 
@@ -146,6 +201,8 @@
     target = jnp.where(col == 0, LANES - 1, 0)
     rows_hid = TH + 2
     span = EDGE_TILES * LANES
+    step = pl.program_id(0)
+    parts = TH // OUT_ROWS
 
     def halo_columns(strip, lane_at):
         moved = pltpu.roll(
@@ -154,17 +211,56 @@
         nothing = jnp.zeros_like(moved)
         return jnp.where(col == 0, nothing, moved), jnp.where(col == 0, moved, nothing)
 
-    @pl.when(pl.program_id(0) == 0)
-    def first_layer():
-        copies = [
-            pltpu.make_async_copy(up_ref, field.at[pl.ds(0, HALO), 1], sems.at[0]),
-            pltpu.make_async_copy(down_ref, field.at[pl.ds(TH + HALO, HALO), 1], sems.at[1]),
-            pltpu.make_async_copy(comp_ref, field.at[pl.ds(HALO, TH), 1], sems.at[2]),
-        ]
-        for copy in copies:
-            copy.start()
-        for copy in copies:
-            copy.wait()
+    def put_row(ref, strip, row, value):
+        left, right = halo_columns(strip, row + LANE_BASE - HALO)
+        before, after = shifted(value, left, right)
+        for half in range(2):
+            place = slice(half * LANES, (half + 1) * LANES)
+            ref[row, 0, :, place] = before[half]
+            ref[row, 2, :, place] = after[half]
+
+    def prepare(row):
+        put_row(field, edge_one, row, field[row, 1])
+
+    def first_group(first_row):
+        window = field[pl.ds(first_row, GROUP + 2)].reshape((GROUP + 2) * 3 * channels, TW)
+        full = jnp.dot(first_ref[...], window, preferred_element_type=F32)
+        bias = jnp.concatenate([bias_first_ref[...]] * 2, axis=1)
+        for r in range(GROUP):
+            value = silu(full[r * hid : (r + 1) * hid] + bias).astype(BF16)
+            hidden[first_row + r, 1] = value
+            put_row(hidden, edge_two, first_row + r, value)
+
+    def second_group(g, first_row):
+        window = hidden[pl.ds(first_row, GROUP + 2)].reshape((GROUP + 2) * 3 * hid, TW)
+        full = jnp.dot(second_ref[...], window, preferred_element_type=F32)
+        bias = bias_second_ref[...]
+        for half in range(2):
+            value = full[:, half * LANES : (half + 1) * LANES] + bias
+            for r in range(GROUP):
+                stage[half, pl.ds(g * GROUP + r, hid, stride=OUT_ROWS), :] = value[
+                    r * hid : (r + 1) * hid
+                ]
+
+    def rows_copy(k):
+        return pltpu.make_async_copy(
+            comp_ref.at[pl.ds(k * OUT_ROWS, OUT_ROWS)],
+            field.at[pl.ds(HALO + k * OUT_ROWS, OUT_ROWS), 1],
+            sems.at[k],
+        )
+
+    @pl.when(step == 0)
+    def start():
+        up = pltpu.make_async_copy(up_ref, field.at[pl.ds(0, HALO), 1], sems.at[parts])
+        down = pltpu.make_async_copy(
+            down_ref, field.at[pl.ds(TH + HALO, HALO), 1], sems.at[parts + 1]
+        )
+        up.start()
+        down.start()
+        for k in range(parts):
+            rows_copy(k).start()
+        up.wait()
+        down.wait()
 
         wide = lane_index((channels, span))
 
@@ -195,7 +291,7 @@
         total = result[0:hid]
         for a in range(1, 3):
             total = total + pltpu.roll(result[hid * a : hid * (a + 1)], span - a, 1)
-        beyond = silu(total + bias_first_ref[0:hid, 0:1])
+        beyond = silu(total + bias_first_ref[:, 0:1])
         lane_hid = lane_index((hid, span))
         first_lane = LANE_BASE - HALO
         drop = ((lane_hid == first_lane) & (at_top == 1)) | (
@@ -206,72 +302,37 @@
             edge_one[tile] = sides[0][:, tile * LANES : (tile + 1) * LANES].astype(BF16)
             edge_two[tile] = beyond[:, tile * LANES : (tile + 1) * LANES]
 
-        def prepare(i, carry):
-            for u in range(PREP):
-                row = i * PREP + u
-                left, right = halo_columns(edge_one, row + LANE_BASE - HALO)
-                before, after = shifted(field[row, 1], left, right)
-                for half in range(2):
-                    place = slice(half * LANES, (half + 1) * LANES)
-                    field[row, 0, :, place] = before[half]
-                    field[row, 2, :, place] = after[half]
-            return carry
-
-        rows_ext = TH + 2 * HALO
-        lax.fori_loop(0, -(-rows_ext // PREP), prepare, 0)
-
-        def one_group(first_row):
-            window = field[pl.ds(first_row, GROUP_ONE + 2)]
-            window = window.reshape((GROUP_ONE + 2) * 3 * channels, TW)
-            full = jnp.dot(first_ref[...], window, preferred_element_type=F32)
-            for r in range(GROUP_ONE):
-                value = full[r * hid : (r + 1) * hid]
-                bias = bias_first_ref[0:hid, :]
-                value = silu(value + jnp.concatenate([bias, bias], axis=1)).astype(BF16)
-                row = first_row + r
-                left, right = halo_columns(edge_two, row + LANE_BASE - HALO)
-                before, after = shifted(value, left, right)
-                hidden[row, 1] = value
-                for half in range(2):
-                    place = slice(half * LANES, (half + 1) * LANES)
-                    hidden[row, 0, :, place] = before[half]
-                    hidden[row, 2, :, place] = after[half]
-
-        def some_groups(i, carry):
-            for u in range(PREP):
-                one_group((i * PREP + u) * GROUP_ONE)
-            return carry
-
-        lax.fori_loop(0, rows_hid // (GROUP_ONE * PREP), some_groups, 0)
-        done = rows_hid // (GROUP_ONE * PREP) * GROUP_ONE * PREP
-        while done < rows_hid:
-            one_group(min(done, rows_hid - GROUP_ONE))
-            done += GROUP_ONE
+        rows_copy(0).wait()
+        for row in range(2 * HALO):
+            prepare(row)
+        first_group(0)
 
         @pl.when(at_top == 1)
         def clear_top():
             hidden[0] = jnp.zeros(hidden.shape[1:], BF16)
 
-        @pl.when(at_bottom == 1)
-        def clear_bottom():
-            hidden[rows_hid - 1] = jnp.zeros(hidden.shape[1:], BF16)
-
-    base = pl.program_id(0) * OUT_ROWS
-    for g in range(OUT_ROWS // GROUP_TWO):
-        window = hidden[pl.ds(base + g * GROUP_TWO, GROUP_TWO + 2)]
-        window = window.reshape((GROUP_TWO + 2) * 3 * hid, TW)
-        full = jnp.dot(second_ref[...], window, preferred_element_type=F32)
-        bias = bias_second_ref[...]
-        for half in range(2):
-            value = full[:, half * LANES : (half + 1) * LANES] + bias
-            for r in range(GROUP_TWO):
-                stage[half, pl.ds(g * GROUP_TWO + r, hid, stride=OUT_ROWS), :] = value[
-                    r * hid : (r + 1) * hid
-                ]
+    @pl.when(step < parts - 1)
+    def arrive():
+        rows_copy(step + 1).wait()
+
+    second_row = (step - LAG) * OUT_ROWS
+    second_row = jnp.maximum(second_row, 0)
+    first_row = jnp.maximum((step - 1) * OUT_ROWS, 0) + GROUP
+    ready_row = step * OUT_ROWS + 2 * GROUP
+    for g in range(OUT_ROWS // GROUP):
+        second_group(g, second_row + g * GROUP)
+    for g in range(OUT_ROWS // GROUP):
+        first_group(first_row + g * GROUP)
+    for r in range(OUT_ROWS):
+        prepare(ready_row + r)
     for half in range(2):
         out_ref[:, :, half * LANES : (half + 1) * LANES] = (
             stage[half].reshape(hid, OUT_ROWS, LANES).astype(BF16)
         )
+
+    @pl.when((step == parts) & (at_bottom == 1))
+    def clear_bottom():
+        hidden[rows_hid - 1] = jnp.zeros(hidden.shape[1:], BF16)
 
 
 def banded(kernel, count):
@@ -287,13 +348,35 @@
     return pl.BlockSpec(memory_space=pltpu.VMEM)
 
 
-def composite(received, cells, templates, col, table, row_weight, capacity, channels):
+def pack(route_block, route_count, sweeps, route_cell, route_templ):
+    peers, capacity = route_block.shape
+    channels = sweeps.shape[1]
+    rows = capacity * channels + INFO_ROWS
+    part = peers // PACK_STEPS
+    return pl.pallas_call(
+        functools.partial(pack_kernel, channels),
+        grid_spec=pltpu.PrefetchScalarGridSpec(
+            num_scalar_prefetch=2,
+            grid=(PACK_STEPS,),
+            in_specs=[pl.BlockSpec(memory_space=pl.ANY), whole_in_vmem(), whole_in_vmem()],
+            out_specs=pl.BlockSpec((part, rows, LANES), lambda i, *_: (i, 0, 0)),
+            scratch_shapes=[pltpu.VMEM((2, peers, LANES), F32), pltpu.SemaphoreType.DMA],
+        ),
+        out_shape=jax.ShapeDtypeStruct((peers, rows, LANES), BF16),
+        compiler_params=pltpu.CompilerParams(
+            dimension_semantics=("arbitrary",), vmem_limit_bytes=VMEM_LIMIT
+        ),
+        name="pack",
+    )(route_block, route_count, sweeps, route_cell, route_templ)
+
+
+def composite(received, col, table, row_weight, capacity, channels):
     peers = received.shape[0]
     rows = TH // ROW_STEPS * channels
     return pl.pallas_call(
         functools.partial(composite_kernel, capacity, channels),
         grid_spec=pltpu.PrefetchScalarGridSpec(
-            num_scalar_prefetch=3,
+            num_scalar_prefetch=1,
             grid=(ROW_STEPS,),
             in_specs=[pl.BlockSpec(memory_space=pl.ANY), whole_in_vmem(), whole_in_vmem()],
             out_specs=[pl.BlockSpec((rows, TW), lambda i, *_: (i, 0)), whole_in_vmem()],
@@ -302,7 +385,10 @@
                 pltpu.VMEM((CBLK + 8, LANES), F32),
                 pltpu.VMEM((2, EDGE_TILES, channels, LANES), BF16),
                 pltpu.VMEM((peers, capacity * channels, LANES), BF16),
-                pltpu.SemaphoreType.DMA((LOADS,)),
+                pltpu.VMEM((peers, INFO_ROWS, LANES), BF16),
+                pltpu.VMEM((2 * peers, LANES), jnp.int32),
+                pltpu.SMEM((2 * peers, LANES), jnp.int32),
+                pltpu.SemaphoreType.DMA((LOADS + 2,)),
             ],
         ),
         out_shape=[
@@ -313,24 +399,28 @@
             dimension_semantics=("arbitrary",), vmem_limit_bytes=VMEM_LIMIT
         ),
         name="composite",
-    )(cells, templates, col, received, table, row_weight)
+    )(col, received, table, row_weight)
 
 
 def encoder(place, field, up, down, own, side, side_up, side_down, weights, channels, hid):
+    parts = TH // OUT_ROWS
+    steps = parts + LAG
     return pl.pallas_call(
         functools.partial(encoder_kernel, channels, hid),
         grid_spec=pltpu.PrefetchScalarGridSpec(
             num_scalar_prefetch=1,
-            grid=(TH // OUT_ROWS,),
+            grid=(steps,),
             in_specs=[pl.BlockSpec(memory_space=pl.ANY)] * 3 + [whole_in_vmem()] * 9,
-            out_specs=pl.BlockSpec((hid, OUT_ROWS, TW), lambda i, *_: (0, i, 0)),
+            out_specs=pl.BlockSpec(
+                (hid, OUT_ROWS, TW), lambda i, *_: (0, jnp.maximum(i - LAG, 0), 0)
+            ),
             scratch_shapes=[
-                pltpu.VMEM((-(-(TH + 2 * HALO) // PREP) * PREP, 3, channels, TW), BF16),
-                pltpu.VMEM((TH + 2, 3, hid, TW), BF16),
+                pltpu.VMEM((steps * OUT_ROWS + 2 * GROUP, 3, channels, TW), BF16),
+                pltpu.VMEM(((steps - 1) * OUT_ROWS + GROUP, 3, hid, TW), BF16),
                 pltpu.VMEM((EDGE_TILES, channels, LANES), BF16),
                 pltpu.VMEM((EDGE_TILES, hid, LANES), BF16),
                 pltpu.VMEM((2, hid * OUT_ROWS, LANES), F32),
-                pltpu.SemaphoreType.DMA((3,)),
+                pltpu.SemaphoreType.DMA((parts + 2,)),
             ],
         ),
         out_shape=jax.ShapeDtypeStruct((hid, TH, TW), BF16),
@@ -348,11 +438,11 @@
     outer = jnp.where(col == 0, taps[:, 0], taps[:, 2])
     edge_first = jnp.concatenate([taps[:, 1], inner, outer], axis=2).reshape(3 * hid, -1)
     return (
-        banded(conv_first, GROUP_ONE),
-        banded(conv_second, GROUP_TWO),
+        banded(conv_first, GROUP),
+        banded(conv_second, GROUP),
         edge_first,
         jnp.broadcast_to(bias_first[:, None], (hid, LANES)),
-        jnp.broadcast_to(bias_second[None, :, None], (GROUP_TWO, hid, LANES)).reshape(-1, LANES),
+        jnp.broadcast_to(bias_second[None, :, None], (GROUP, hid, LANES)).reshape(-1, LANES),
     )
 
 
@@ -368,25 +458,16 @@
     row = lax.axis_index("ty")
     tiles = ("ty", "tx")
 
-    packets = sweeps[route_block[0]].reshape(peers, capacity * channels, LANES)
+    packets = pack(route_block[0], route_count, sweeps, route_cell, route_templ)
     received = lax.all_to_all(packets, tiles, split_axis=0, concat_axis=0, tiled=True)
-
-    live = lax.broadcasted_iota(jnp.int32, (peers, capacity), 1) < route_count[0][:, None]
-    cell = jnp.where(live, route_cell[0], CBLK)
-    info = jnp.concatenate([cell, route_templ[0]], axis=1)
-    info = lax.all_gather(info, tiles, axis=0, tiled=False)
-    info = lax.dynamic_index_in_dim(info, lax.axis_index(tiles), 1, keepdims=False)
-    cells = info[:, :capacity].reshape(-1)
-    templates = info[:, capacity:].reshape(-1)
     table = jnp.transpose(footprint, (0, 2, 1))
     row_weight = jnp.sum(footprint.astype(F32), axis=2)
     place = jnp.stack([col, row == 0, row == rows - 1]).astype(jnp.int32)
     weights = layer_weights(conv_first, bias_first, conv_second, bias_second, col)
-    ready = lax.optimization_barrier((received, cells, templates, table, row_weight, place, weights))
-    received, cells, templates, table, row_weight, place, weights = ready
-    field, own = composite(
-        received, cells, templates, place[:1], table, row_weight, capacity, channels
+    received, table, row_weight, place, weights = lax.optimization_barrier(
+        (received, table, row_weight, place, weights)
     )
+    field, own = composite(received, place[:1], table, row_weight, capacity, channels)
 
     field = field.reshape(TH, channels, TW)
     onward = [(i, i + 1) for i in range(rows - 1)]

time: 166 us -> 142 us (0.86)
  blocking collectives: 79.4 us -> 0 us
  waiting for transfers between devices: 1.43 us -> 60.3 us
  local copies, waits for them, and re-layouts: 12.5 us -> 8.95 us
    all_gather x1 -> x0, blocking collectives: 79.4 us -> none  [shards(): info = lax.all_gather(info, tiles, axis=0, tiled=False)]
    all_to_all x1, waiting for transfers between devices: 0.01 us -> 57.4 us  [shards(): lax.all_to_all(packets, tiles, split_axis=0, concat_axis=0, tiled=True)]
    pallas_call x0 -> x1, Pallas kernels: none -> 5.15 us  [pack(): pl.pallas_call(functools.partial(pack_kernel, channels), grid_spec=pltpu....]
    pallas_call x1, Pallas kernels: 34.8 us -> 30.1 us  [encoder(): pl.pallas_call(functools.partial(encoder_kernel, channels, hid), grid_spe...]
    ppermute x1, starting transfers between devices: 1.91 us -> 5.12 us  [shards(): up = lax.ppermute(field[-HALO:], 'ty', onward)]
    gather x1 -> x0, local copies, waits for them, and re-layouts: 2.64 us -> none  [shards(): packets = sweeps[route_block[0]].reshape(peers, capacity * channels, LANES)]
    ppermute x1, starting transfers between devices: 4.26 us -> 1.92 us  [shards(): down = lax.ppermute(field[:HALO], 'ty', back)]
    unnamed x25 -> x21, local copies, waits for them, and re-layouts: 3.93 us -> 2.95 us
  transfers between devices with their start and end apart: 6 -> 6, of which waited for: 2 -> 3; matrix products, arithmetic and copies ran while one was open for 7% -> 8% of each run, Pallas kernels for 0% -> 0%
where the time goes in v3:
time: 142 us; the launch traced here: 141 us
  waiting for transfers between devices  60.3 us (42%)
  Pallas kernels  48.6 us (34%)
  starting transfers between devices  16.5 us (12%)
  local copies, waits for them, and re-layouts  8.95 us (6%)
  other arithmetic  5.97 us (4%)
    all_to_all x1, waiting for transfers between devices, shards(): lax.all_to_all(packets, tiles, split_axis=0, concat_axis=0, tiled=True)  57.4 us
    pallas_call x1, Pallas kernels, encoder(): pl.pallas_call(functools.partial(encoder_kernel, channels, hid), grid_spe...  30.1 us
    pallas_call x1, Pallas kernels, composite(): pl.pallas_call(functools.partial(composite_kernel, capacity, channels), g...  13.4 us
    all_to_all x1, starting transfers between devices, shards(): lax.all_to_all(packets, tiles, split_axis=0, concat_axis=0, tiled=True)  6.86 us
    pallas_call x1, Pallas kernels, pack(): pl.pallas_call(functools.partial(pack_kernel, channels), grid_spec=pltpu....  5.15 us
    ppermute x1, starting transfers between devices, shards(): up = lax.ppermute(field[-HALO:], 'ty', onward)  5.12 us
    unnamed x21, local copies, waits for them, and re-layouts  2.95 us
  transfers between devices with their start and end apart: 6, of which 3 were waited for; matrix products, arithmetic and copies ran while one was open for 8% of the time, Pallas kernels for 0%

profile of v3, /device:TPU:9, one launch (start us, length us, event | category | flops | bytes accessed | tf_op | source)
XLA Modules:
  0.0 140.5 jit_solution(12916379188486838438)
XLA Ops:
  0.0 5.2 %pack.1 = bf16[16,784,128]{2,1,0:T(8,128)(2,1)} custom-call(s32[16,16]{1,0:T(8,128)} %bitcast.32, s32[1,16]{1,0:T(1,128)} %count_ref.1, bf16[256,48,128]{2,1,0:T(8,128)(2,1)} %sweeps_ref.1, s32[1,16,16]{2,1,0:T(8,128)} %cell_ref.1, s32[1,16,16]{2,1,0:T(8,128)} %templ_ref.1), custom_call_target="tpu_custom_call" | custom-call | tf_op jit(solution)/shard_map/pack/pallas_call | solution.py:356
  5.2 6.9 %all-to-all-start = ((bf16[16,784,128]{2,1,0:T(8,128)(2,1)}), bf16[16,784,128]{2,1,0:T(8,128)(2,1)S(1)}, u32[]{:S(2)}, u32[]{:S(2)}) async-start(bf16[16,784,128]{2,1,0:T(8,128)(2,1)} %pack.1), calls=%async_computation | async-start | bytes 6422528 | tf_op jit(solution)/shard_map/all_to_all | solution.py:462
  12.1 0.7 broadcast_in_dim.18
  13.0 0.7 copy.25
  13.7 0.7 copy.24
  14.4 1.0 copy.20
  15.6 2.3 %copy.17 = bf16[32,128,128]{1,2,0:T(8,128)(2,1)} copy(bf16[32,128,128]{2,1,0:T(8,128)(2,1)} %param.15) | data formatting | bytes 2097152 | tf_op args[5]
  17.9 0.7 pad_add_fusion.place_ref
  18.6 1.6 %pad_maximum_fusion.edge_first_ref = bf16[192,144]{1,0:T(8,128)(2,1)} fusion(bf16[192,48]{1,0:T(8,128)(2,1)} %bitcast.27, bf16[192,48]{1,0:T(8,128)(2,1)} %bitcast.28, bf16[192,48]{1,0:T(8,128)(2,1)S(1)} %bitcast.26), kind=kLoop, calls=%fused_computation.11 | loop fusion | flops 165888 | bytes 110592 | tf_op jit(solution)/shard_map/concatenate | solution.py:439
  20.2 0.7 fusion.5.first_ref
  20.9 0.8 fusion.4.second_ref
  21.7 2.2 %convert_reduce_fusion.weight_ref = f32[32,128]{1,0:T(8,128)} fusion(bf16[32,128,128]{2,1,0:T(8,128)(2,1)} %param.15), kind=kLoop, calls=%fused_computation | loop fusion | flops 1044480 | bytes 1064960 | tf_op jit(solution)/shard_map/reduce_sum | solution.py:464
  23.9 57.4 %all-to-all-done.recv_ref = bf16[16,784,128]{2,1,0:T(8,128)(2,1)S(1)} async-done(((bf16[16,784,128]{2,1,0:T(8,128)(2,1)}), bf16[16,784,128]{2,1,0:T(8,128)(2,1)S(1)}, u32[]{:S(2)}, u32[]{:S(2)}) %all-to-all-start) | async-done | bytes 3211296 | tf_op jit(solution)/shard_map/all_to_all | solution.py:462
  81.3 0.8 broadcast_in_dim.16.bias_first_ref
  82.1 0.9 broadcast_in_dim.19.bias_second_ref
  83.0 13.4 %composite.1 = (bf16[9216,256]{1,0:T(8,128)(2,1)}, bf16[2,2,48,128]{3,2,1,0:T(8,128)(2,1)}) custom-call(s32[1]{0:T(128)} %bitcast.33, bf16[16,784,128]{2,1,0:T(8,128)(2,1)} %copy-done, bf16[32,128,128]{2,1,0:T(8,128)(2,1)} %bitcast.22, f32[32,128]{1,0:T(8,128)} %convert_reduce_fusion.weight_ref), custom_call_target="tpu_custom_call" | custom-call | tf_op jit(solution)/shard_map/composite/pallas_call | solution.py:376
  96.4 0.8 fusion.6
  97.3 5.1 %collective-permute-start = (bf16[2,48,256]{2,1,0:T(8,128)(2,1)S(1)}, bf16[2,48,256]{2,1,0:T(8,128)(2,1)S(1)}, u32[]{:S(2)}, u32[]{:S(2)}) collective-permute-start(bf16[2,48,256]{2,1,0:T(8,128)(2,1)S(1)} %bitcast.31), channel_id=1, source_target_pairs={{0,2},{2,4},{4,6},{6,8},{8,10},{10,12},{12,14},{1,3},{3,5},{5,7},{... | collective-permute-start | bytes 147464 | tf_op jit(solution)/shard_map/ppermute | solution.py:476
  102.4 1.9 %collective-permute-start.1 = (bf16[2,48,256]{2,1,0:T(8,128)(2,1)S(1)}, bf16[2,48,256]{2,1,0:T(8,128)(2,1)S(1)}, u32[]{:S(2)}, u32[]{:S(2)}) collective-permute-start(bf16[2,48,256]{2,1,0:T(8,128)(2,1)S(1)} %bitcast.30), channel_id=1, source_target_pairs={{2,0},{4,2},{6,4},{8,6},{10,8},{12,10},{14,12},{3,1},{5,3},{7,5},{... | collective-permute-start | bytes 147464 | tf_op jit(solution)/shard_map/ppermute | solution.py:477
  104.3 0.8 collective-permute-start.2
  105.2 2.0 %collective-permute-done.1.down_ref = bf16[2,48,256]{2,1,0:T(8,128)(2,1)S(1)} collective-permute-done((bf16[2,48,256]{2,1,0:T(8,128)(2,1)S(1)}, bf16[2,48,256]{2,1,0:T(8,128)(2,1)S(1)}, u32[]{:S(2)}, u32[]{:S(2)}) %collective-permute-start.1) | collective-permute-done | bytes 49184 | tf_op jit(solution)/shard_map/ppermute | solution.py:477
  107.2 1.7 %collective-permute-start.4 = (bf16[2,48,256]{2,1,0:T(8,128)(2,1)S(1)}, bf16[2,48,256]{2,1,0:T(8,128)(2,1)S(1)}, u32[]{:S(2)}, u32[]{:S(2)}) collective-permute-start(bf16[2,48,256]{2,1,0:T(8,128)(2,1)S(1)} %collective-permute-done.1.down_ref), channel_id=1, source_target_pairs={{0,1},{1,0},{2,3},{3,2},{4,5},{5,4},{6,7},{7,6},{8,9},{9,8},{10,11... | collective-permute-start | bytes 147464 | tf_op jit(solution)/shard_map/ppermute | solution.py:480
  109.0 0.9 collective-permute-done.4.side_down_ref
  110.5 30.1 %encoder.1 = bf16[64,192,256]{2,1,0:T(8,128)(2,1)} custom-call(s32[3]{0:T(128)} %pad_add_fusion.place_ref, bf16[192,48,256]{2,1,0:T(8,128)(2,1)} %bitcast.21, bf16[2,48,256]{2,1,0:T(8,128)(2,1)} %copy-done.2, bf16[2,48,256]{2,1,0:T(8,128)(2,1)} %copy-done.3, bf16[2,2,48,128]{3,2,1,0:T(8,128)(2,1)} %get-tuple-element.21.own_ref, ...), custom_call_target="tpu_custom_call" | custom-call | tf_op jit(solution)/shard_map/encoder/pallas_call | solution.py:408
  (29 shorter events, 1.1 us)
Async XLA Ops:
  5.2 6.9 %copy-start.9 = (f32[64]{0:T(128)S(1)}, f32[64]{0:T(128)}, u32[]{:S(2)}) copy-start(f32[64]{0:T(128)} %param.19) | copy-start | bytes 772
  5.2 7.6 %copy-start.1 = (bf16[9,64,48]{1,2,0:T(8,128)(2,1)S(1)}, bf16[9,64,48]{1,2,0:T(8,128)(2,1)}, u32[]{:S(2)}) copy-start(bf16[9,64,48]{1,2,0:T(8,128)(2,1)} %param.16) | copy-start | bytes 165892
  5.2 76.1 %all-to-all-start = ((bf16[16,784,128]{2,1,0:T(8,128)(2,1)}), bf16[16,784,128]{2,1,0:T(8,128)(2,1)S(1)}, u32[]{:S(2)}, u32[]{:S(2)}) async-start(bf16[16,784,128]{2,1,0:T(8,128)(2,1)} %pack.1), calls=%async_computation | async-start | bytes 6422528 | tf_op jit(solution)/shard_map/all_to_all | solution.py:462
  15.6 65.7 %copy-start.7 = (f32[64]{0:T(128)S(1)}, f32[64]{0:T(128)}, u32[]{:S(2)}) copy-start(f32[64]{0:T(128)} %param.17) | copy-start | bytes 772
  15.6 66.5 %copy-start.8 = (f32[128]{0:T(128)S(1)}, f32[128]{0:T(128)}, u32[]{:S(2)}) copy-start(f32[128]{0:T(128)} %broadcast_in_dim.18) | copy-start | bytes 1540
  81.3 1.7 %copy-start = (bf16[16,784,128]{2,1,0:T(8,128)(2,1)}, bf16[16,784,128]{2,1,0:T(8,128)(2,1)S(1)}, u32[]{:S(2)}) copy-start(bf16[16,784,128]{2,1,0:T(8,128)(2,1)S(1)} %all-to-all-done.recv_ref) | copy-start | bytes 9633796
  97.3 7.9 %collective-permute-start = (bf16[2,48,256]{2,1,0:T(8,128)(2,1)S(1)}, bf16[2,48,256]{2,1,0:T(8,128)(2,1)S(1)}, u32[]{:S(2)}, u32[]{:S(2)}) collective-permute-start(bf16[2,48,256]{2,1,0:T(8,128)(2,1)S(1)} %bitcast.31), channel_id=1, source_target_pairs={{0,2},{2,4},{4,6},{6,8},{8,10},{10,12},{12,14},{1,3},{3,5},{5,7},{... | collective-permute-start | bytes 147464 | tf_op jit(solution)/shard_map/ppermute | solution.py:476
  102.4 4.8 %collective-permute-start.1 = (bf16[2,48,256]{2,1,0:T(8,128)(2,1)S(1)}, bf16[2,48,256]{2,1,0:T(8,128)(2,1)S(1)}, u32[]{:S(2)}, u32[]{:S(2)}) collective-permute-start(bf16[2,48,256]{2,1,0:T(8,128)(2,1)S(1)} %bitcast.30), channel_id=1, source_target_pairs={{2,0},{4,2},{6,4},{8,6},{10,8},{12,10},{14,12},{3,1},{5,3},{7,5},{... | collective-permute-start | bytes 147464 | tf_op jit(solution)/shard_map/ppermute | solution.py:477
  104.3 4.6 %collective-permute-start.2 = (bf16[2,2,48,128]{3,2,1,0:T(8,128)(2,1)}, bf16[2,2,48,128]{3,2,1,0:T(8,128)(2,1)S(1)}, u32[]{:S(2)}, u32[]{:S(2)}) collective-permute-start(bf16[2,2,48,128]{3,2,1,0:T(8,128)(2,1)} %get-tuple-element.21.own_ref), channel_id=1, source_target_pairs={{0,1},{1,0},{2,3},{3,2},{4,5},{5,4},{6,7},{7,6},{8,9},{9,8},{10,11... | collective-permute-start | bytes 147464 | tf_op jit(solution)/shard_map/ppermute | solution.py:478
  105.1 4.7 %copy-start.2 = (bf16[2,48,256]{2,1,0:T(8,128)(2,1)}, bf16[2,48,256]{2,1,0:T(8,128)(2,1)S(1)}, u32[]{:S(2)}) copy-start(bf16[2,48,256]{2,1,0:T(8,128)(2,1)S(1)} %collective-permute-done.up_ref) | copy-start | bytes 147460
  105.1 3.8 %collective-permute-start.3 = (bf16[2,48,256]{2,1,0:T(8,128)(2,1)S(1)}, bf16[2,48,256]{2,1,0:T(8,128)(2,1)S(1)}, u32[]{:S(2)}, u32[]{:S(2)}) collective-permute-start(bf16[2,48,256]{2,1,0:T(8,128)(2,1)S(1)} %collective-permute-done.up_ref), channel_id=1, source_target_pairs={{0,1},{1,0},{2,3},{3,2},{4,5},{5,4},{6,7},{7,6},{8,9},{9,8},{10,11... | collective-permute-start | bytes 147464 | tf_op jit(solution)/shard_map/ppermute | solution.py:479
  107.2 2.6 %copy-start.3 = (bf16[2,48,256]{2,1,0:T(8,128)(2,1)}, bf16[2,48,256]{2,1,0:T(8,128)(2,1)S(1)}, u32[]{:S(2)}) copy-start(bf16[2,48,256]{2,1,0:T(8,128)(2,1)S(1)} %collective-permute-done.1.down_ref) | copy-start | bytes 147460
  107.2 2.6 %collective-permute-start.4 = (bf16[2,48,256]{2,1,0:T(8,128)(2,1)S(1)}, bf16[2,48,256]{2,1,0:T(8,128)(2,1)S(1)}, u32[]{:S(2)}, u32[]{:S(2)}) collective-permute-start(bf16[2,48,256]{2,1,0:T(8,128)(2,1)S(1)} %collective-permute-done.1.down_ref), channel_id=1, source_target_pairs={{0,1},{1,0},{2,3},{3,2},{4,5},{5,4},{6,7},{7,6},{8,9},{9,8},{10,11... | collective-permute-start | bytes 147464 | tf_op jit(solution)/shard_map/ppermute | solution.py:480
  109.0 0.9 copy-start.4
  109.0 0.9 copy-start.5
  109.8 0.6 copy-start.6

commit v4 on v3

--- a/solution.py
+++ b/solution.py
@@ -75,12 +75,13 @@
 
 def composite_kernel(
     capacity, channels, col_ref, recv_ref, table_ref, weight_ref,
-    comp_ref, edge_ref, acc, den, strip, recv, raw, numbers, slots, sems,
+    comp_ref, edge_ref, rim_a, rim_b, acc, den, strip, recv, raw, numbers, slots, sems,
 ):
     step = pl.program_id(0)
     peers = recv_ref.shape[0]
     part = peers // LOADS
     col = col_ref[0]
+    odd = col_ref[3]
 
     @pl.when(step == 0)
     def add_up():
@@ -169,7 +170,21 @@
 
     lax.fori_loop(0, rows // CHUNK, some_rows, 0)
 
-    @pl.when(step == ROW_STEPS - 1)
+    rim = HALO * channels
+    top = step == 0
+    bottom = step == ROW_STEPS - 1
+
+    @pl.when((top & (odd == 1)) | (bottom & (odd == 0)))
+    def rim_to_a():
+        begin = pl.multiple_of(jnp.where(top, 0, rows * channels - rim), 16)
+        rim_a[...] = comp_ref[pl.ds(begin, rim), :].reshape(HALO, channels, TW)
+
+    @pl.when((top & (odd == 0)) | (bottom & (odd == 1)))
+    def rim_to_b():
+        begin = pl.multiple_of(jnp.where(top, 0, rows * channels - rim), 16)
+        rim_b[...] = comp_ref[pl.ds(begin, rim), :].reshape(HALO, channels, TW)
+
+    @pl.when(bottom)
     def finish():
         edge_ref[...] = strip[...]
 
@@ -191,13 +206,14 @@
 
 
 def encoder_kernel(
-    channels, hid, place_ref, comp_ref, up_ref, down_ref, own_ref, side_ref, side_up_ref, side_down_ref,
+    channels, hid, place_ref, comp_ref, rim_a_ref, rim_b_ref, own_ref, side_ref, side_a_ref, side_b_ref,
     first_ref, second_ref, edge_first_ref, bias_first_ref, bias_second_ref,
-    out_ref, field, hidden, edge_one, edge_two, stage, sems,
+    out_ref, field, hidden, edge_one, edge_two, biases, stage, sems,
 ):
     col = place_ref[0]
     at_top = place_ref[1]
     at_bottom = place_ref[2]
+    odd = place_ref[3]
     target = jnp.where(col == 0, LANES - 1, 0)
     rows_hid = TH + 2
     span = EDGE_TILES * LANES
@@ -225,7 +241,7 @@
     def first_group(first_row):
         window = field[pl.ds(first_row, GROUP + 2)].reshape((GROUP + 2) * 3 * channels, TW)
         full = jnp.dot(first_ref[...], window, preferred_element_type=F32)
-        bias = jnp.concatenate([bias_first_ref[...]] * 2, axis=1)
+        bias = jnp.concatenate([biases[0]] * 2, axis=1)
         for r in range(GROUP):
             value = silu(full[r * hid : (r + 1) * hid] + bias).astype(BF16)
             hidden[first_row + r, 1] = value
@@ -234,13 +250,11 @@
     def second_group(g, first_row):
         window = hidden[pl.ds(first_row, GROUP + 2)].reshape((GROUP + 2) * 3 * hid, TW)
         full = jnp.dot(second_ref[...], window, preferred_element_type=F32)
-        bias = bias_second_ref[...]
+        bias = jnp.concatenate([biases[1]] * GROUP, axis=0)
         for half in range(2):
             value = full[:, half * LANES : (half + 1) * LANES] + bias
             for r in range(GROUP):
-                stage[half, pl.ds(g * GROUP + r, hid, stride=OUT_ROWS), :] = value[
-                    r * hid : (r + 1) * hid
-                ]
+                stage[half, g * GROUP + r] = value[r * hid : (r + 1) * hid]
 
     def rows_copy(k):
         return pltpu.make_async_copy(
@@ -251,16 +265,25 @@
 
     @pl.when(step == 0)
     def start():
-        up = pltpu.make_async_copy(up_ref, field.at[pl.ds(0, HALO), 1], sems.at[parts])
-        down = pltpu.make_async_copy(
-            down_ref, field.at[pl.ds(TH + HALO, HALO), 1], sems.at[parts + 1]
-        )
-        up.start()
-        down.start()
+        row_a = jnp.where(odd == 1, 0, TH + HALO)
+        row_b = jnp.where(odd == 1, TH + HALO, 0)
+        rims = [
+            pltpu.make_async_copy(
+                ref, field.at[pl.ds(row, HALO), 1], sems.at[parts + k]
+            )
+            for k, (ref, row) in enumerate(((rim_a_ref, row_a), (rim_b_ref, row_b)))
+        ]
+        for rim in rims:
+            rim.start()
         for k in range(parts):
             rows_copy(k).start()
-        up.wait()
-        down.wait()
+        for rim in rims:
+            rim.wait()
+
+        across = lax.broadcasted_iota(jnp.int32, (hid, hid), 0)
+        for k, ref in enumerate((bias_first_ref, bias_second_ref)):
+            square = jnp.where(across == lane_index((hid, hid)), ref[...], 0.0)
+            biases[k] = jnp.broadcast_to(jnp.sum(square, axis=1, keepdims=True), (hid, LANES))
 
         wide = lane_index((channels, span))
 
@@ -274,12 +297,14 @@
         own = strip_of(own_ref, 0)
         sides = [strip_of(side_ref, p) for p in range(2)]
         starts = [jnp.where(col == 0, 0, LANES - 1), jnp.where(col == 0, 1, LANES - 2)]
-        for ref, at_row, lane_at in (
-            (side_up_ref, 0, LANE_BASE - HALO),
-            (side_down_ref, TH + HALO, TH + LANE_BASE),
+        for above, at_row, lane_at in (
+            (1, 0, LANE_BASE - HALO),
+            (0, TH + HALO, TH + LANE_BASE),
         ):
             for k in range(HALO):
-                tiles = ref[k].astype(F32)
+                tiles = jnp.where(
+                    odd == above, side_a_ref[k].astype(F32), side_b_ref[k].astype(F32)
+                )
                 tile = jnp.where(col == 0, tiles[:, :LANES], tiles[:, LANES:])
                 sides = [put(sides[p], lane_at + k, tile, starts[p]) for p in range(2)]
                 tiles = field[at_row + k, 1].astype(F32)
@@ -291,7 +316,7 @@
         total = result[0:hid]
         for a in range(1, 3):
             total = total + pltpu.roll(result[hid * a : hid * (a + 1)], span - a, 1)
-        beyond = silu(total + bias_first_ref[:, 0:1])
+        beyond = silu(total + jnp.concatenate([biases[0]] * EDGE_TILES, axis=1))
         lane_hid = lane_index((hid, span))
         first_lane = LANE_BASE - HALO
         drop = ((lane_hid == first_lane) & (at_top == 1)) | (
@@ -315,20 +340,40 @@
     def arrive():
         rows_copy(step + 1).wait()
 
-    second_row = (step - LAG) * OUT_ROWS
-    second_row = jnp.maximum(second_row, 0)
-    first_row = jnp.maximum((step - 1) * OUT_ROWS, 0) + GROUP
-    ready_row = step * OUT_ROWS + 2 * GROUP
-    for g in range(OUT_ROWS // GROUP):
-        second_group(g, second_row + g * GROUP)
-    for g in range(OUT_ROWS // GROUP):
-        first_group(first_row + g * GROUP)
-    for r in range(OUT_ROWS):
-        prepare(ready_row + r)
-    for half in range(2):
-        out_ref[:, :, half * LANES : (half + 1) * LANES] = (
-            stage[half].reshape(hid, OUT_ROWS, LANES).astype(BF16)
-        )
+    @pl.when((step >= LAG) & (step < parts))
+    def steady():
+        second_row = jnp.maximum((step - LAG) * OUT_ROWS, 0)
+        first_row = jnp.maximum((step - 1) * OUT_ROWS, 0) + GROUP
+        for g in range(OUT_ROWS // GROUP):
+            second_group(g, second_row + g * GROUP)
+        for g in range(OUT_ROWS // GROUP):
+            first_group(first_row + g * GROUP)
+        for r in range(OUT_ROWS):
+            prepare(step * OUT_ROWS + 2 * GROUP + r)
+        for half in range(2):
+            out_ref[:, :, half * LANES : (half + 1) * LANES] = jnp.swapaxes(stage[half], 0, 1).astype(
+                BF16
+            )
+
+
+    @pl.when(step >= parts)
+    def last_ones():
+        for g in range(OUT_ROWS // GROUP):
+            second_group(g, (step - LAG) * OUT_ROWS + g * GROUP)
+        for half in range(2):
+            out_ref[:, :, half * LANES : (half + 1) * LANES] = jnp.swapaxes(
+                stage[half], 0, 1
+            ).astype(BF16)
+
+    @pl.when(((step >= 1) & (step < LAG)) | (step == parts))
+    def first_ones():
+        for g in range(OUT_ROWS // GROUP):
+            first_group((step - 1) * OUT_ROWS + GROUP + g * GROUP)
+
+    @pl.when(step < LAG)
+    def shift_ones():
+        for r in range(OUT_ROWS):
+            prepare(step * OUT_ROWS + 2 * GROUP + r)
 
     @pl.when((step == parts) & (at_bottom == 1))
     def clear_bottom():
@@ -379,7 +424,7 @@
             num_scalar_prefetch=1,
             grid=(ROW_STEPS,),
             in_specs=[pl.BlockSpec(memory_space=pl.ANY), whole_in_vmem(), whole_in_vmem()],
-            out_specs=[pl.BlockSpec((rows, TW), lambda i, *_: (i, 0)), whole_in_vmem()],
+            out_specs=[pl.BlockSpec((rows, TW), lambda i, *_: (i, 0))] + [whole_in_vmem()] * 3,
             scratch_shapes=[
                 pltpu.VMEM((CBLK + 1, channels, LANES), F32),
                 pltpu.VMEM((CBLK + 8, LANES), F32),
@@ -394,6 +439,8 @@
         out_shape=[
             jax.ShapeDtypeStruct((TH * channels, TW), BF16),
             jax.ShapeDtypeStruct((2, EDGE_TILES, channels, LANES), BF16),
+            jax.ShapeDtypeStruct((HALO, channels, TW), BF16),
+            jax.ShapeDtypeStruct((HALO, channels, TW), BF16),
         ],
         compiler_params=pltpu.CompilerParams(
             dimension_semantics=("arbitrary",), vmem_limit_bytes=VMEM_LIMIT
@@ -402,7 +449,7 @@
     )(col, received, table, row_weight)
 
 
-def encoder(place, field, up, down, own, side, side_up, side_down, weights, channels, hid):
+def encoder(place, field, rim_a, rim_b, own, side, side_a, side_b, weights, channels, hid):
     parts = TH // OUT_ROWS
     steps = parts + LAG
     return pl.pallas_call(
@@ -419,7 +466,8 @@
                 pltpu.VMEM(((steps - 1) * OUT_ROWS + GROUP, 3, hid, TW), BF16),
                 pltpu.VMEM((EDGE_TILES, channels, LANES), BF16),
                 pltpu.VMEM((EDGE_TILES, hid, LANES), BF16),
-                pltpu.VMEM((2, hid * OUT_ROWS, LANES), F32),
+                pltpu.VMEM((2, hid, LANES), F32),
+                pltpu.VMEM((2, OUT_ROWS, hid, LANES), F32),
                 pltpu.SemaphoreType.DMA((parts + 2,)),
             ],
         ),
@@ -428,7 +476,7 @@
             dimension_semantics=("arbitrary",), vmem_limit_bytes=VMEM_LIMIT
         ),
         name="encoder",
-    )(place, field, up, down, own, side, side_up, side_down, *weights)
+    )(place, field, rim_a, rim_b, own, side, side_a, side_b, *weights)
 
 
 def layer_weights(conv_first, bias_first, conv_second, bias_second, col):
@@ -441,8 +489,8 @@
         banded(conv_first, GROUP),
         banded(conv_second, GROUP),
         edge_first,
-        jnp.broadcast_to(bias_first[:, None], (hid, LANES)),
-        jnp.broadcast_to(bias_second[None, :, None], (GROUP, hid, LANES)).reshape(-1, LANES),
+        bias_first.reshape(1, hid),
+        bias_second.reshape(1, hid),
     )
 
 
@@ -462,23 +510,23 @@
     received = lax.all_to_all(packets, tiles, split_axis=0, concat_axis=0, tiled=True)
     table = jnp.transpose(footprint, (0, 2, 1))
     row_weight = jnp.sum(footprint.astype(F32), axis=2)
-    place = jnp.stack([col, row == 0, row == rows - 1]).astype(jnp.int32)
+    place = jnp.stack([col, row == 0, row == rows - 1, row % 2]).astype(jnp.int32)
     weights = layer_weights(conv_first, bias_first, conv_second, bias_second, col)
     received, table, row_weight, place, weights = lax.optimization_barrier(
         (received, table, row_weight, place, weights)
     )
-    field, own = composite(received, place[:1], table, row_weight, capacity, channels)
+    field, own, rim_a, rim_b = composite(received, place, table, row_weight, capacity, channels)
 
     field = field.reshape(TH, channels, TW)
-    onward = [(i, i + 1) for i in range(rows - 1)]
-    back = [(i + 1, i) for i in range(rows - 1)]
     swap = [(0, 1), (1, 0)]
-    up = lax.ppermute(field[-HALO:], "ty", onward)
-    down = lax.ppermute(field[:HALO], "ty", back)
+    pairs_a = [p for i in range(0, rows - 1, 2) for p in ((i, i + 1), (i + 1, i))]
+    pairs_b = [p for i in range(1, rows - 1, 2) for p in ((i, i + 1), (i + 1, i))]
     side = lax.ppermute(own, "tx", swap)
-    side_up = lax.ppermute(up, "tx", swap)
-    side_down = lax.ppermute(down, "tx", swap)
-    return encoder(place, field, up, down, own, side, side_up, side_down, weights, channels, hid)
+    rim_a = lax.ppermute(rim_a, "ty", pairs_a)
+    rim_b = lax.ppermute(rim_b, "ty", pairs_b)
+    side_a = lax.ppermute(rim_a, "tx", swap)
+    side_b = lax.ppermute(rim_b, "tx", swap)
+    return encoder(place, field, rim_a, rim_b, own, side, side_a, side_b, weights, channels, hid)
 
 
 def solution(mesh):

time: 142 us -> 134 us (0.944)
  Pallas kernels: 48.6 us -> 43.6 us
  starting transfers between devices: 16.5 us -> 14.5 us
  waiting for transfers between devices: 60.3 us -> 62.1 us
  local copies, waits for them, and re-layouts: 8.95 us -> 7.42 us
    pallas_call x1, Pallas kernels: 30.1 us -> 24.7 us  [encoder(): pl.pallas_call(functools.partial(encoder_kernel, channels, hid), grid_spe...]
    broadcast_in_dim x4 -> x0, local copies, waits for them, and re-layouts: 2.35 us -> none  [the longest x3 1.56 us: layer_weights(): jnp.broadcast_to(bias_second[None, :, None], (GROUP, hid, LANES))]
    ppermute x4, starting transfers between devices: 8.86 us -> 7.18 us  [the longest x1 3.2 us: shards(): rim_a = lax.ppermute(rim_a, 'ty', pairs_a)]
    unnamed x21 -> x15, local copies, waits for them, and re-layouts: 2.95 us -> 4.62 us
where the time goes in v4:
time: 134 us
  waiting for transfers between devices  62.1 us (46%)
  Pallas kernels  43.6 us (33%)
  starting transfers between devices  14.5 us (11%)
  local copies, waits for them, and re-layouts  7.42 us (6%)
  other arithmetic  5.9 us (4%)
    all_to_all x1, waiting for transfers between devices, shards(): lax.all_to_all(packets, tiles, split_axis=0, concat_axis=0, tiled=True)  58.2 us
    pallas_call x1, Pallas kernels, encoder(): pl.pallas_call(functools.partial(encoder_kernel, channels, hid), grid_spe...  24.7 us
    pallas_call x1, Pallas kernels, composite(): pl.pallas_call(functools.partial(composite_kernel, capacity, channels), g...  13.7 us
    all_to_all x1, starting transfers between devices, shards(): lax.all_to_all(packets, tiles, split_axis=0, concat_axis=0, tiled=True)  6.84 us
    pallas_call x1, Pallas kernels, pack(): pl.pallas_call(functools.partial(pack_kernel, channels), grid_spec=pltpu....  5.15 us
    unnamed x15, local copies, waits for them, and re-layouts  4.62 us
    ppermute x1, starting transfers between devices, shards(): rim_a = lax.ppermute(rim_a, 'ty', pairs_a)  3.2 us
    ppermute x1, waiting for transfers between devices, shards(): rim_b = lax.ppermute(rim_b, 'ty', pairs_b)  3.02 us
  transfers between devices with their start and end apart: 6, of which 3 were waited for; matrix products, arithmetic and copies ran while one was open for 8% of the time, Pallas kernels for 0%

profile of v4, /device:TPU:9, one launch (start us, length us, event | category | flops | bytes accessed | tf_op | source)
XLA Modules:
  0.0 133.6 jit_solution(13377457689888822799)
XLA Ops:
  0.0 5.2 %pack.1 = bf16[16,784,128]{2,1,0:T(8,128)(2,1)} custom-call(s32[16,16]{1,0:T(8,128)} %bitcast.30, s32[1,16]{1,0:T(1,128)} %count_ref.1, bf16[256,48,128]{2,1,0:T(8,128)(2,1)} %sweeps_ref.1, s32[1,16,16]{2,1,0:T(8,128)} %cell_ref.1, s32[1,16,16]{2,1,0:T(8,128)} %templ_ref.1), custom_call_target="tpu_custom_call" | custom-call | tf_op jit(solution)/shard_map/pack/pallas_call | solution.py:401
  5.2 6.8 %all-to-all-start = ((bf16[16,784,128]{2,1,0:T(8,128)(2,1)}), bf16[16,784,128]{2,1,0:T(8,128)(2,1)S(1)}, u32[]{:S(2)}, u32[]{:S(2)}) async-start(bf16[16,784,128]{2,1,0:T(8,128)(2,1)} %pack.1), calls=%async_computation | async-start | bytes 6422528 | tf_op jit(solution)/shard_map/all_to_all | solution.py:510
  12.2 0.7 copy.25
  13.0 0.7 copy.24
  13.7 1.0 copy.20
  14.7 0.1 copy.21
  14.9 2.3 %copy.17 = bf16[32,128,128]{1,2,0:T(8,128)(2,1)} copy(bf16[32,128,128]{2,1,0:T(8,128)(2,1)} %param.15) | data formatting | bytes 2097152 | tf_op args[5]
  17.2 0.6 pad_add_fusion.col_ref.place_ref
  17.8 1.6 %pad_maximum_fusion.edge_first_ref = bf16[192,144]{1,0:T(8,128)(2,1)} fusion(bf16[192,48]{1,0:T(8,128)(2,1)} %bitcast.27, bf16[192,48]{1,0:T(8,128)(2,1)} %bitcast.28, bf16[192,48]{1,0:T(8,128)(2,1)S(1)} %bitcast.26), kind=kLoop, calls=%fused_computation.11 | loop fusion | flops 165888 | bytes 110592 | tf_op jit(solution)/shard_map/concatenate | solution.py:487
  19.4 0.7 fusion.5.first_ref
  20.1 0.8 fusion.4.second_ref
  20.9 2.2 %convert_reduce_fusion.weight_ref = f32[32,128]{1,0:T(8,128)} fusion(bf16[32,128,128]{2,1,0:T(8,128)(2,1)} %param.15), kind=kLoop, calls=%fused_computation | loop fusion | flops 1044480 | bytes 1064960 | tf_op jit(solution)/shard_map/reduce_sum | solution.py:512
  23.1 58.2 %all-to-all-done.recv_ref = bf16[16,784,128]{2,1,0:T(8,128)(2,1)S(1)} async-done(((bf16[16,784,128]{2,1,0:T(8,128)(2,1)}), bf16[16,784,128]{2,1,0:T(8,128)(2,1)S(1)}, u32[]{:S(2)}, u32[]{:S(2)}) %all-to-all-start) | async-done | bytes 3211296 | tf_op jit(solution)/shard_map/all_to_all | solution.py:510
  81.3 1.7 %copy-done = bf16[16,784,128]{2,1,0:T(8,128)(2,1)} copy-done((bf16[16,784,128]{2,1,0:T(8,128)(2,1)}, bf16[16,784,128]{2,1,0:T(8,128)(2,1)S(1)}, u32[]{:S(2)}) %copy-start) | copy-done | bytes 3211288
  82.9 13.7 %composite.1 = (bf16[9216,256]{1,0:T(8,128)(2,1)}, bf16[2,2,48,128]{3,2,1,0:T(8,128)(2,1)}, bf16[2,48,256]{2,1,0:T(8,128)(2,1)}, bf16[2,48,256]{2,1,0:T(8,128)(2,1)}) custom-call(s32[4]{0:T(128)} %pad_add_fusion.col_ref.place_ref, bf16[16,784,128]{2,1,0:T(8,128)(2,1)} %copy-done, bf16[32,128,128]{2,1,0:T(8,128)(2,1)} %bitcast.22, ...), custom_call_target="tpu_custom_call" | custom-call | tf_op jit(solution)/shard_map/composite/pallas_call | solution.py:421
  96.6 3.2 %collective-permute-start = (bf16[2,48,256]{2,1,0:T(8,128)(2,1)}, bf16[2,48,256]{2,1,0:T(8,128)(2,1)S(1)}, u32[]{:S(2)}, u32[]{:S(2)}) collective-permute-start(bf16[2,48,256]{2,1,0:T(8,128)(2,1)} %get-tuple-element.23), channel_id=1, source_target_pairs={{0,2},{2,0},{4,6},{6,4},{8,10},{10,8},{12,14},{14,12},{1,3},{3,1},... | collective-permute-start | bytes 147464 | tf_op jit(solution)/shard_map/ppermute | solution.py:525
  99.8 1.9 %collective-permute-start.1 = (bf16[2,48,256]{2,1,0:T(8,128)(2,1)}, bf16[2,48,256]{2,1,0:T(8,128)(2,1)S(1)}, u32[]{:S(2)}, u32[]{:S(2)}) collective-permute-start(bf16[2,48,256]{2,1,0:T(8,128)(2,1)} %get-tuple-element.24), channel_id=1, source_target_pairs={{2,4},{4,2},{6,8},{8,6},{10,12},{12,10},{3,5},{5,3},{7,9},{9,7},{1... | collective-permute-start | bytes 147464 | tf_op jit(solution)/shard_map/ppermute | solution.py:526
  101.7 0.5 collective-permute-start.2
  102.2 0.5 collective-permute-start.3
  102.7 3.0 %collective-permute-done.1.rim_b_ref = bf16[2,48,256]{2,1,0:T(8,128)(2,1)S(1)} collective-permute-done((bf16[2,48,256]{2,1,0:T(8,128)(2,1)}, bf16[2,48,256]{2,1,0:T(8,128)(2,1)S(1)}, u32[]{:S(2)}, u32[]{:S(2)}) %collective-permute-start.1) | collective-permute-done | bytes 49184 | tf_op jit(solution)/shard_map/ppermute | solution.py:526
  105.7 1.6 %collective-permute-start.4 = (bf16[2,48,256]{2,1,0:T(8,128)(2,1)S(1)}, bf16[2,48,256]{2,1,0:T(8,128)(2,1)S(1)}, u32[]{:S(2)}, u32[]{:S(2)}) collective-permute-start(bf16[2,48,256]{2,1,0:T(8,128)(2,1)S(1)} %collective-permute-done.1.rim_b_ref), channel_id=1, source_target_pairs={{0,1},{1,0},{2,3},{3,2},{4,5},{5,4},{6,7},{7,6},{8,9},{9,8},{10,11... | collective-permute-start | bytes 147464 | tf_op jit(solution)/shard_map/ppermute | solution.py:528
  107.3 0.9 collective-permute-done.4.side_b_ref
  108.2 0.6 copy-done.6
  108.8 24.7 %encoder.1 = bf16[64,192,256]{2,1,0:T(8,128)(2,1)} custom-call(s32[4]{0:T(128)} %pad_add_fusion.col_ref.place_ref, bf16[192,48,256]{2,1,0:T(8,128)(2,1)} %bitcast.21, bf16[2,48,256]{2,1,0:T(8,128)(2,1)} %copy-done.2, bf16[2,48,256]{2,1,0:T(8,128)(2,1)} %copy-done.3, bf16[2,2,48,128]{3,2,1,0:T(8,128)(2,1)} %get-tuple-element.25.own_ref, ...), custom_call_target="tpu_custom_call" | custom-call | tf_op jit(solution)/shard_map/encoder/pallas_call | solution.py:455
  (18 shorter events, 0.2 us)
Async XLA Ops:
  5.2 6.9 %copy-start.1 = (bf16[9,64,48]{1,2,0:T(8,128)(2,1)S(1)}, bf16[9,64,48]{1,2,0:T(8,128)(2,1)}, u32[]{:S(2)}) copy-start(bf16[9,64,48]{1,2,0:T(8,128)(2,1)} %param.16) | copy-start | bytes 165892
  5.2 76.1 %all-to-all-start = ((bf16[16,784,128]{2,1,0:T(8,128)(2,1)}), bf16[16,784,128]{2,1,0:T(8,128)(2,1)S(1)}, u32[]{:S(2)}, u32[]{:S(2)}) async-start(bf16[16,784,128]{2,1,0:T(8,128)(2,1)} %pack.1), calls=%async_computation | async-start | bytes 6422528 | tf_op jit(solution)/shard_map/all_to_all | solution.py:510
  81.3 1.7 %copy-start = (bf16[16,784,128]{2,1,0:T(8,128)(2,1)}, bf16[16,784,128]{2,1,0:T(8,128)(2,1)S(1)}, u32[]{:S(2)}) copy-start(bf16[16,784,128]{2,1,0:T(8,128)(2,1)S(1)} %all-to-all-done.recv_ref) | copy-start | bytes 9633796
  96.6 5.6 %collective-permute-start = (bf16[2,48,256]{2,1,0:T(8,128)(2,1)}, bf16[2,48,256]{2,1,0:T(8,128)(2,1)S(1)}, u32[]{:S(2)}, u32[]{:S(2)}) collective-permute-start(bf16[2,48,256]{2,1,0:T(8,128)(2,1)} %get-tuple-element.23), channel_id=1, source_target_pairs={{0,2},{2,0},{4,6},{6,4},{8,10},{10,8},{12,14},{14,12},{1,3},{3,1},... | collective-permute-start | bytes 147464 | tf_op jit(solution)/shard_map/ppermute | solution.py:525
  99.8 5.9 %collective-permute-start.1 = (bf16[2,48,256]{2,1,0:T(8,128)(2,1)}, bf16[2,48,256]{2,1,0:T(8,128)(2,1)S(1)}, u32[]{:S(2)}, u32[]{:S(2)}) collective-permute-start(bf16[2,48,256]{2,1,0:T(8,128)(2,1)} %get-tuple-element.24), channel_id=1, source_target_pairs={{2,4},{4,2},{6,8},{8,6},{10,12},{12,10},{3,5},{5,3},{7,9},{9,7},{1... | collective-permute-start | bytes 147464 | tf_op jit(solution)/shard_map/ppermute | solution.py:526
  101.7 5.6 %collective-permute-start.2 = (bf16[2,2,48,128]{3,2,1,0:T(8,128)(2,1)}, bf16[2,2,48,128]{3,2,1,0:T(8,128)(2,1)S(1)}, u32[]{:S(2)}, u32[]{:S(2)}) collective-permute-start(bf16[2,2,48,128]{3,2,1,0:T(8,128)(2,1)} %get-tuple-element.25.own_ref), channel_id=1, source_target_pairs={{0,1},{1,0},{2,3},{3,2},{4,5},{5,4},{6,7},{7,6},{8,9},{9,8},{10,11... | collective-permute-start | bytes 147464 | tf_op jit(solution)/shard_map/ppermute | solution.py:524
  102.2 6.0 %copy-start.2 = (bf16[2,48,256]{2,1,0:T(8,128)(2,1)}, bf16[2,48,256]{2,1,0:T(8,128)(2,1)S(1)}, u32[]{:S(2)}) copy-start(bf16[2,48,256]{2,1,0:T(8,128)(2,1)S(1)} %collective-permute-done.rim_a_ref) | copy-start | bytes 147460
  102.2 5.1 %collective-permute-start.3 = (bf16[2,48,256]{2,1,0:T(8,128)(2,1)S(1)}, bf16[2,48,256]{2,1,0:T(8,128)(2,1)S(1)}, u32[]{:S(2)}, u32[]{:S(2)}) collective-permute-start(bf16[2,48,256]{2,1,0:T(8,128)(2,1)S(1)} %collective-permute-done.rim_a_ref), channel_id=1, source_target_pairs={{0,1},{1,0},{2,3},{3,2},{4,5},{5,4},{6,7},{7,6},{8,9},{9,8},{10,11... | collective-permute-start | bytes 147464 | tf_op jit(solution)/shard_map/ppermute | solution.py:527
  105.7 2.5 %copy-start.3 = (bf16[2,48,256]{2,1,0:T(8,128)(2,1)}, bf16[2,48,256]{2,1,0:T(8,128)(2,1)S(1)}, u32[]{:S(2)}) copy-start(bf16[2,48,256]{2,1,0:T(8,128)(2,1)S(1)} %collective-permute-done.1.rim_b_ref) | copy-start | bytes 147460
  105.7 2.5 %collective-permute-start.4 = (bf16[2,48,256]{2,1,0:T(8,128)(2,1)S(1)}, bf16[2,48,256]{2,1,0:T(8,128)(2,1)S(1)}, u32[]{:S(2)}, u32[]{:S(2)}) collective-permute-start(bf16[2,48,256]{2,1,0:T(8,128)(2,1)S(1)} %collective-permute-done.1.rim_b_ref), channel_id=1, source_target_pairs={{0,1},{1,0},{2,3},{3,2},{4,5},{5,4},{6,7},{7,6},{8,9},{9,8},{10,11... | collective-permute-start | bytes 147464 | tf_op jit(solution)/shard_map/ppermute | solution.py:528
  107.3 0.9 copy-start.4
  107.3 0.9 copy-start.5
  108.2 0.6 copy-start.6

commit v5 on v4

--- a/solution.py
+++ b/solution.py
@@ -23,7 +23,10 @@
 PACK_STEPS = 1
 INFO_ROWS = 16
 CELL_BASE = 32
-VMEM_LIMIT = 56 * 1024 * 1024
+MIB = 1024 * 1024
+PACK_VMEM = 12 * MIB
+COMPOSITE_VMEM = 26 * MIB
+ENCODER_VMEM = 45 * MIB
 
 F32 = jnp.float32
 BF16 = jnp.bfloat16
@@ -409,7 +412,7 @@
         ),
         out_shape=jax.ShapeDtypeStruct((peers, rows, LANES), BF16),
         compiler_params=pltpu.CompilerParams(
-            dimension_semantics=("arbitrary",), vmem_limit_bytes=VMEM_LIMIT
+            dimension_semantics=("arbitrary",), vmem_limit_bytes=PACK_VMEM
         ),
         name="pack",
     )(route_block, route_count, sweeps, route_cell, route_templ)
@@ -443,7 +446,7 @@
             jax.ShapeDtypeStruct((HALO, channels, TW), BF16),
         ],
         compiler_params=pltpu.CompilerParams(
-            dimension_semantics=("arbitrary",), vmem_limit_bytes=VMEM_LIMIT
+            dimension_semantics=("arbitrary",), vmem_limit_bytes=COMPOSITE_VMEM
         ),
         name="composite",
     )(col, received, table, row_weight)
@@ -473,7 +476,7 @@
         ),
         out_shape=jax.ShapeDtypeStruct((hid, TH, TW), BF16),
         compiler_params=pltpu.CompilerParams(
-            dimension_semantics=("arbitrary",), vmem_limit_bytes=VMEM_LIMIT
+            dimension_semantics=("arbitrary",), vmem_limit_bytes=ENCODER_VMEM
         ),
         name="encoder",
     )(place, field, rim_a, rim_b, own, side, side_a, side_b, *weights)

time: 134 us -> 136 us (1.015)
  local copies, waits for them, and re-layouts: 7.42 us -> 11.7 us
  Pallas kernels: 43.6 us -> 41.3 us
    unnamed x15 -> x21, local copies, waits for them, and re-layouts: 4.62 us -> 8.14 us
    pallas_call x1, Pallas kernels: 13.7 us -> 10.4 us  [composite(): pl.pallas_call(functools.partial(composite_kernel, capacity, channels), g...]
    pallas_call x1, Pallas kernels: 5.15 us -> 7.73 us  [pack(): pl.pallas_call(functools.partial(pack_kernel, channels), grid_spec=pltpu....]
    pallas_call x1, Pallas kernels: 24.7 us -> 23.2 us  [encoder(): pl.pallas_call(functools.partial(encoder_kernel, channels, hid), grid_spe...]
where the time goes in v5:
time: 136 us; the launch traced here: 135 us
  waiting for transfers between devices  62.2 us (46%)
  Pallas kernels  41.3 us (30%)
  starting transfers between devices  14.6 us (11%)
  local copies, waits for them, and re-layouts  11.7 us (9%)
  other arithmetic  5.01 us (4%)
    all_to_all x1, waiting for transfers between devices, shards(): lax.all_to_all(packets, tiles, split_axis=0, concat_axis=0, tiled=True)  58.3 us
    pallas_call x1, Pallas kernels, encoder(): pl.pallas_call(functools.partial(encoder_kernel, channels, hid), grid_spe...  23.2 us
    pallas_call x1, Pallas kernels, composite(): pl.pallas_call(functools.partial(composite_kernel, capacity, channels), g...  10.4 us
    unnamed x21, local copies, waits for them, and re-layouts  8.14 us
    pallas_call x1, Pallas kernels, pack(): pl.pallas_call(functools.partial(pack_kernel, channels), grid_spec=pltpu....  7.73 us
    all_to_all x1, starting transfers between devices, shards(): lax.all_to_all(packets, tiles, split_axis=0, concat_axis=0, tiled=True)  6.75 us
    ppermute x1, starting transfers between devices, shards(): rim_a = lax.ppermute(rim_a, 'ty', pairs_a)  3.29 us
    ppermute x1, waiting for transfers between devices, shards(): rim_b = lax.ppermute(rim_b, 'ty', pairs_b)  2.96 us
  transfers between devices with their start and end apart: 6, of which 3 were waited for; matrix products, arithmetic and copies ran while one was open for 8% of the time, Pallas kernels for 0%

profile of v5, /device:TPU:9, one launch (start us, length us, event | category | flops | bytes accessed | tf_op | source)
XLA Modules:
  0.0 135.0 jit_solution(5498801608414355406)
XLA Ops:
  0.0 1.9 %copy-done.1 = bf16[256,48,128]{2,1,0:T(8,128)(2,1)S(1)} copy-done((bf16[256,48,128]{2,1,0:T(8,128)(2,1)S(1)}, bf16[256,48,128]{2,1,0:T(8,128)(2,1)}, u32[]{:S(2)}) %copy-start.1) | copy-done | bytes 3145752
  1.9 0.7 copy-done.3
  2.6 0.7 copy-done.4
  4.6 7.7 %pack.1 = bf16[16,784,128]{2,1,0:T(8,128)(2,1)} custom-call(s32[16,16]{1,0:T(8,128)S(1)} %bitcast.23, s32[1,16]{1,0:T(1,128)S(1)} %copy-done.6, bf16[256,48,128]{2,1,0:T(8,128)(2,1)S(1)} %copy-done.1, s32[1,16,16]{2,1,0:T(8,128)S(1)} %copy-done.4, s32[1,16,16]{2,1,0:T(8,128)S(1)} %copy-done.5), custom_call_target="tpu_custom_call" | custom-call | tf_op jit(solution)/shard_map/pack/pallas_call | solution.py:404
  12.4 6.8 %all-to-all-start = ((bf16[16,784,128]{2,1,0:T(8,128)(2,1)}), bf16[16,784,128]{2,1,0:T(8,128)(2,1)S(1)}, u32[]{:S(2)}, u32[]{:S(2)}) async-start(bf16[16,784,128]{2,1,0:T(8,128)(2,1)} %pack.1), calls=%async_computation | async-start | bytes 6422528 | tf_op jit(solution)/shard_map/all_to_all | solution.py:513
  20.0 0.9 copy.25
  20.8 0.7 copy.24
  21.5 1.0 copy.20
  22.6 0.8 copy.21
  23.4 2.3 %copy.17 = bf16[32,128,128]{1,2,0:T(8,128)(2,1)} copy(bf16[32,128,128]{2,1,0:T(8,128)(2,1)} %param.15) | data formatting | bytes 2097152 | tf_op args[5]
  25.7 0.9 pad_maximum_fusion.edge_first_ref
  26.6 0.8 fusion.5.first_ref
  27.4 1.1 fusion.4.second_ref
  28.5 1.6 %convert_reduce_fusion.weight_ref = f32[32,128]{1,0:T(8,128)S(1)} fusion(bf16[32,128,128]{2,1,0:T(8,128)(2,1)} %param.15), kind=kLoop, calls=%fused_computation | loop fusion | flops 1044480 | bytes 1064960 | tf_op jit(solution)/shard_map/reduce_sum | solution.py:515
  30.0 58.3 %all-to-all-done.recv_ref = bf16[16,784,128]{2,1,0:T(8,128)(2,1)S(1)} async-done(((bf16[16,784,128]{2,1,0:T(8,128)(2,1)}), bf16[16,784,128]{2,1,0:T(8,128)(2,1)S(1)}, u32[]{:S(2)}, u32[]{:S(2)}) %all-to-all-start) | async-done | bytes 3211296 | tf_op jit(solution)/shard_map/all_to_all | solution.py:513
  88.4 1.2 copy-done
  89.6 10.4 %composite.1 = (bf16[9216,256]{1,0:T(8,128)(2,1)S(1)}, bf16[2,2,48,128]{3,2,1,0:T(8,128)(2,1)S(1)}, bf16[2,48,256]{2,1,0:T(8,128)(2,1)S(1)}, bf16[2,48,256]{2,1,0:T(8,128)(2,1)S(1)}) custom-call(s32[4]{0:T(128)S(1)} %pad_add_fusion.col_ref.place_ref, bf16[16,784,128]{2,1,0:T(8,128)(2,1)S(1)} %all-to-all-done.recv_ref, bf16[32,128,128]{2,1,0:T(8,128)(2,1)S(1)} %bitcast.22, ...), custom_call_target="tpu_custom_call" | custom-call | tf_op jit(solution)/shard_map/composite/pallas_call | solution.py:424
  100.0 3.3 %collective-permute-start = (bf16[2,48,256]{2,1,0:T(8,128)(2,1)S(1)}, bf16[2,48,256]{2,1,0:T(8,128)(2,1)S(1)}, u32[]{:S(2)}, u32[]{:S(2)}) collective-permute-start(bf16[2,48,256]{2,1,0:T(8,128)(2,1)S(1)} %get-tuple-element.23), channel_id=1, source_target_pairs={{0,2},{2,0},{4,6},{6,4},{8,10},{10,8},{12,14},{14,12},{1,3},{3,1},... | collective-permute-start | bytes 147464 | tf_op jit(solution)/shard_map/ppermute | solution.py:528
  103.3 1.9 %collective-permute-start.1 = (bf16[2,48,256]{2,1,0:T(8,128)(2,1)S(1)}, bf16[2,48,256]{2,1,0:T(8,128)(2,1)S(1)}, u32[]{:S(2)}, u32[]{:S(2)}) collective-permute-start(bf16[2,48,256]{2,1,0:T(8,128)(2,1)S(1)} %get-tuple-element.24), channel_id=1, source_target_pairs={{2,4},{4,2},{6,8},{8,6},{10,12},{12,10},{3,5},{5,3},{7,9},{9,7},{1... | collective-permute-start | bytes 147464 | tf_op jit(solution)/shard_map/ppermute | solution.py:529
  105.2 0.8 collective-permute-start.2
  106.1 3.0 %collective-permute-done.1.rim_b_ref = bf16[2,48,256]{2,1,0:T(8,128)(2,1)S(1)} collective-permute-done((bf16[2,48,256]{2,1,0:T(8,128)(2,1)S(1)}, bf16[2,48,256]{2,1,0:T(8,128)(2,1)S(1)}, u32[]{:S(2)}, u32[]{:S(2)}) %collective-permute-start.1) | collective-permute-done | bytes 49184 | tf_op jit(solution)/shard_map/ppermute | solution.py:529
  109.0 1.8 %collective-permute-start.4 = (bf16[2,48,256]{2,1,0:T(8,128)(2,1)S(1)}, bf16[2,48,256]{2,1,0:T(8,128)(2,1)S(1)}, u32[]{:S(2)}, u32[]{:S(2)}) collective-permute-start(bf16[2,48,256]{2,1,0:T(8,128)(2,1)S(1)} %collective-permute-done.1.rim_b_ref), channel_id=1, source_target_pairs={{0,1},{1,0},{2,3},{3,2},{4,5},{5,4},{6,7},{7,6},{8,9},{9,8},{10,11... | collective-permute-start | bytes 147464 | tf_op jit(solution)/shard_map/ppermute | solution.py:531
  110.9 0.9 collective-permute-done.4.side_b_ref
  111.8 23.2 %encoder.1 = bf16[64,192,256]{2,1,0:T(8,128)(2,1)} custom-call(s32[4]{0:T(128)S(1)} %pad_add_fusion.col_ref.place_ref, bf16[192,48,256]{2,1,0:T(8,128)(2,1)S(1)} %bitcast.21, bf16[2,48,256]{2,1,0:T(8,128)(2,1)S(1)} %collective-permute-done.rim_a_ref, bf16[2,48,256]{2,1,0:T(8,128)(2,1)S(1)} %collective-permute-done.1.rim_b_ref, ...), custom_call_target="tpu_custom_call" | custom-call | tf_op jit(solution)/shard_map/encoder/pallas_call | solution.py:458
  (24 shorter events, 2.4 us)
Async XLA Ops:
  0.0 1.9 %copy-start.1 = (bf16[256,48,128]{2,1,0:T(8,128)(2,1)S(1)}, bf16[256,48,128]{2,1,0:T(8,128)(2,1)}, u32[]{:S(2)}) copy-start(bf16[256,48,128]{2,1,0:T(8,128)(2,1)} %sweeps_ref.1) | copy-start | bytes 9437188
  1.9 0.7 copy-start.3
  2.6 0.7 copy-start.4
  3.3 0.7 copy-start.5
  4.0 0.7 copy-start.6
  12.4 6.8 %copy-start.9 = (bf16[9,64,48]{1,2,0:T(8,128)(2,1)S(1)}, bf16[9,64,48]{1,2,0:T(8,128)(2,1)}, u32[]{:S(2)}) copy-start(bf16[9,64,48]{1,2,0:T(8,128)(2,1)} %param.16) | copy-start | bytes 165892
  12.4 76.0 %all-to-all-start = ((bf16[16,784,128]{2,1,0:T(8,128)(2,1)}), bf16[16,784,128]{2,1,0:T(8,128)(2,1)S(1)}, u32[]{:S(2)}, u32[]{:S(2)}) async-start(bf16[16,784,128]{2,1,0:T(8,128)(2,1)} %pack.1), calls=%async_computation | async-start | bytes 6422528 | tf_op jit(solution)/shard_map/all_to_all | solution.py:513
  25.6 86.1 %copy-start.7 = (f32[64]{0:T(128)S(1)}, f32[64]{0:T(128)}, u32[]{:S(2)}) copy-start(f32[64]{0:T(128)} %param.17) | copy-start | bytes 772
  25.6 86.1 %copy-start.8 = (f32[64]{0:T(128)S(1)}, f32[64]{0:T(128)}, u32[]{:S(2)}) copy-start(f32[64]{0:T(128)} %param.19) | copy-start | bytes 772
  88.4 1.2 copy-start
  89.6 22.1 %copy-start.2 = (bf16[128,576]{1,0:T(8,128)(2,1)S(1)}, bf16[128,576]{1,0:T(8,128)(2,1)}, u32[]{:S(2)}) copy-start(bf16[128,576]{1,0:T(8,128)(2,1)} %fusion.5.first_ref) | copy-start | bytes 442372
  100.0 6.0 %collective-permute-start = (bf16[2,48,256]{2,1,0:T(8,128)(2,1)S(1)}, bf16[2,48,256]{2,1,0:T(8,128)(2,1)S(1)}, u32[]{:S(2)}, u32[]{:S(2)}) collective-permute-start(bf16[2,48,256]{2,1,0:T(8,128)(2,1)S(1)} %get-tuple-element.23), channel_id=1, source_target_pairs={{0,2},{2,0},{4,6},{6,4},{8,10},{10,8},{12,14},{14,12},{1,3},{3,1},... | collective-permute-start | bytes 147464 | tf_op jit(solution)/shard_map/ppermute | solution.py:528
  103.3 5.7 %collective-permute-start.1 = (bf16[2,48,256]{2,1,0:T(8,128)(2,1)S(1)}, bf16[2,48,256]{2,1,0:T(8,128)(2,1)S(1)}, u32[]{:S(2)}, u32[]{:S(2)}) collective-permute-start(bf16[2,48,256]{2,1,0:T(8,128)(2,1)S(1)} %get-tuple-element.24), channel_id=1, source_target_pairs={{2,4},{4,2},{6,8},{8,6},{10,12},{12,10},{3,5},{5,3},{7,9},{9,7},{1... | collective-permute-start | bytes 147464 | tf_op jit(solution)/shard_map/ppermute | solution.py:529
  105.2 5.7 %collective-permute-start.2 = (bf16[2,2,48,128]{3,2,1,0:T(8,128)(2,1)S(1)}, bf16[2,2,48,128]{3,2,1,0:T(8,128)(2,1)S(1)}, u32[]{:S(2)}, u32[]{:S(2)}) collective-permute-start(bf16[2,2,48,128]{3,2,1,0:T(8,128)(2,1)S(1)} %get-tuple-element.25.own_ref), channel_id=1, source_target_pairs={{0,1},{1,0},{2,3},{3,2},{4,5},{5,4},{6,7},{7,6},{8,9},{9,8},{10,11... | collective-permute-start | bytes 147464 | tf_op jit(solution)/shard_map/ppermute | solution.py:527
  106.0 4.9 %collective-permute-start.3 = (bf16[2,48,256]{2,1,0:T(8,128)(2,1)S(1)}, bf16[2,48,256]{2,1,0:T(8,128)(2,1)S(1)}, u32[]{:S(2)}, u32[]{:S(2)}) collective-permute-start(bf16[2,48,256]{2,1,0:T(8,128)(2,1)S(1)} %collective-permute-done.rim_a_ref), channel_id=1, source_target_pairs={{0,1},{1,0},{2,3},{3,2},{4,5},{5,4},{6,7},{7,6},{8,9},{9,8},{10,11... | collective-permute-start | bytes 147464 | tf_op jit(solution)/shard_map/ppermute | solution.py:530
  109.0 2.7 %collective-permute-start.4 = (bf16[2,48,256]{2,1,0:T(8,128)(2,1)S(1)}, bf16[2,48,256]{2,1,0:T(8,128)(2,1)S(1)}, u32[]{:S(2)}, u32[]{:S(2)}) collective-permute-start(bf16[2,48,256]{2,1,0:T(8,128)(2,1)S(1)} %collective-permute-done.1.rim_b_ref), channel_id=1, source_target_pairs={{0,1},{1,0},{2,3},{3,2},{4,5},{5,4},{6,7},{7,6},{8,9},{9,8},{10,11... | collective-permute-start | bytes 147464 | tf_op jit(solution)/shard_map/ppermute | solution.py:531

commit v6 on v5

--- a/solution.py
+++ b/solution.py
@@ -24,7 +24,7 @@
 INFO_ROWS = 16
 CELL_BASE = 32
 MIB = 1024 * 1024
-PACK_VMEM = 12 * MIB
+PACK_VMEM = 56 * MIB
 COMPOSITE_VMEM = 26 * MIB
 ENCODER_VMEM = 45 * MIB
 

time: 136 us -> 128 us (0.941)
  local copies, waits for them, and re-layouts: 11.7 us -> 7.08 us
  Pallas kernels: 41.3 us -> 38.7 us
    unnamed x21 -> x11, local copies, waits for them, and re-layouts: 8.14 us -> 3.49 us
    pallas_call x1, Pallas kernels: 7.73 us -> 5.15 us  [pack(): pl.pallas_call(functools.partial(pack_kernel, channels), grid_spec=pltpu....]
where the time goes in v6:
time: 128 us
  waiting for transfers between devices  62.3 us (49%)
  Pallas kernels  38.7 us (30%)
  starting transfers between devices  14.5 us (11%)
  local copies, waits for them, and re-layouts  7.08 us (6%)
  other arithmetic  4.98 us (4%)
    all_to_all x1, waiting for transfers between devices, shards(): lax.all_to_all(packets, tiles, split_axis=0, concat_axis=0, tiled=True)  58.4 us
    pallas_call x1, Pallas kernels, encoder(): pl.pallas_call(functools.partial(encoder_kernel, channels, hid), grid_spe...  23.2 us
    pallas_call x1, Pallas kernels, composite(): pl.pallas_call(functools.partial(composite_kernel, capacity, channels), g...  10.3 us
    all_to_all x1, starting transfers between devices, shards(): lax.all_to_all(packets, tiles, split_axis=0, concat_axis=0, tiled=True)  6.82 us
    pallas_call x1, Pallas kernels, pack(): pl.pallas_call(functools.partial(pack_kernel, channels), grid_spec=pltpu....  5.15 us
    ppermute x1, starting transfers between devices, shards(): rim_a = lax.ppermute(rim_a, 'ty', pairs_a)  3.58 us
    unnamed x11, local copies, waits for them, and re-layouts  3.49 us
    ppermute x1, waiting for transfers between devices, shards(): rim_b = lax.ppermute(rim_b, 'ty', pairs_b)  3.02 us
  transfers between devices with their start and end apart: 6, of which 3 were waited for; matrix products, arithmetic and copies ran while one was open for 8% of the time, Pallas kernels for 0%

profile of v6, /device:TPU:9, one launch (start us, length us, event | category | flops | bytes accessed | tf_op | source)
XLA Modules:
  0.0 127.6 jit_solution(1737537642963283116)
XLA Ops:
  0.0 5.1 %pack.1 = bf16[16,784,128]{2,1,0:T(8,128)(2,1)} custom-call(s32[16,16]{1,0:T(8,128)} %bitcast.32, s32[1,16]{1,0:T(1,128)} %count_ref.1, bf16[256,48,128]{2,1,0:T(8,128)(2,1)} %sweeps_ref.1, s32[1,16,16]{2,1,0:T(8,128)} %cell_ref.1, s32[1,16,16]{2,1,0:T(8,128)} %templ_ref.1), custom_call_target="tpu_custom_call" | custom-call | tf_op jit(solution)/shard_map/pack/pallas_call | solution.py:404
  5.2 6.8 %all-to-all-start = ((bf16[16,784,128]{2,1,0:T(8,128)(2,1)}), bf16[16,784,128]{2,1,0:T(8,128)(2,1)S(1)}, u32[]{:S(2)}, u32[]{:S(2)}) async-start(bf16[16,784,128]{2,1,0:T(8,128)(2,1)} %pack.1), calls=%async_computation | async-start | bytes 6422528 | tf_op jit(solution)/shard_map/all_to_all | solution.py:513
  12.1 0.6 fusion.6
  12.7 0.1 copy.23
  12.8 0.9 copy.25
  13.7 0.7 copy.24
  14.4 1.0 copy.20
  15.4 0.8 copy.21
  16.2 2.2 %copy.17 = bf16[32,128,128]{1,2,0:T(8,128)(2,1)} copy(bf16[32,128,128]{2,1,0:T(8,128)(2,1)} %param.15) | data formatting | bytes 2097152 | tf_op args[5]
  18.6 0.9 pad_maximum_fusion.edge_first_ref
  19.5 0.7 fusion.5.first_ref
  20.2 1.1 fusion.4.second_ref
  21.3 1.6 %convert_reduce_fusion.weight_ref = f32[32,128]{1,0:T(8,128)S(1)} fusion(bf16[32,128,128]{2,1,0:T(8,128)(2,1)} %param.15), kind=kLoop, calls=%fused_computation | loop fusion | flops 1044480 | bytes 1064960 | tf_op jit(solution)/shard_map/reduce_sum | solution.py:515
  22.9 58.4 %all-to-all-done.recv_ref = bf16[16,784,128]{2,1,0:T(8,128)(2,1)S(1)} async-done(((bf16[16,784,128]{2,1,0:T(8,128)(2,1)}), bf16[16,784,128]{2,1,0:T(8,128)(2,1)S(1)}, u32[]{:S(2)}, u32[]{:S(2)}) %all-to-all-start) | async-done | bytes 3211296 | tf_op jit(solution)/shard_map/all_to_all | solution.py:513
  81.2 1.2 copy-done
  82.5 10.3 %composite.1 = (bf16[9216,256]{1,0:T(8,128)(2,1)S(1)}, bf16[2,2,48,128]{3,2,1,0:T(8,128)(2,1)S(1)}, bf16[2,48,256]{2,1,0:T(8,128)(2,1)S(1)}, bf16[2,48,256]{2,1,0:T(8,128)(2,1)S(1)}) custom-call(s32[4]{0:T(128)S(1)} %pad_add_fusion.col_ref.place_ref, bf16[16,784,128]{2,1,0:T(8,128)(2,1)S(1)} %all-to-all-done.recv_ref, bf16[32,128,128]{2,1,0:T(8,128)(2,1)S(1)} %bitcast.22, ...), custom_call_target="tpu_custom_call" | custom-call | tf_op jit(solution)/shard_map/composite/pallas_call | solution.py:424
  92.8 3.6 %collective-permute-start = (bf16[2,48,256]{2,1,0:T(8,128)(2,1)S(1)}, bf16[2,48,256]{2,1,0:T(8,128)(2,1)S(1)}, u32[]{:S(2)}, u32[]{:S(2)}) collective-permute-start(bf16[2,48,256]{2,1,0:T(8,128)(2,1)S(1)} %get-tuple-element.23), channel_id=1, source_target_pairs={{0,2},{2,0},{4,6},{6,4},{8,10},{10,8},{12,14},{14,12},{1,3},{3,1},... | collective-permute-start | bytes 147464 | tf_op jit(solution)/shard_map/ppermute | solution.py:528
  96.4 1.9 %collective-permute-start.1 = (bf16[2,48,256]{2,1,0:T(8,128)(2,1)S(1)}, bf16[2,48,256]{2,1,0:T(8,128)(2,1)S(1)}, u32[]{:S(2)}, u32[]{:S(2)}) collective-permute-start(bf16[2,48,256]{2,1,0:T(8,128)(2,1)S(1)} %get-tuple-element.24), channel_id=1, source_target_pairs={{2,4},{4,2},{6,8},{8,6},{10,12},{12,10},{3,5},{5,3},{7,9},{9,7},{1... | collective-permute-start | bytes 147464 | tf_op jit(solution)/shard_map/ppermute | solution.py:529
  98.3 0.3 collective-permute-start.2
  98.6 0.4 collective-permute-start.3
  99.1 3.0 %collective-permute-done.1.rim_b_ref = bf16[2,48,256]{2,1,0:T(8,128)(2,1)S(1)} collective-permute-done((bf16[2,48,256]{2,1,0:T(8,128)(2,1)S(1)}, bf16[2,48,256]{2,1,0:T(8,128)(2,1)S(1)}, u32[]{:S(2)}, u32[]{:S(2)}) %collective-permute-start.1) | collective-permute-done | bytes 49184 | tf_op jit(solution)/shard_map/ppermute | solution.py:529
  102.1 1.4 %collective-permute-start.4 = (bf16[2,48,256]{2,1,0:T(8,128)(2,1)S(1)}, bf16[2,48,256]{2,1,0:T(8,128)(2,1)S(1)}, u32[]{:S(2)}, u32[]{:S(2)}) collective-permute-start(bf16[2,48,256]{2,1,0:T(8,128)(2,1)S(1)} %collective-permute-done.1.rim_b_ref), channel_id=1, source_target_pairs={{0,1},{1,0},{2,3},{3,2},{4,5},{5,4},{6,7},{7,6},{8,9},{9,8},{10,11... | collective-permute-start | bytes 147464 | tf_op jit(solution)/shard_map/ppermute | solution.py:531
  103.5 0.9 collective-permute-done.4.side_b_ref
  104.4 23.2 %encoder.1 = bf16[64,192,256]{2,1,0:T(8,128)(2,1)} custom-call(s32[4]{0:T(128)S(1)} %pad_add_fusion.col_ref.place_ref, bf16[192,48,256]{2,1,0:T(8,128)(2,1)S(1)} %bitcast.21, bf16[2,48,256]{2,1,0:T(8,128)(2,1)S(1)} %collective-permute-done.rim_a_ref, bf16[2,48,256]{2,1,0:T(8,128)(2,1)S(1)} %collective-permute-done.1.rim_b_ref, ...), custom_call_target="tpu_custom_call" | custom-call | tf_op jit(solution)/shard_map/encoder/pallas_call | solution.py:458
  (14 shorter events, 0.2 us)
Async XLA Ops:
  5.2 6.8 %copy-start.4 = (bf16[9,64,48]{1,2,0:T(8,128)(2,1)S(1)}, bf16[9,64,48]{1,2,0:T(8,128)(2,1)}, u32[]{:S(2)}) copy-start(bf16[9,64,48]{1,2,0:T(8,128)(2,1)} %param.16) | copy-start | bytes 165892
  5.2 76.1 %all-to-all-start = ((bf16[16,784,128]{2,1,0:T(8,128)(2,1)}), bf16[16,784,128]{2,1,0:T(8,128)(2,1)S(1)}, u32[]{:S(2)}, u32[]{:S(2)}) async-start(bf16[16,784,128]{2,1,0:T(8,128)(2,1)} %pack.1), calls=%async_computation | async-start | bytes 6422528 | tf_op jit(solution)/shard_map/all_to_all | solution.py:513
  18.5 85.9 %copy-start.2 = (f32[64]{0:T(128)S(1)}, f32[64]{0:T(128)}, u32[]{:S(2)}) copy-start(f32[64]{0:T(128)} %param.17) | copy-start | bytes 772
  18.5 85.9 %copy-start.3 = (f32[64]{0:T(128)S(1)}, f32[64]{0:T(128)}, u32[]{:S(2)}) copy-start(f32[64]{0:T(128)} %param.19) | copy-start | bytes 772
  81.2 1.2 copy-start
  82.5 22.0 %copy-start.1 = (bf16[128,576]{1,0:T(8,128)(2,1)S(1)}, bf16[128,576]{1,0:T(8,128)(2,1)}, u32[]{:S(2)}) copy-start(bf16[128,576]{1,0:T(8,128)(2,1)} %fusion.5.first_ref) | copy-start | bytes 442372
  92.8 5.8 %collective-permute-start = (bf16[2,48,256]{2,1,0:T(8,128)(2,1)S(1)}, bf16[2,48,256]{2,1,0:T(8,128)(2,1)S(1)}, u32[]{:S(2)}, u32[]{:S(2)}) collective-permute-start(bf16[2,48,256]{2,1,0:T(8,128)(2,1)S(1)} %get-tuple-element.23), channel_id=1, source_target_pairs={{0,2},{2,0},{4,6},{6,4},{8,10},{10,8},{12,14},{14,12},{1,3},{3,1},... | collective-permute-start | bytes 147464 | tf_op jit(solution)/shard_map/ppermute | solution.py:528
  96.4 5.7 %collective-permute-start.1 = (bf16[2,48,256]{2,1,0:T(8,128)(2,1)S(1)}, bf16[2,48,256]{2,1,0:T(8,128)(2,1)S(1)}, u32[]{:S(2)}, u32[]{:S(2)}) collective-permute-start(bf16[2,48,256]{2,1,0:T(8,128)(2,1)S(1)} %get-tuple-element.24), channel_id=1, source_target_pairs={{2,4},{4,2},{6,8},{8,6},{10,12},{12,10},{3,5},{5,3},{7,9},{9,7},{1... | collective-permute-start | bytes 147464 | tf_op jit(solution)/shard_map/ppermute | solution.py:529
  98.3 5.2 %collective-permute-start.2 = (bf16[2,2,48,128]{3,2,1,0:T(8,128)(2,1)S(1)}, bf16[2,2,48,128]{3,2,1,0:T(8,128)(2,1)S(1)}, u32[]{:S(2)}, u32[]{:S(2)}) collective-permute-start(bf16[2,2,48,128]{3,2,1,0:T(8,128)(2,1)S(1)} %get-tuple-element.25.own_ref), channel_id=1, source_target_pairs={{0,1},{1,0},{2,3},{3,2},{4,5},{5,4},{6,7},{7,6},{8,9},{9,8},{10,11... | collective-permute-start | bytes 147464 | tf_op jit(solution)/shard_map/ppermute | solution.py:527
  98.6 4.9 %collective-permute-start.3 = (bf16[2,48,256]{2,1,0:T(8,128)(2,1)S(1)}, bf16[2,48,256]{2,1,0:T(8,128)(2,1)S(1)}, u32[]{:S(2)}, u32[]{:S(2)}) collective-permute-start(bf16[2,48,256]{2,1,0:T(8,128)(2,1)S(1)} %collective-permute-done.rim_a_ref), channel_id=1, source_target_pairs={{0,1},{1,0},{2,3},{3,2},{4,5},{5,4},{6,7},{7,6},{8,9},{9,8},{10,11... | collective-permute-start | bytes 147464 | tf_op jit(solution)/shard_map/ppermute | solution.py:530
  102.1 2.3 %collective-permute-start.4 = (bf16[2,48,256]{2,1,0:T(8,128)(2,1)S(1)}, bf16[2,48,256]{2,1,0:T(8,128)(2,1)S(1)}, u32[]{:S(2)}, u32[]{:S(2)}) collective-permute-start(bf16[2,48,256]{2,1,0:T(8,128)(2,1)S(1)} %collective-permute-done.1.rim_b_ref), channel_id=1, source_target_pairs={{0,1},{1,0},{2,3},{3,2},{4,5},{5,4},{6,7},{7,6},{8,9},{9,8},{10,11... | collective-permute-start | bytes 147464 | tf_op jit(solution)/shard_map/ppermute | solution.py:531

commit v7 on v6

--- a/solution.py
+++ b/solution.py
@@ -14,19 +14,19 @@
 HALO = 2
 EDGE_TILES = 2
 LANE_BASE = 8
-ROW_STEPS = 4
+ROW_STEPS = 3
 CHUNK = 8
 LOADS = 4
 GROUP = 2
-OUT_ROWS = 16
+OUT_ROWS = 32
 LAG = 2
-PACK_STEPS = 1
+PACK_PARTS = 8
 INFO_ROWS = 16
 CELL_BASE = 32
 MIB = 1024 * 1024
 PACK_VMEM = 56 * MIB
 COMPOSITE_VMEM = 26 * MIB
-ENCODER_VMEM = 45 * MIB
+ENCODER_VMEM = 48 * MIB
 
 F32 = jnp.float32
 BF16 = jnp.bfloat16
@@ -42,43 +42,51 @@
 
 
 def pack_kernel(
-    channels, block_ref, count_ref, sweeps_ref, cell_ref, templ_ref, out_ref, padded, sem
+    channels, block_ref, count_ref, sweeps_ref, cell_ref, templ_ref, out_ref, packets, padded, sems
 ):
-    part = out_ref.shape[0]
-    capacity = block_ref.shape[1]
+    peers, capacity = block_ref.shape
     held = capacity * channels
-    first = pl.program_id(0) * part
+    part = peers // PACK_PARTS
 
     def send_tile(d, carry):
         for q in range(capacity):
             pltpu.make_async_copy(
-                sweeps_ref.at[block_ref[first + d, q]],
-                out_ref.at[d, pl.ds(q * channels, channels), :],
-                sem,
+                sweeps_ref.at[block_ref[d, q]],
+                packets.at[d, pl.ds(q * channels, channels), :],
+                sems.at[d // part],
             ).start()
         return carry
 
-    lax.fori_loop(0, part, send_tile, 0)
+    lax.fori_loop(0, peers, send_tile, 0)
     padded[...] = jnp.zeros(padded.shape, F32)
     padded[0, :, 0:capacity] = cell_ref[0].astype(F32)
     padded[1, :, 0:capacity] = templ_ref[0].astype(F32)
     lane = lane_index((1, LANES))
     which = lax.broadcasted_iota(jnp.int32, (INFO_ROWS, LANES), 0)
-    for d in range(part):
-        live = lane < count_ref[0, first + d]
-        cell = jnp.where(live, padded[0, pl.ds(first + d, 1), :], float(CBLK))
+    for d in range(peers):
+        live = lane < count_ref[0, d]
+        cell = jnp.where(live, padded[0, d : d + 1, :], float(CBLK))
         high = jnp.floor(cell * (1.0 / CELL_BASE))
         low = cell - high * CELL_BASE
-        template = padded[1, pl.ds(first + d, 1), :]
+        template = padded[1, d : d + 1, :]
         rows = jnp.where(which == 0, high, jnp.where(which == 1, low, template))
-        out_ref[d, held : held + INFO_ROWS, :] = rows.astype(BF16)
-    arrived = out_ref.at[:, pl.ds(0, held), :]
-    pltpu.make_async_copy(arrived, arrived, sem).wait()
+        packets[d, held : held + INFO_ROWS, :] = rows.astype(BF16)
+    leaving = []
+    for k in range(PACK_PARTS):
+        mine = pl.ds(k * part, part)
+        arrived = packets.at[mine, pl.ds(0, held), :]
+        pltpu.make_async_copy(arrived, arrived, sems.at[k]).wait()
+        leaving.append(
+            pltpu.make_async_copy(packets.at[mine], out_ref.at[mine], sems.at[PACK_PARTS + k])
+        )
+        leaving[-1].start()
+    for copy in leaving:
+        copy.wait()
 
 
 def composite_kernel(
     capacity, channels, col_ref, recv_ref, table_ref, weight_ref,
-    comp_ref, edge_ref, rim_a, rim_b, acc, den, strip, recv, raw, numbers, slots, sems,
+    comp_ref, edge_ref, rim_a, rim_b, acc, den, strip, recv, table, raw, numbers, slots, sems,
 ):
     step = pl.program_id(0)
     peers = recv_ref.shape[0]
@@ -101,6 +109,8 @@
             )
             for k in range(LOADS)
         ]
+        tables = pltpu.make_async_copy(table_ref, table, sems.at[LOADS + 2])
+        tables.start()
         for copy in copies:
             copy.start()
         listing.wait()
@@ -122,13 +132,14 @@
         strip[...] = jnp.zeros(strip.shape, BF16)
 
         moved.wait()
+        tables.wait()
 
         def add_slots(source, carry):
             terms = []
             for q in range(capacity):
                 block = recv[source, q * channels : (q + 1) * channels, :]
                 template = slots[peers + source, q]
-                terms.append(jnp.dot(block, table_ref[template], preferred_element_type=F32))
+                terms.append(jnp.dot(block, table[template], preferred_element_type=F32))
             for q in range(capacity):
                 cell = slots[source, q]
                 acc[cell] += terms[q]
@@ -138,7 +149,7 @@
 
         for k in range(LOADS):
             copies[k].wait()
-            lax.fori_loop(k * part, (k + 1) * part, add_slots, 0)
+            lax.fori_loop(k * part, (k + 1) * part, add_slots, 0, unroll=4)
         den[...] = 1.0 / (1.0 + den[...])
 
     rows = TH // ROW_STEPS
@@ -148,14 +159,14 @@
 
     def some_rows(i, carry):
         base = step * rows + i * CHUNK
-        picked = [jnp.zeros((channels, LANES), F32), jnp.zeros((channels, LANES), F32)]
+        picked = [jnp.zeros((channels, LANES), BF16), jnp.zeros((channels, LANES), BF16)]
         for u in range(CHUNK):
             r = base + u
             out = pl.multiple_of((i * CHUNK + u) * channels, 16)
             parts = []
             for m in range(2):
-                value = acc[2 * r + m] * den[pl.ds(2 * r + m, 1), :]
-                comp_ref[pl.ds(out, channels), m * LANES : (m + 1) * LANES] = value.astype(BF16)
+                value = (acc[2 * r + m] * den[pl.ds(2 * r + m, 1), :]).astype(BF16)
+                comp_ref[pl.ds(out, channels), m * LANES : (m + 1) * LANES] = value
                 parts.append(value)
             side = jnp.where(col == 0, parts[1], parts[0])
             at = (r + LANE_BASE) % LANES
@@ -166,12 +177,10 @@
         first = (base + LANE_BASE) % LANES
         inside = (lane >= first) & (lane < first + CHUNK)
         for p in range(2):
-            strip[p, tile] = jnp.where(
-                inside, picked[p], strip[p, tile].astype(F32)
-            ).astype(BF16)
+            strip[p, tile] = jnp.where(inside, picked[p], strip[p, tile])
         return carry
 
-    lax.fori_loop(0, rows // CHUNK, some_rows, 0)
+    lax.fori_loop(0, rows // CHUNK, some_rows, 0, unroll=2)
 
     rim = HALO * channels
     top = step == 0
@@ -400,15 +409,18 @@
     peers, capacity = route_block.shape
     channels = sweeps.shape[1]
     rows = capacity * channels + INFO_ROWS
-    part = peers // PACK_STEPS
     return pl.pallas_call(
         functools.partial(pack_kernel, channels),
         grid_spec=pltpu.PrefetchScalarGridSpec(
             num_scalar_prefetch=2,
-            grid=(PACK_STEPS,),
+            grid=(1,),
             in_specs=[pl.BlockSpec(memory_space=pl.ANY), whole_in_vmem(), whole_in_vmem()],
-            out_specs=pl.BlockSpec((part, rows, LANES), lambda i, *_: (i, 0, 0)),
-            scratch_shapes=[pltpu.VMEM((2, peers, LANES), F32), pltpu.SemaphoreType.DMA],
+            out_specs=pl.BlockSpec(memory_space=pl.ANY),
+            scratch_shapes=[
+                pltpu.VMEM((peers, rows, LANES), BF16),
+                pltpu.VMEM((2, peers, LANES), F32),
+                pltpu.SemaphoreType.DMA((2 * PACK_PARTS,)),
+            ],
         ),
         out_shape=jax.ShapeDtypeStruct((peers, rows, LANES), BF16),
         compiler_params=pltpu.CompilerParams(
@@ -426,17 +438,22 @@
         grid_spec=pltpu.PrefetchScalarGridSpec(
             num_scalar_prefetch=1,
             grid=(ROW_STEPS,),
-            in_specs=[pl.BlockSpec(memory_space=pl.ANY), whole_in_vmem(), whole_in_vmem()],
+            in_specs=[
+                pl.BlockSpec(memory_space=pl.ANY),
+                pl.BlockSpec(memory_space=pltpu.HBM),
+                whole_in_vmem(),
+            ],
             out_specs=[pl.BlockSpec((rows, TW), lambda i, *_: (i, 0))] + [whole_in_vmem()] * 3,
             scratch_shapes=[
                 pltpu.VMEM((CBLK + 1, channels, LANES), F32),
                 pltpu.VMEM((CBLK + 8, LANES), F32),
                 pltpu.VMEM((2, EDGE_TILES, channels, LANES), BF16),
                 pltpu.VMEM((peers, capacity * channels, LANES), BF16),
+                pltpu.VMEM(table.shape, BF16),
                 pltpu.VMEM((peers, INFO_ROWS, LANES), BF16),
                 pltpu.VMEM((2 * peers, LANES), jnp.int32),
                 pltpu.SMEM((2 * peers, LANES), jnp.int32),
-                pltpu.SemaphoreType.DMA((LOADS + 2,)),
+                pltpu.SemaphoreType.DMA((LOADS + 3,)),
             ],
         ),
         out_shape=[
@@ -465,8 +482,8 @@
                 (hid, OUT_ROWS, TW), lambda i, *_: (0, jnp.maximum(i - LAG, 0), 0)
             ),
             scratch_shapes=[
-                pltpu.VMEM((steps * OUT_ROWS + 2 * GROUP, 3, channels, TW), BF16),
-                pltpu.VMEM(((steps - 1) * OUT_ROWS + GROUP, 3, hid, TW), BF16),
+                pltpu.VMEM((TH + 2 * HALO, 3, channels, TW), BF16),
+                pltpu.VMEM((TH + 2, 3, hid, TW), BF16),
                 pltpu.VMEM((EDGE_TILES, channels, LANES), BF16),
                 pltpu.VMEM((EDGE_TILES, hid, LANES), BF16),
                 pltpu.VMEM((2, hid, LANES), F32),

time: 128 us -> 125 us (0.977)
  Pallas kernels: 38.7 us -> 35.3 us
    pallas_call x1, Pallas kernels: 10.3 us -> 8.41 us  [composite(): pl.pallas_call(functools.partial(composite_kernel, capacity, channels), g...]
    pallas_call x1, Pallas kernels: 23.2 us -> 21.7 us  [encoder(): pl.pallas_call(functools.partial(encoder_kernel, channels, hid), grid_spe...]
  transfers between devices with their start and end apart: 6 -> 6, of which waited for: 3 -> 3; matrix products, arithmetic and copies ran while one was open for 8% -> 9% of each run, Pallas kernels for 0% -> 0%
where the time goes in v7:
time: 125 us; the launch traced here: 124 us
  waiting for transfers between devices  62.3 us (50%)
  Pallas kernels  35.3 us (28%)
  starting transfers between devices  14.4 us (12%)
  local copies, waits for them, and re-layouts  7.08 us (6%)
  other arithmetic  4.98 us (4%)
    all_to_all x1, waiting for transfers between devices, shards(): lax.all_to_all(packets, tiles, split_axis=0, concat_axis=0, tiled=True)  58.4 us
    pallas_call x1, Pallas kernels, encoder(): pl.pallas_call(functools.partial(encoder_kernel, channels, hid), grid_spe...  21.7 us
    pallas_call x1, Pallas kernels, composite(): pl.pallas_call(functools.partial(composite_kernel, capacity, channels), g...  8.41 us
    all_to_all x1, starting transfers between devices, shards(): lax.all_to_all(packets, tiles, split_axis=0, concat_axis=0, tiled=True)  6.81 us
    pallas_call x1, Pallas kernels, pack(): pl.pallas_call(functools.partial(pack_kernel, channels), grid_spec=pltpu....  5.18 us
    unnamed x11, local copies, waits for them, and re-layouts  3.49 us
    ppermute x1, starting transfers between devices, shards(): rim_a = lax.ppermute(rim_a, 'ty', pairs_a)  3.3 us
    ppermute x1, waiting for transfers between devices, shards(): rim_b = lax.ppermute(rim_b, 'ty', pairs_b)  3.02 us
  transfers between devices with their start and end apart: 6, of which 3 were waited for; matrix products, arithmetic and copies ran while one was open for 9% of the time, Pallas kernels for 0%

profile of v7, /device:TPU:9, one launch (start us, length us, event | category | flops | bytes accessed | tf_op | source)
XLA Modules:
  0.0 124.1 jit_solution(111584577404420415)
XLA Ops:
  0.0 5.2 %pack.1 = bf16[16,784,128]{2,1,0:T(8,128)(2,1)} custom-call(s32[16,16]{1,0:T(8,128)} %bitcast.32, s32[1,16]{1,0:T(1,128)} %count_ref.1, bf16[256,48,128]{2,1,0:T(8,128)(2,1)} %sweeps_ref.1, s32[1,16,16]{2,1,0:T(8,128)} %cell_ref.1, s32[1,16,16]{2,1,0:T(8,128)} %templ_ref.1), custom_call_target="tpu_custom_call" | custom-call | tf_op jit(solution)/shard_map/pack/pallas_call | solution.py:412
  5.2 6.8 %all-to-all-start = ((bf16[16,784,128]{2,1,0:T(8,128)(2,1)}), bf16[16,784,128]{2,1,0:T(8,128)(2,1)S(1)}, u32[]{:S(2)}, u32[]{:S(2)}) async-start(bf16[16,784,128]{2,1,0:T(8,128)(2,1)} %pack.1), calls=%async_computation | async-start | bytes 6422528 | tf_op jit(solution)/shard_map/all_to_all | solution.py:530
  12.1 0.6 fusion.6
  12.7 0.1 copy.23
  12.8 0.9 copy.25
  13.7 0.7 copy.24
  14.4 1.0 copy.20
  15.5 0.8 copy.21
  16.2 2.2 %copy.17 = bf16[32,128,128]{1,2,0:T(8,128)(2,1)} copy(bf16[32,128,128]{2,1,0:T(8,128)(2,1)} %param.15) | data formatting | bytes 2097152 | tf_op args[5]
  18.6 0.9 pad_maximum_fusion.edge_first_ref
  19.5 0.7 fusion.5.first_ref
  20.2 1.1 fusion.4.second_ref
  21.3 1.6 %convert_reduce_fusion.weight_ref = f32[32,128]{1,0:T(8,128)S(1)} fusion(bf16[32,128,128]{2,1,0:T(8,128)(2,1)} %param.15), kind=kLoop, calls=%fused_computation | loop fusion | flops 1044480 | bytes 1064960 | tf_op jit(solution)/shard_map/reduce_sum | solution.py:532
  22.9 58.4 %all-to-all-done.recv_ref = bf16[16,784,128]{2,1,0:T(8,128)(2,1)S(1)} async-done(((bf16[16,784,128]{2,1,0:T(8,128)(2,1)}), bf16[16,784,128]{2,1,0:T(8,128)(2,1)S(1)}, u32[]{:S(2)}, u32[]{:S(2)}) %all-to-all-start) | async-done | bytes 3211296 | tf_op jit(solution)/shard_map/all_to_all | solution.py:530
  81.3 1.2 copy-done
  82.5 8.4 %composite.1 = (bf16[9216,256]{1,0:T(8,128)(2,1)S(1)}, bf16[2,2,48,128]{3,2,1,0:T(8,128)(2,1)S(1)}, bf16[2,48,256]{2,1,0:T(8,128)(2,1)S(1)}, bf16[2,48,256]{2,1,0:T(8,128)(2,1)S(1)}) custom-call(s32[4]{0:T(128)S(1)} %pad_add_fusion.col_ref.place_ref, bf16[16,784,128]{2,1,0:T(8,128)(2,1)S(1)} %all-to-all-done.recv_ref, bf16[32,128,128]{2,1,0:T(8,128)(2,1)S(1)} %bitcast.22, ...), custom_call_target="tpu_custom_call" | custom-call | tf_op jit(solution)/shard_map/composite/pallas_call | solution.py:436
  90.9 3.3 %collective-permute-start = (bf16[2,48,256]{2,1,0:T(8,128)(2,1)S(1)}, bf16[2,48,256]{2,1,0:T(8,128)(2,1)S(1)}, u32[]{:S(2)}, u32[]{:S(2)}) collective-permute-start(bf16[2,48,256]{2,1,0:T(8,128)(2,1)S(1)} %get-tuple-element.23), channel_id=1, source_target_pairs={{0,2},{2,0},{4,6},{6,4},{8,10},{10,8},{12,14},{14,12},{1,3},{3,1},... | collective-permute-start | bytes 147464 | tf_op jit(solution)/shard_map/ppermute | solution.py:545
  94.2 1.9 %collective-permute-start.1 = (bf16[2,48,256]{2,1,0:T(8,128)(2,1)S(1)}, bf16[2,48,256]{2,1,0:T(8,128)(2,1)S(1)}, u32[]{:S(2)}, u32[]{:S(2)}) collective-permute-start(bf16[2,48,256]{2,1,0:T(8,128)(2,1)S(1)} %get-tuple-element.24), channel_id=1, source_target_pairs={{2,4},{4,2},{6,8},{8,6},{10,12},{12,10},{3,5},{5,3},{7,9},{9,7},{1... | collective-permute-start | bytes 147464 | tf_op jit(solution)/shard_map/ppermute | solution.py:546
  96.1 0.5 collective-permute-start.2
  96.7 0.2 collective-permute-start.3
  96.9 3.0 %collective-permute-done.1.rim_b_ref = bf16[2,48,256]{2,1,0:T(8,128)(2,1)S(1)} collective-permute-done((bf16[2,48,256]{2,1,0:T(8,128)(2,1)S(1)}, bf16[2,48,256]{2,1,0:T(8,128)(2,1)S(1)}, u32[]{:S(2)}, u32[]{:S(2)}) %collective-permute-start.1) | collective-permute-done | bytes 49184 | tf_op jit(solution)/shard_map/ppermute | solution.py:546
  99.9 1.6 %collective-permute-start.4 = (bf16[2,48,256]{2,1,0:T(8,128)(2,1)S(1)}, bf16[2,48,256]{2,1,0:T(8,128)(2,1)S(1)}, u32[]{:S(2)}, u32[]{:S(2)}) collective-permute-start(bf16[2,48,256]{2,1,0:T(8,128)(2,1)S(1)} %collective-permute-done.1.rim_b_ref), channel_id=1, source_target_pairs={{0,1},{1,0},{2,3},{3,2},{4,5},{5,4},{6,7},{7,6},{8,9},{9,8},{10,11... | collective-permute-start | bytes 147464 | tf_op jit(solution)/shard_map/ppermute | solution.py:548
  101.5 0.9 collective-permute-done.4.side_b_ref
  102.4 21.7 %encoder.1 = bf16[64,192,256]{2,1,0:T(8,128)(2,1)} custom-call(s32[4]{0:T(128)S(1)} %pad_add_fusion.col_ref.place_ref, bf16[192,48,256]{2,1,0:T(8,128)(2,1)S(1)} %bitcast.21, bf16[2,48,256]{2,1,0:T(8,128)(2,1)S(1)} %collective-permute-done.rim_a_ref, bf16[2,48,256]{2,1,0:T(8,128)(2,1)S(1)} %collective-permute-done.1.rim_b_ref, ...), custom_call_target="tpu_custom_call" | custom-call | tf_op jit(solution)/shard_map/encoder/pallas_call | solution.py:475
  (14 shorter events, 0.2 us)
Async XLA Ops:
  5.2 6.8 %copy-start.4 = (bf16[9,64,48]{1,2,0:T(8,128)(2,1)S(1)}, bf16[9,64,48]{1,2,0:T(8,128)(2,1)}, u32[]{:S(2)}) copy-start(bf16[9,64,48]{1,2,0:T(8,128)(2,1)} %param.16) | copy-start | bytes 165892
  5.2 76.1 %all-to-all-start = ((bf16[16,784,128]{2,1,0:T(8,128)(2,1)}), bf16[16,784,128]{2,1,0:T(8,128)(2,1)S(1)}, u32[]{:S(2)}, u32[]{:S(2)}) async-start(bf16[16,784,128]{2,1,0:T(8,128)(2,1)} %pack.1), calls=%async_computation | async-start | bytes 6422528 | tf_op jit(solution)/shard_map/all_to_all | solution.py:530
  18.5 83.9 %copy-start.2 = (f32[64]{0:T(128)S(1)}, f32[64]{0:T(128)}, u32[]{:S(2)}) copy-start(f32[64]{0:T(128)} %param.17) | copy-start | bytes 772
  18.5 83.9 %copy-start.3 = (f32[64]{0:T(128)S(1)}, f32[64]{0:T(128)}, u32[]{:S(2)}) copy-start(f32[64]{0:T(128)} %param.19) | copy-start | bytes 772
  81.3 1.2 copy-start
  82.5 20.0 %copy-start.1 = (bf16[128,576]{1,0:T(8,128)(2,1)S(1)}, bf16[128,576]{1,0:T(8,128)(2,1)}, u32[]{:S(2)}) copy-start(bf16[128,576]{1,0:T(8,128)(2,1)} %fusion.5.first_ref) | copy-start | bytes 442372
  90.9 5.8 %collective-permute-start = (bf16[2,48,256]{2,1,0:T(8,128)(2,1)S(1)}, bf16[2,48,256]{2,1,0:T(8,128)(2,1)S(1)}, u32[]{:S(2)}, u32[]{:S(2)}) collective-permute-start(bf16[2,48,256]{2,1,0:T(8,128)(2,1)S(1)} %get-tuple-element.23), channel_id=1, source_target_pairs={{0,2},{2,0},{4,6},{6,4},{8,10},{10,8},{12,14},{14,12},{1,3},{3,1},... | collective-permute-start | bytes 147464 | tf_op jit(solution)/shard_map/ppermute | solution.py:545
  94.2 5.7 %collective-permute-start.1 = (bf16[2,48,256]{2,1,0:T(8,128)(2,1)S(1)}, bf16[2,48,256]{2,1,0:T(8,128)(2,1)S(1)}, u32[]{:S(2)}, u32[]{:S(2)}) collective-permute-start(bf16[2,48,256]{2,1,0:T(8,128)(2,1)S(1)} %get-tuple-element.24), channel_id=1, source_target_pairs={{2,4},{4,2},{6,8},{8,6},{10,12},{12,10},{3,5},{5,3},{7,9},{9,7},{1... | collective-permute-start | bytes 147464 | tf_op jit(solution)/shard_map/ppermute | solution.py:546
  96.1 5.4 %collective-permute-start.2 = (bf16[2,2,48,128]{3,2,1,0:T(8,128)(2,1)S(1)}, bf16[2,2,48,128]{3,2,1,0:T(8,128)(2,1)S(1)}, u32[]{:S(2)}, u32[]{:S(2)}) collective-permute-start(bf16[2,2,48,128]{3,2,1,0:T(8,128)(2,1)S(1)} %get-tuple-element.25.own_ref), channel_id=1, source_target_pairs={{0,1},{1,0},{2,3},{3,2},{4,5},{5,4},{6,7},{7,6},{8,9},{9,8},{10,11... | collective-permute-start | bytes 147464 | tf_op jit(solution)/shard_map/ppermute | solution.py:544
  96.7 4.9 %collective-permute-start.3 = (bf16[2,48,256]{2,1,0:T(8,128)(2,1)S(1)}, bf16[2,48,256]{2,1,0:T(8,128)(2,1)S(1)}, u32[]{:S(2)}, u32[]{:S(2)}) collective-permute-start(bf16[2,48,256]{2,1,0:T(8,128)(2,1)S(1)} %collective-permute-done.rim_a_ref), channel_id=1, source_target_pairs={{0,1},{1,0},{2,3},{3,2},{4,5},{5,4},{6,7},{7,6},{8,9},{9,8},{10,11... | collective-permute-start | bytes 147464 | tf_op jit(solution)/shard_map/ppermute | solution.py:547
  99.9 2.5 %collective-permute-start.4 = (bf16[2,48,256]{2,1,0:T(8,128)(2,1)S(1)}, bf16[2,48,256]{2,1,0:T(8,128)(2,1)S(1)}, u32[]{:S(2)}, u32[]{:S(2)}) collective-permute-start(bf16[2,48,256]{2,1,0:T(8,128)(2,1)S(1)} %collective-permute-done.1.rim_b_ref), channel_id=1, source_target_pairs={{0,1},{1,0},{2,3},{3,2},{4,5},{5,4},{6,7},{7,6},{8,9},{9,8},{10,11... | collective-permute-start | bytes 147464 | tf_op jit(solution)/shard_map/ppermute | solution.py:548

commit v8 on v7

--- a/solution.py
+++ b/solution.py
@@ -16,7 +16,7 @@
 LANE_BASE = 8
 ROW_STEPS = 3
 CHUNK = 8
-LOADS = 4
+LOADS = 2
 GROUP = 2
 OUT_ROWS = 32
 LAG = 2
@@ -149,7 +149,7 @@
 
         for k in range(LOADS):
             copies[k].wait()
-            lax.fori_loop(k * part, (k + 1) * part, add_slots, 0, unroll=4)
+            lax.fori_loop(k * part, (k + 1) * part, add_slots, 0, unroll=8)
         den[...] = 1.0 / (1.0 + den[...])
 
     rows = TH // ROW_STEPS
@@ -180,7 +180,7 @@
             strip[p, tile] = jnp.where(inside, picked[p], strip[p, tile])
         return carry
 
-    lax.fori_loop(0, rows // CHUNK, some_rows, 0, unroll=2)
+    lax.fori_loop(0, rows // CHUNK, some_rows, 0, unroll=4)
 
     rim = HALO * channels
     top = step == 0

time: 125 us -> 124 us (level)
  no operation moved by 1% of the time
where the time goes in v8:
time: 124 us; the launch traced here: 123 us
  waiting for transfers between devices  62.3 us (50%)
  Pallas kernels  34.5 us (28%)
  starting transfers between devices  14.5 us (12%)
  local copies, waits for them, and re-layouts  7.08 us (6%)
  other arithmetic  4.98 us (4%)
    all_to_all x1, waiting for transfers between devices, shards(): lax.all_to_all(packets, tiles, split_axis=0, concat_axis=0, tiled=True)  58.4 us
    pallas_call x1, Pallas kernels, encoder(): pl.pallas_call(functools.partial(encoder_kernel, channels, hid), grid_spe...  21.7 us
    pallas_call x1, Pallas kernels, composite(): pl.pallas_call(functools.partial(composite_kernel, capacity, channels), g...  7.49 us
    all_to_all x1, starting transfers between devices, shards(): lax.all_to_all(packets, tiles, split_axis=0, concat_axis=0, tiled=True)  6.99 us
    pallas_call x1, Pallas kernels, pack(): pl.pallas_call(functools.partial(pack_kernel, channels), grid_spec=pltpu....  5.25 us
    unnamed x11, local copies, waits for them, and re-layouts  3.49 us
    ppermute x1, starting transfers between devices, shards(): rim_a = lax.ppermute(rim_a, 'ty', pairs_a)  3.22 us
    ppermute x1, waiting for transfers between devices, shards(): rim_b = lax.ppermute(rim_b, 'ty', pairs_b)  3.02 us
  transfers between devices with their start and end apart: 6, of which 3 were waited for; matrix products, arithmetic and copies ran while one was open for 9% of the time, Pallas kernels for 0%

profile of v8, /device:TPU:9, one launch (start us, length us, event | category | flops | bytes accessed | tf_op | source)
XLA Modules:
  0.0 123.4 jit_solution(13119787748038231948)
XLA Ops:
  0.0 5.2 %pack.1 = bf16[16,784,128]{2,1,0:T(8,128)(2,1)} custom-call(s32[16,16]{1,0:T(8,128)} %bitcast.32, s32[1,16]{1,0:T(1,128)} %count_ref.1, bf16[256,48,128]{2,1,0:T(8,128)(2,1)} %sweeps_ref.1, s32[1,16,16]{2,1,0:T(8,128)} %cell_ref.1, s32[1,16,16]{2,1,0:T(8,128)} %templ_ref.1), custom_call_target="tpu_custom_call" | custom-call | tf_op jit(solution)/shard_map/pack/pallas_call | solution.py:412
  5.3 7.0 %all-to-all-start = ((bf16[16,784,128]{2,1,0:T(8,128)(2,1)}), bf16[16,784,128]{2,1,0:T(8,128)(2,1)S(1)}, u32[]{:S(2)}, u32[]{:S(2)}) async-start(bf16[16,784,128]{2,1,0:T(8,128)(2,1)} %pack.1), calls=%async_computation | async-start | bytes 6422528 | tf_op jit(solution)/shard_map/all_to_all | solution.py:530
  12.4 0.6 fusion.6
  13.0 0.1 copy.23
  13.1 0.9 copy.25
  14.0 0.7 copy.24
  14.7 1.0 copy.20
  15.7 0.8 copy.21
  16.5 2.2 %copy.17 = bf16[32,128,128]{1,2,0:T(8,128)(2,1)} copy(bf16[32,128,128]{2,1,0:T(8,128)(2,1)} %param.15) | data formatting | bytes 2097152 | tf_op args[5]
  18.8 0.9 pad_maximum_fusion.edge_first_ref
  19.7 0.7 fusion.5.first_ref
  20.5 1.1 fusion.4.second_ref
  21.5 1.6 %convert_reduce_fusion.weight_ref = f32[32,128]{1,0:T(8,128)S(1)} fusion(bf16[32,128,128]{2,1,0:T(8,128)(2,1)} %param.15), kind=kLoop, calls=%fused_computation | loop fusion | flops 1044480 | bytes 1064960 | tf_op jit(solution)/shard_map/reduce_sum | solution.py:532
  23.1 58.4 %all-to-all-done.recv_ref = bf16[16,784,128]{2,1,0:T(8,128)(2,1)S(1)} async-done(((bf16[16,784,128]{2,1,0:T(8,128)(2,1)}), bf16[16,784,128]{2,1,0:T(8,128)(2,1)S(1)}, u32[]{:S(2)}, u32[]{:S(2)}) %all-to-all-start) | async-done | bytes 3211296 | tf_op jit(solution)/shard_map/all_to_all | solution.py:530
  81.5 1.2 copy-done
  82.7 7.5 %composite.1 = (bf16[9216,256]{1,0:T(8,128)(2,1)S(1)}, bf16[2,2,48,128]{3,2,1,0:T(8,128)(2,1)S(1)}, bf16[2,48,256]{2,1,0:T(8,128)(2,1)S(1)}, bf16[2,48,256]{2,1,0:T(8,128)(2,1)S(1)}) custom-call(s32[4]{0:T(128)S(1)} %pad_add_fusion.col_ref.place_ref, bf16[16,784,128]{2,1,0:T(8,128)(2,1)S(1)} %all-to-all-done.recv_ref, bf16[32,128,128]{2,1,0:T(8,128)(2,1)S(1)} %bitcast.22, ...), custom_call_target="tpu_custom_call" | custom-call | tf_op jit(solution)/shard_map/composite/pallas_call | solution.py:436
  90.2 3.2 %collective-permute-start = (bf16[2,48,256]{2,1,0:T(8,128)(2,1)S(1)}, bf16[2,48,256]{2,1,0:T(8,128)(2,1)S(1)}, u32[]{:S(2)}, u32[]{:S(2)}) collective-permute-start(bf16[2,48,256]{2,1,0:T(8,128)(2,1)S(1)} %get-tuple-element.23), channel_id=1, source_target_pairs={{0,2},{2,0},{4,6},{6,4},{8,10},{10,8},{12,14},{14,12},{1,3},{3,1},... | collective-permute-start | bytes 147464 | tf_op jit(solution)/shard_map/ppermute | solution.py:545
  93.5 1.9 %collective-permute-start.1 = (bf16[2,48,256]{2,1,0:T(8,128)(2,1)S(1)}, bf16[2,48,256]{2,1,0:T(8,128)(2,1)S(1)}, u32[]{:S(2)}, u32[]{:S(2)}) collective-permute-start(bf16[2,48,256]{2,1,0:T(8,128)(2,1)S(1)} %get-tuple-element.24), channel_id=1, source_target_pairs={{2,4},{4,2},{6,8},{8,6},{10,12},{12,10},{3,5},{5,3},{7,9},{9,7},{1... | collective-permute-start | bytes 147464 | tf_op jit(solution)/shard_map/ppermute | solution.py:546
  95.4 0.6 collective-permute-start.2
  95.9 0.2 collective-permute-start.3
  96.2 3.0 %collective-permute-done.1.rim_b_ref = bf16[2,48,256]{2,1,0:T(8,128)(2,1)S(1)} collective-permute-done((bf16[2,48,256]{2,1,0:T(8,128)(2,1)S(1)}, bf16[2,48,256]{2,1,0:T(8,128)(2,1)S(1)}, u32[]{:S(2)}, u32[]{:S(2)}) %collective-permute-start.1) | collective-permute-done | bytes 49184 | tf_op jit(solution)/shard_map/ppermute | solution.py:546
  99.2 1.6 %collective-permute-start.4 = (bf16[2,48,256]{2,1,0:T(8,128)(2,1)S(1)}, bf16[2,48,256]{2,1,0:T(8,128)(2,1)S(1)}, u32[]{:S(2)}, u32[]{:S(2)}) collective-permute-start(bf16[2,48,256]{2,1,0:T(8,128)(2,1)S(1)} %collective-permute-done.1.rim_b_ref), channel_id=1, source_target_pairs={{0,1},{1,0},{2,3},{3,2},{4,5},{5,4},{6,7},{7,6},{8,9},{9,8},{10,11... | collective-permute-start | bytes 147464 | tf_op jit(solution)/shard_map/ppermute | solution.py:548
  100.8 0.9 collective-permute-done.4.side_b_ref
  101.7 21.7 %encoder.1 = bf16[64,192,256]{2,1,0:T(8,128)(2,1)} custom-call(s32[4]{0:T(128)S(1)} %pad_add_fusion.col_ref.place_ref, bf16[192,48,256]{2,1,0:T(8,128)(2,1)S(1)} %bitcast.21, bf16[2,48,256]{2,1,0:T(8,128)(2,1)S(1)} %collective-permute-done.rim_a_ref, bf16[2,48,256]{2,1,0:T(8,128)(2,1)S(1)} %collective-permute-done.1.rim_b_ref, ...), custom_call_target="tpu_custom_call" | custom-call | tf_op jit(solution)/shard_map/encoder/pallas_call | solution.py:475
  (14 shorter events, 0.2 us)
Async XLA Ops:
  5.3 7.0 %copy-start.4 = (bf16[9,64,48]{1,2,0:T(8,128)(2,1)S(1)}, bf16[9,64,48]{1,2,0:T(8,128)(2,1)}, u32[]{:S(2)}) copy-start(bf16[9,64,48]{1,2,0:T(8,128)(2,1)} %param.16) | copy-start | bytes 165892
  5.3 76.2 %all-to-all-start = ((bf16[16,784,128]{2,1,0:T(8,128)(2,1)}), bf16[16,784,128]{2,1,0:T(8,128)(2,1)S(1)}, u32[]{:S(2)}, u32[]{:S(2)}) async-start(bf16[16,784,128]{2,1,0:T(8,128)(2,1)} %pack.1), calls=%async_computation | async-start | bytes 6422528 | tf_op jit(solution)/shard_map/all_to_all | solution.py:530
  18.7 83.0 %copy-start.2 = (f32[64]{0:T(128)S(1)}, f32[64]{0:T(128)}, u32[]{:S(2)}) copy-start(f32[64]{0:T(128)} %param.17) | copy-start | bytes 772
  18.7 83.0 %copy-start.3 = (f32[64]{0:T(128)S(1)}, f32[64]{0:T(128)}, u32[]{:S(2)}) copy-start(f32[64]{0:T(128)} %param.19) | copy-start | bytes 772
  81.5 1.2 copy-start
  82.7 19.0 %copy-start.1 = (bf16[128,576]{1,0:T(8,128)(2,1)S(1)}, bf16[128,576]{1,0:T(8,128)(2,1)}, u32[]{:S(2)}) copy-start(bf16[128,576]{1,0:T(8,128)(2,1)} %fusion.5.first_ref) | copy-start | bytes 442372
  90.2 5.7 %collective-permute-start = (bf16[2,48,256]{2,1,0:T(8,128)(2,1)S(1)}, bf16[2,48,256]{2,1,0:T(8,128)(2,1)S(1)}, u32[]{:S(2)}, u32[]{:S(2)}) collective-permute-start(bf16[2,48,256]{2,1,0:T(8,128)(2,1)S(1)} %get-tuple-element.23), channel_id=1, source_target_pairs={{0,2},{2,0},{4,6},{6,4},{8,10},{10,8},{12,14},{14,12},{1,3},{3,1},... | collective-permute-start | bytes 147464 | tf_op jit(solution)/shard_map/ppermute | solution.py:545
  93.5 5.7 %collective-permute-start.1 = (bf16[2,48,256]{2,1,0:T(8,128)(2,1)S(1)}, bf16[2,48,256]{2,1,0:T(8,128)(2,1)S(1)}, u32[]{:S(2)}, u32[]{:S(2)}) collective-permute-start(bf16[2,48,256]{2,1,0:T(8,128)(2,1)S(1)} %get-tuple-element.24), channel_id=1, source_target_pairs={{2,4},{4,2},{6,8},{8,6},{10,12},{12,10},{3,5},{5,3},{7,9},{9,7},{1... | collective-permute-start | bytes 147464 | tf_op jit(solution)/shard_map/ppermute | solution.py:546
  95.4 5.5 %collective-permute-start.2 = (bf16[2,2,48,128]{3,2,1,0:T(8,128)(2,1)S(1)}, bf16[2,2,48,128]{3,2,1,0:T(8,128)(2,1)S(1)}, u32[]{:S(2)}, u32[]{:S(2)}) collective-permute-start(bf16[2,2,48,128]{3,2,1,0:T(8,128)(2,1)S(1)} %get-tuple-element.25.own_ref), channel_id=1, source_target_pairs={{0,1},{1,0},{2,3},{3,2},{4,5},{5,4},{6,7},{7,6},{8,9},{9,8},{10,11... | collective-permute-start | bytes 147464 | tf_op jit(solution)/shard_map/ppermute | solution.py:544
  95.9 4.9 %collective-permute-start.3 = (bf16[2,48,256]{2,1,0:T(8,128)(2,1)S(1)}, bf16[2,48,256]{2,1,0:T(8,128)(2,1)S(1)}, u32[]{:S(2)}, u32[]{:S(2)}) collective-permute-start(bf16[2,48,256]{2,1,0:T(8,128)(2,1)S(1)} %collective-permute-done.rim_a_ref), channel_id=1, source_target_pairs={{0,1},{1,0},{2,3},{3,2},{4,5},{5,4},{6,7},{7,6},{8,9},{9,8},{10,11... | collective-permute-start | bytes 147464 | tf_op jit(solution)/shard_map/ppermute | solution.py:547
  99.2 2.5 %collective-permute-start.4 = (bf16[2,48,256]{2,1,0:T(8,128)(2,1)S(1)}, bf16[2,48,256]{2,1,0:T(8,128)(2,1)S(1)}, u32[]{:S(2)}, u32[]{:S(2)}) collective-permute-start(bf16[2,48,256]{2,1,0:T(8,128)(2,1)S(1)} %collective-permute-done.1.rim_b_ref), channel_id=1, source_target_pairs={{0,1},{1,0},{2,3},{3,2},{4,5},{5,4},{6,7},{7,6},{8,9},{9,8},{10,11... | collective-permute-start | bytes 147464 | tf_op jit(solution)/shard_map/ppermute | solution.py:548

commit v9 on v8

--- a/solution.py
+++ b/solution.py
@@ -18,7 +18,7 @@
 CHUNK = 8
 LOADS = 2
 GROUP = 2
-OUT_ROWS = 32
+OUT_ROWS = 48
 LAG = 2
 PACK_PARTS = 8
 INFO_ROWS = 16
@@ -26,7 +26,7 @@
 MIB = 1024 * 1024
 PACK_VMEM = 56 * MIB
 COMPOSITE_VMEM = 26 * MIB
-ENCODER_VMEM = 48 * MIB
+ENCODER_VMEM = 50 * MIB
 
 F32 = jnp.float32
 BF16 = jnp.bfloat16

time: 124 us -> 126 us (1.016)
  local copies, waits for them, and re-layouts: 7.08 us -> 9.22 us
    unnamed x11 -> x13, local copies, waits for them, and re-layouts: 3.49 us -> 5.63 us
where the time goes in v9:
time: 126 us
  waiting for transfers between devices  62.1 us (49%)
  Pallas kernels  34.6 us (27%)
  starting transfers between devices  14.6 us (12%)
  local copies, waits for them, and re-layouts  9.22 us (7%)
  other arithmetic  5.02 us (4%)
    all_to_all x1, waiting for transfers between devices, shards(): lax.all_to_all(packets, tiles, split_axis=0, concat_axis=0, tiled=True)  58.3 us
    pallas_call x1, Pallas kernels, encoder(): pl.pallas_call(functools.partial(encoder_kernel, channels, hid), grid_spe...  21.9 us
    pallas_call x1, Pallas kernels, composite(): pl.pallas_call(functools.partial(composite_kernel, capacity, channels), g...  7.58 us
    all_to_all x1, starting transfers between devices, shards(): lax.all_to_all(packets, tiles, split_axis=0, concat_axis=0, tiled=True)  6.9 us
    unnamed x13, local copies, waits for them, and re-layouts  5.63 us
    pallas_call x1, Pallas kernels, pack(): pl.pallas_call(functools.partial(pack_kernel, channels), grid_spec=pltpu....  5.07 us
    ppermute x1, starting transfers between devices, shards(): rim_a = lax.ppermute(rim_a, 'ty', pairs_a)  3.14 us
    ppermute x1, waiting for transfers between devices, shards(): rim_b = lax.ppermute(rim_b, 'ty', pairs_b)  2.9 us
  transfers between devices with their start and end apart: 6, of which 3 were waited for; matrix products, arithmetic and copies ran while one was open for 9% of the time, Pallas kernels for 0%

profile of v9, /device:TPU:9, one launch (start us, length us, event | category | flops | bytes accessed | tf_op | source)
XLA Modules:
  0.0 125.7 jit_solution(315666195466316482)
XLA Ops:
  0.0 5.1 %pack.1 = bf16[16,784,128]{2,1,0:T(8,128)(2,1)} custom-call(s32[16,16]{1,0:T(8,128)} %bitcast.32, s32[1,16]{1,0:T(1,128)} %count_ref.1, bf16[256,48,128]{2,1,0:T(8,128)(2,1)} %sweeps_ref.1, s32[1,16,16]{2,1,0:T(8,128)} %cell_ref.1, s32[1,16,16]{2,1,0:T(8,128)} %templ_ref.1), custom_call_target="tpu_custom_call" | custom-call | tf_op jit(solution)/shard_map/pack/pallas_call | solution.py:412
  5.1 6.9 %all-to-all-start = ((bf16[16,784,128]{2,1,0:T(8,128)(2,1)}), bf16[16,784,128]{2,1,0:T(8,128)(2,1)S(1)}, u32[]{:S(2)}, u32[]{:S(2)}) async-start(bf16[16,784,128]{2,1,0:T(8,128)(2,1)} %pack.1), calls=%async_computation | async-start | bytes 6422528 | tf_op jit(solution)/shard_map/all_to_all | solution.py:530
  12.1 0.6 fusion.6
  12.7 0.1 copy.23
  12.8 0.9 copy.25
  13.7 0.7 copy.24
  14.4 1.0 copy.20
  15.5 0.8 copy.21
  16.2 2.3 %copy.17 = bf16[32,128,128]{1,2,0:T(8,128)(2,1)} copy(bf16[32,128,128]{2,1,0:T(8,128)(2,1)} %param.15) | data formatting | bytes 2097152 | tf_op args[5]
  18.6 0.9 pad_maximum_fusion.edge_first_ref
  19.5 0.8 fusion.5.first_ref
  20.3 1.1 fusion.4.second_ref
  21.3 1.6 %convert_reduce_fusion.weight_ref = f32[32,128]{1,0:T(8,128)S(1)} fusion(bf16[32,128,128]{2,1,0:T(8,128)(2,1)} %param.15), kind=kLoop, calls=%fused_computation | loop fusion | flops 1044480 | bytes 1064960 | tf_op jit(solution)/shard_map/reduce_sum | solution.py:532
  22.9 58.3 %all-to-all-done.recv_ref = bf16[16,784,128]{2,1,0:T(8,128)(2,1)S(1)} async-done(((bf16[16,784,128]{2,1,0:T(8,128)(2,1)}), bf16[16,784,128]{2,1,0:T(8,128)(2,1)S(1)}, u32[]{:S(2)}, u32[]{:S(2)}) %all-to-all-start) | async-done | bytes 3211296 | tf_op jit(solution)/shard_map/all_to_all | solution.py:530
  81.2 1.2 copy-done.1
  82.5 7.6 %composite.1 = (bf16[9216,256]{1,0:T(8,128)(2,1)S(1)}, bf16[2,2,48,128]{3,2,1,0:T(8,128)(2,1)S(1)}, bf16[2,48,256]{2,1,0:T(8,128)(2,1)S(1)}, bf16[2,48,256]{2,1,0:T(8,128)(2,1)S(1)}) custom-call(s32[4]{0:T(128)S(1)} %pad_add_fusion.col_ref.place_ref, bf16[16,784,128]{2,1,0:T(8,128)(2,1)S(1)} %all-to-all-done.recv_ref, bf16[32,128,128]{2,1,0:T(8,128)(2,1)S(1)} %bitcast.22, ...), custom_call_target="tpu_custom_call" | custom-call | tf_op jit(solution)/shard_map/composite/pallas_call | solution.py:436
  90.1 2.1 %copy-done = bf16[9216,256]{1,0:T(8,128)(2,1)} copy-done((bf16[9216,256]{1,0:T(8,128)(2,1)}, bf16[9216,256]{1,0:T(8,128)(2,1)S(1)}, u32[]{:S(2)}) %copy-start) | copy-done | bytes 4718616
  92.2 3.1 %collective-permute-start = (bf16[2,48,256]{2,1,0:T(8,128)(2,1)S(1)}, bf16[2,48,256]{2,1,0:T(8,128)(2,1)S(1)}, u32[]{:S(2)}, u32[]{:S(2)}) collective-permute-start(bf16[2,48,256]{2,1,0:T(8,128)(2,1)S(1)} %get-tuple-element.23), channel_id=1, source_target_pairs={{0,2},{2,0},{4,6},{6,4},{8,10},{10,8},{12,14},{14,12},{1,3},{3,1},... | collective-permute-start | bytes 147464 | tf_op jit(solution)/shard_map/ppermute | solution.py:545
  95.3 2.1 %collective-permute-start.1 = (bf16[2,48,256]{2,1,0:T(8,128)(2,1)S(1)}, bf16[2,48,256]{2,1,0:T(8,128)(2,1)S(1)}, u32[]{:S(2)}, u32[]{:S(2)}) collective-permute-start(bf16[2,48,256]{2,1,0:T(8,128)(2,1)S(1)} %get-tuple-element.24), channel_id=1, source_target_pairs={{2,4},{4,2},{6,8},{8,6},{10,12},{12,10},{3,5},{5,3},{7,9},{9,7},{1... | collective-permute-start | bytes 147464 | tf_op jit(solution)/shard_map/ppermute | solution.py:546
  97.4 0.6 collective-permute-start.2
  98.2 2.9 %collective-permute-done.1.rim_b_ref = bf16[2,48,256]{2,1,0:T(8,128)(2,1)S(1)} collective-permute-done((bf16[2,48,256]{2,1,0:T(8,128)(2,1)S(1)}, bf16[2,48,256]{2,1,0:T(8,128)(2,1)S(1)}, u32[]{:S(2)}, u32[]{:S(2)}) %collective-permute-start.1) | collective-permute-done | bytes 49184 | tf_op jit(solution)/shard_map/ppermute | solution.py:546
  101.1 1.7 %collective-permute-start.4 = (bf16[2,48,256]{2,1,0:T(8,128)(2,1)S(1)}, bf16[2,48,256]{2,1,0:T(8,128)(2,1)S(1)}, u32[]{:S(2)}, u32[]{:S(2)}) collective-permute-start(bf16[2,48,256]{2,1,0:T(8,128)(2,1)S(1)} %collective-permute-done.1.rim_b_ref), channel_id=1, source_target_pairs={{0,1},{1,0},{2,3},{3,2},{4,5},{5,4},{6,7},{7,6},{8,9},{9,8},{10,11... | collective-permute-start | bytes 147464 | tf_op jit(solution)/shard_map/ppermute | solution.py:548
  102.8 0.9 collective-permute-done.4.side_b_ref
  103.7 21.9 %encoder.1 = bf16[64,192,256]{2,1,0:T(8,128)(2,1)} custom-call(s32[4]{0:T(128)S(1)} %pad_add_fusion.col_ref.place_ref, bf16[192,48,256]{2,1,0:T(8,128)(2,1)} %bitcast.21, bf16[2,48,256]{2,1,0:T(8,128)(2,1)S(1)} %collective-permute-done.rim_a_ref, bf16[2,48,256]{2,1,0:T(8,128)(2,1)S(1)} %collective-permute-done.1.rim_b_ref, ...), custom_call_target="tpu_custom_call" | custom-call | tf_op jit(solution)/shard_map/encoder/pallas_call | solution.py:475
  (16 shorter events, 0.3 us)
Async XLA Ops:
  5.1 6.9 %copy-start.5 = (bf16[9,64,48]{1,2,0:T(8,128)(2,1)S(1)}, bf16[9,64,48]{1,2,0:T(8,128)(2,1)}, u32[]{:S(2)}) copy-start(bf16[9,64,48]{1,2,0:T(8,128)(2,1)} %param.16) | copy-start | bytes 165892
  5.1 76.1 %all-to-all-start = ((bf16[16,784,128]{2,1,0:T(8,128)(2,1)}), bf16[16,784,128]{2,1,0:T(8,128)(2,1)S(1)}, u32[]{:S(2)}, u32[]{:S(2)}) async-start(bf16[16,784,128]{2,1,0:T(8,128)(2,1)} %pack.1), calls=%async_computation | async-start | bytes 6422528 | tf_op jit(solution)/shard_map/all_to_all | solution.py:530
  18.5 85.2 %copy-start.3 = (f32[64]{0:T(128)S(1)}, f32[64]{0:T(128)}, u32[]{:S(2)}) copy-start(f32[64]{0:T(128)} %param.17) | copy-start | bytes 772
  18.5 85.2 %copy-start.4 = (f32[64]{0:T(128)S(1)}, f32[64]{0:T(128)}, u32[]{:S(2)}) copy-start(f32[64]{0:T(128)} %param.19) | copy-start | bytes 772
  81.2 1.2 copy-start.1
  82.5 21.2 %copy-start.2 = (bf16[128,576]{1,0:T(8,128)(2,1)S(1)}, bf16[128,576]{1,0:T(8,128)(2,1)}, u32[]{:S(2)}) copy-start(bf16[128,576]{1,0:T(8,128)(2,1)} %fusion.5.first_ref) | copy-start | bytes 442372
  90.1 2.1 %copy-start = (bf16[9216,256]{1,0:T(8,128)(2,1)}, bf16[9216,256]{1,0:T(8,128)(2,1)S(1)}, u32[]{:S(2)}) copy-start(bf16[9216,256]{1,0:T(8,128)(2,1)S(1)} %get-tuple-element.22) | copy-start | bytes 14155780
  92.2 5.9 %collective-permute-start = (bf16[2,48,256]{2,1,0:T(8,128)(2,1)S(1)}, bf16[2,48,256]{2,1,0:T(8,128)(2,1)S(1)}, u32[]{:S(2)}, u32[]{:S(2)}) collective-permute-start(bf16[2,48,256]{2,1,0:T(8,128)(2,1)S(1)} %get-tuple-element.23), channel_id=1, source_target_pairs={{0,2},{2,0},{4,6},{6,4},{8,10},{10,8},{12,14},{14,12},{1,3},{3,1},... | collective-permute-start | bytes 147464 | tf_op jit(solution)/shard_map/ppermute | solution.py:545
  95.3 5.7 %collective-permute-start.1 = (bf16[2,48,256]{2,1,0:T(8,128)(2,1)S(1)}, bf16[2,48,256]{2,1,0:T(8,128)(2,1)S(1)}, u32[]{:S(2)}, u32[]{:S(2)}) collective-permute-start(bf16[2,48,256]{2,1,0:T(8,128)(2,1)S(1)} %get-tuple-element.24), channel_id=1, source_target_pairs={{2,4},{4,2},{6,8},{8,6},{10,12},{12,10},{3,5},{5,3},{7,9},{9,7},{1... | collective-permute-start | bytes 147464 | tf_op jit(solution)/shard_map/ppermute | solution.py:546
  97.4 5.3 %collective-permute-start.2 = (bf16[2,2,48,128]{3,2,1,0:T(8,128)(2,1)S(1)}, bf16[2,2,48,128]{3,2,1,0:T(8,128)(2,1)S(1)}, u32[]{:S(2)}, u32[]{:S(2)}) collective-permute-start(bf16[2,2,48,128]{3,2,1,0:T(8,128)(2,1)S(1)} %get-tuple-element.25.own_ref), channel_id=1, source_target_pairs={{0,1},{1,0},{2,3},{3,2},{4,5},{5,4},{6,7},{7,6},{8,9},{9,8},{10,11... | collective-permute-start | bytes 147464 | tf_op jit(solution)/shard_map/ppermute | solution.py:544
  98.1 4.7 %collective-permute-start.3 = (bf16[2,48,256]{2,1,0:T(8,128)(2,1)S(1)}, bf16[2,48,256]{2,1,0:T(8,128)(2,1)S(1)}, u32[]{:S(2)}, u32[]{:S(2)}) collective-permute-start(bf16[2,48,256]{2,1,0:T(8,128)(2,1)S(1)} %collective-permute-done.rim_a_ref), channel_id=1, source_target_pairs={{0,1},{1,0},{2,3},{3,2},{4,5},{5,4},{6,7},{7,6},{8,9},{9,8},{10,11... | collective-permute-start | bytes 147464 | tf_op jit(solution)/shard_map/ppermute | solution.py:547
  101.1 2.6 %collective-permute-start.4 = (bf16[2,48,256]{2,1,0:T(8,128)(2,1)S(1)}, bf16[2,48,256]{2,1,0:T(8,128)(2,1)S(1)}, u32[]{:S(2)}, u32[]{:S(2)}) collective-permute-start(bf16[2,48,256]{2,1,0:T(8,128)(2,1)S(1)} %collective-permute-done.1.rim_b_ref), channel_id=1, source_target_pairs={{0,1},{1,0},{2,3},{3,2},{4,5},{5,4},{6,7},{7,6},{8,9},{9,8},{10,11... | collective-permute-start | bytes 147464 | tf_op jit(solution)/shard_map/ppermute | solution.py:548
